TPU v7x, 1024 devices: a whole 8x8x8 slice. The times are simulated.
1024 devices in a mesh: dp: 16 (over z, core), expert: 64 (over x, y).
Axes of the slice: x: 8, y: 8, z: 8, core: 2. Of those that a mesh axis runs over, the one named last changes fastest.
Arguments:
- tokens: bfloat16 [8192, 4096], P('expert', 'dp'), may hold values from -6 to 6
- routes: int32 [8192, 8], P('expert'), may hold values from 0 to 63, all different within a row; in each aligned block of 128 rows (0 to 127, 128 to 255, ...) at most 18 rows name the same one
- combine: float32 [8192, 8], P('expert'), may hold values from 0.05 to 0.5
- clip_mask: int32 [8192], P('expert'), may hold values 0 or 1
- limits: int32 [64], replicated, may hold values from 1 to 18, as said below
- cotangent: bfloat16 [8192, 4096], P('expert', 'dp'), may hold values from -6 to 6
- gate_weight: bfloat16 [64, 4096, 768], P('expert', 'dp'), may hold values from -0.09375 to 0.09375
- up_weight: bfloat16 [64, 4096, 768], P('expert', 'dp'), may hold values from -0.09375 to 0.09375
- down_weight: bfloat16 [64, 768, 4096], P('expert', None, 'dp'), may hold values from -0.21875 to 0.21875
Outputs:
- layer_out: bfloat16 [8192, 4096], P('expert', 'dp')
- token_grads: bfloat16 [8192, 4096], P('expert', 'dp')
- gate_grads: bfloat16 [64, 4096, 768], P('expert', 'dp')
- up_grads: bfloat16 [64, 4096, 768], P('expert', 'dp')
- down_grads: bfloat16 [64, 768, 4096], P('expert', None, 'dp')
Inputs may be any that keep to these rules, and one draw needn't show every extreme that they name: `routes`: each token lists 8 different experts. Among the 128 tokens of one index of expert (an aligned block), no expert is listed more than 18 times, a bound that some block reaches. `limits`: some expert's limit is exactly 18.
All inputs are finite; a program needn't handle non-finite values. No bound on the sum of `clip_mask` on one device may be relied on, other than what follows from the above.
Results may differ from a plain program's by a relative error of at most 0.035.
Values may be sent and summed in bfloat16 or wider, within the bound.
No kernel may reach another device: no remote copies, remote signals or barrier semaphores. Data moves between devices by JAX's collectives and lax.ppermute only.
A program may use at most 64 MiB of HBM per device.

v0:
```python
import jax
import jax.numpy as jnp
from jax import lax
from jax.sharding import PartitionSpec as P


def swish_parts(gate_val):
    sigma = jax.nn.sigmoid(gate_val)
    return (gate_val * sigma, sigma * (1.0 + gate_val * (1.0 - sigma)))


def member(stacked, index, axis):
    return lax.index_in_dim(stacked, index, axis, keepdims=False)


def body(
    tokens, routes, combine, clip_mask, limits, cotangent, gate_weight, up_weight, down_weight
):
    tok_rows, top_count = routes.shape
    experts = limits.shape[0]
    capacity = 9 * tok_rows * top_count // (8 * experts)
    owners = lax.axis_size("expert")
    held_count = gate_weight.shape[0]
    piece_width = tokens.shape[1]
    slots_all = experts * capacity
    flat_ids = routes.reshape(-1)
    labels = jnp.arange(experts, dtype=jnp.int32)
    onehot = (flat_ids[:, None] == labels[None, :]).astype(jnp.int32)
    rank_ids = jnp.sum((jnp.cumsum(onehot, axis=0) - onehot) * onehot, axis=1)
    limit_ids = jnp.sum(onehot * limits[None, :], axis=1)
    order_ids = flat_ids % held_count * owners + flat_ids // held_count
    place_ids = jnp.where(rank_ids < limit_ids, order_ids * capacity + rank_ids, slots_all)
    assigned = (place_ids[None, :] == jnp.arange(slots_all, dtype=jnp.int32)[:, None]).astype(
        jnp.float32
    )
    picked = jnp.sum(assigned.reshape(slots_all, tok_rows, top_count), axis=2)
    weights_tok = jnp.sum(
        (assigned * combine.reshape(1, -1)).reshape(slots_all, tok_rows, top_count), axis=2
    )
    scaled = combine * clip_mask.astype(jnp.float32)[:, None]
    slot_coef = jnp.sum(assigned * scaled.reshape(1, -1), axis=1)
    picked_low = picked.astype(jnp.bfloat16)
    send_shape = (held_count, owners, capacity, piece_width)
    token_send = (
        jnp.dot(picked_low, tokens, preferred_element_type=jnp.float32)
        .astype(jnp.bfloat16)
        .reshape(send_shape)
    )
    grad_send = (
        (jnp.dot(picked_low, cotangent, preferred_element_type=jnp.float32) * slot_coef[:, None])
        .astype(jnp.bfloat16)
        .reshape(send_shape)
    )
    token_recv = lax.all_to_all(token_send, "expert", split_axis=1, concat_axis=1, tiled=True)
    grad_recv = lax.all_to_all(grad_send, "expert", split_axis=1, concat_axis=1, tiled=True)
    row_count = owners * capacity
    token_rows = token_recv.reshape(held_count, row_count, piece_width)
    grad_rows = grad_recv.reshape(held_count, row_count, piece_width)
    fwd_spec = "lrd,ldf->lrf"
    back_spec = "lrd,lfd->lrf"
    down_spec = "lrf,lfd->lrd"
    input_spec = "lrf,ldf->lrd"
    weight_spec = "lrd,lrf->ldf"
    lower_spec = "lrf,lrd->lfd"
    stack_axis = 2
    gate_part = jnp.einsum(fwd_spec, token_rows, gate_weight, preferred_element_type=jnp.float32)
    up_part = jnp.einsum(fwd_spec, token_rows, up_weight, preferred_element_type=jnp.float32)
    gate_up = jnp.stack([gate_part, up_part], axis=stack_axis)
    shares = lax.psum_scatter(
        gate_up.astype(jnp.bfloat16), "dp", scatter_dimension=1, tiled=True
    ).astype(jnp.float32)
    gate_val = member(shares, 0, stack_axis)
    up_val = member(shares, 1, stack_axis)
    active, slope = swish_parts(gate_val)
    hidden = (active * up_val).astype(jnp.bfloat16)
    hidden_full = lax.all_gather(hidden, "dp", axis=1, tiled=True)
    out_piece = (
        jnp.einsum(down_spec, hidden_full, down_weight, preferred_element_type=jnp.float32)
        .astype(jnp.bfloat16)
        .reshape(send_shape)
    )
    grad_part = jnp.einsum(back_spec, grad_rows, down_weight, preferred_element_type=jnp.float32)
    grad_hidden = lax.psum_scatter(
        grad_part.astype(jnp.bfloat16), "dp", scatter_dimension=1, tiled=True
    ).astype(jnp.float32)
    grad_up = (grad_hidden * active).astype(jnp.bfloat16)
    grad_gate = (grad_hidden * up_val * slope).astype(jnp.bfloat16)
    derived = jnp.stack([grad_gate, grad_up], axis=stack_axis)
    gathered = lax.all_gather(derived, "dp", axis=1, tiled=True)
    gate_full = member(gathered, 0, stack_axis)
    up_full = member(gathered, 1, stack_axis)
    back_rows = lax.all_to_all(out_piece, "expert", split_axis=1, concat_axis=1, tiled=True)
    input_piece = jnp.einsum(
        input_spec, gate_full, gate_weight, preferred_element_type=jnp.float32
    ) + jnp.einsum(input_spec, up_full, up_weight, preferred_element_type=jnp.float32)
    input_piece = input_piece.astype(jnp.bfloat16).reshape(send_shape)
    gate_grads = jnp.einsum(
        weight_spec, token_rows, gate_full, preferred_element_type=jnp.float32
    ).astype(jnp.bfloat16)
    up_grads = jnp.einsum(
        weight_spec, token_rows, up_full, preferred_element_type=jnp.float32
    ).astype(jnp.bfloat16)
    down_grads = jnp.einsum(
        lower_spec, hidden_full, grad_rows, preferred_element_type=jnp.float32
    ).astype(jnp.bfloat16)
    grads_back = lax.all_to_all(input_piece, "expert", split_axis=1, concat_axis=1, tiled=True)
    layer_out = jnp.dot(
        weights_tok.T,
        back_rows.reshape(slots_all, piece_width).astype(jnp.float32),
        precision=lax.Precision.HIGHEST,
    ).astype(jnp.bfloat16)
    token_grads = jnp.dot(
        picked_low.T, grads_back.reshape(slots_all, piece_width), preferred_element_type=jnp.float32
    ).astype(jnp.bfloat16)
    return (layer_out, token_grads, gate_grads, up_grads, down_grads)


def solution(mesh):
    in_specs = (
        P("expert", "dp"),
        P("expert", None),
        P("expert", None),
        P("expert"),
        P(),
        P("expert", "dp"),
        P("expert", "dp", None),
        P("expert", "dp", None),
        P("expert", None, "dp"),
    )
    out_specs = (
        P("expert", "dp"),
        P("expert", "dp"),
        P("expert", "dp", None),
        P("expert", "dp", None),
        P("expert", None, "dp"),
    )
    return jax.shard_map(body, mesh=mesh, in_specs=in_specs, out_specs=out_specs, check_vma=False)
```

profile of v0, /device:TPU:4, one launch (start us, length us, event | category | flops | bytes accessed | tf_op | source)
XLA Modules:
  0.0 390.2 jit_solution(13449439759825142639)
XLA Ops:
  7.2 0.0 copy-start
  7.2 0.0 reduce-scatter.7.cloned.1.call-start
  7.3 0.8 copy.48
  8.1 0.1 eq.48
  8.2 0.1 eq.52
  8.3 0.0 copy-start.6
  8.3 18.0 %reduce-window.6 = s32[64,8,128]{2,1,0:T(8,128)S(1)} reduce-window(s32[64,8,128]{2,1,0:T(8,128)S(1)} %fusion.30, s32[]{:T(128)} %constant.35.clone.1), window={size=1x1x128 pad=0_0x0_0x127_0}, to_apply=%region_0.0 | reduce-window | flops 8323072 | bytes 524292 | tf_op jit(solution)/shard_map/reduce-window
  26.3 0.1 slice.24
  26.5 0.1 copy.50
  26.6 0.1 copy.51
  26.7 0.1 broadcast_add_fusion
  26.9 0.1 select_reduce_fusion.2
  27.0 0.1 reduce_sum.50
  27.1 0.1 reduce_sum.52
  27.3 0.0 copy-done.8
  27.3 5.7 %convert_reduce_fusion = (bf16[1152,128]{1,0:T(8,128)(2,1)S(1)}, f32[1152,128]{1,0:T(8,128)S(1)}) fusion(s32[128,8]{0,1:T(8,128)S(1)} %add_select_fusion.1, f32[128,8]{0,1:T(8,128)S(1)} %copy-done.8), kind=kLoop, calls=%fused_computation.2 | loop fusion | flops 5603328 | bytes 892928 | tf_op jit(solution)/shard_map/reduce_sum | solution.py:36
  33.1 0.3 convolution_convert_fusion.4
  33.4 0.2 reshape.284
  33.5 38.3 %all_to_all.20 = bf16[1,64,18,256]{3,2,0,1:T(8,128)(2,1)S(1)} all-to-all(bf16[1,64,18,256]{3,2,0,1:T(8,128)(2,1)S(1)} %bitcast.128), channel_id=1, replica_groups=mesh['dp'=16,'expert'=64] {'expert'}, dimensions={1} | all-to-all | bytes 1179648 | tf_op jit(solution)/shard_map/all_to_all | solution.py:54
  71.9 0.2 reshape.285
  72.1 1.6 fusion.1
  73.7 0.6 fusion
  74.3 0.3 pad_maximum_fusion
  74.7 25.4 %copy.60 = bf16[1,1152,2,768]{3,2,0,1:T(2,128)(2,1)S(1)} copy(bf16[1,1152,2,768]{3,1,2,0:T(8,128)(2,1)S(1)} %pad_maximum_fusion) | data formatting | bytes 7077888
  100.0 2.5 copy.63
  102.5 0.0 reduce-scatter.7.cloned.1.call-update
  102.5 0.0 reduce-scatter.5.cloned.1.call-start
  102.6 0.6 copy-done.11
  103.2 0.1 copy.57
  103.3 0.1 mul.134
  103.4 0.6 select_reduce_fusion
  103.9 0.3 fusion.3
  104.2 0.2 reshape.292
  104.4 28.2 %all_to_all.21 = bf16[1,64,18,256]{3,2,0,1:T(8,128)(2,1)S(1)} all-to-all(bf16[1,64,18,256]{3,2,0,1:T(8,128)(2,1)S(1)} %bitcast.129), channel_id=1, replica_groups=mesh['dp'=16,'expert'=64] {'expert'}, dimensions={1} | all-to-all | bytes 1179648 | tf_op jit(solution)/shard_map/all_to_all | solution.py:55
  132.7 0.2 reshape.293
  132.9 1.9 fusion.2
  134.8 0.0 reduce-scatter.5.cloned.1.call-update
  134.8 0.0 all-gather.3.cloned.1.call-start
  134.8 40.3 %reduce-scatter.7.cloned.1.call-done = bf16[72,1536]{1,0:T(8,128)(2,1)} async-done(((bf16[1152,1536]{1,0:T(8,128)(2,1)}), bf16[72,1536]{1,0:T(8,128)(2,1)}) %reduce-scatter.7.cloned.1.call-update) | async-done | bytes 221200
  175.2 1.0 reshape.299
  176.2 65.4 %reduce-scatter.5.cloned.1.call-done = bf16[1,72,768]{2,1,0:T(8,128)(2,1)} async-done(((bf16[1,1152,768]{2,1,0:T(8,128)(2,1)}), bf16[1,72,768]{2,1,0:T(8,128)(2,1)}) %reduce-scatter.5.cloned.1.call-update) | async-done | bytes 110608 | tf_op jit(solution)/shard_map/reduce_scatter | solution.py:83
  241.6 1.7 fusion.36
  243.3 0.0 all-gather.3.cloned.1.call-update
  243.3 0.2 all-gather.5.cloned.1.call-start
  243.5 0.7 pad_maximum_fusion.1
  244.2 0.0 all-gather.5.cloned.1.call-update
  244.3 44.9 %all-gather.3.cloned.1.call-done = bf16[1,1152,768]{2,1,0:T(8,128)(2,1)} async-done(((bf16[1,72,768]{2,1,0:T(8,128)(2,1)}), bf16[1,1152,768]{2,1,0:T(8,128)(2,1)}) %all-gather.3.cloned.1.call-update) | async-done | bytes 1769488 | tf_op jit(solution)/shard_map/all_gather | solution.py:76
  289.2 2.1 convolution_convert_fusion.3
  291.3 1.1 reshape.290
  292.4 12.8 %all-to-all-start.1 = ((bf16[1,64,18,256]{3,2,0,1:T(8,128)(2,1)}), bf16[1,64,18,256]{3,2,0,1:T(8,128)(2,1)S(1)}, u32[]{:S(2)}, u32[]{:S(2)}) async-start(bf16[1,64,18,256]{3,2,0,1:T(8,128)(2,1)} %bitcast.11), calls=%async_computation.1 | async-start | bytes 1572864 | tf_op jit(solution)/shard_map/all_to_all | solution.py:92
  305.1 34.0 %all-gather.5.cloned.1.call-done = bf16[1,1152,2,768]{3,1,2,0:T(8,128)(2,1)} async-done(((bf16[1,72,2,768]{3,1,2,0:T(8,128)(2,1)}), bf16[1,1152,2,768]{3,1,2,0:T(8,128)(2,1)}) %all-gather.5.cloned.1.call-update) | async-done | bytes 3538960 | tf_op jit(solution)/shard_map/all_gather | solution.py:89
  339.1 2.3 fusion.9
  341.4 0.2 copy-done.1
  341.7 1.7 fusion.4
  343.3 1.1 reshape.296
  344.4 12.8 %all-to-all-start.3 = ((bf16[1,64,18,256]{3,2,0,1:T(8,128)(2,1)}), bf16[1,64,18,256]{3,2,0,1:T(8,128)(2,1)S(1)}, u32[]{:S(2)}, u32[]{:S(2)}) async-start(bf16[1,64,18,256]{3,2,0,1:T(8,128)(2,1)} %bitcast.18), calls=%async_computation.4 | async-start | bytes 1572864 | tf_op jit(solution)/shard_map/all_to_all | solution.py:106
  357.2 3.1 fusion.16
  360.3 1.0 reshape.291
  361.3 2.5 convolution_convert_fusion.5
  363.8 2.9 fusion.19
  366.7 1.5 fusion.20
  368.2 14.4 %all-to-all-done.3 = bf16[1,64,18,256]{3,2,0,1:T(8,128)(2,1)S(1)} async-done(((bf16[1,64,18,256]{3,2,0,1:T(8,128)(2,1)}), bf16[1,64,18,256]{3,2,0,1:T(8,128)(2,1)S(1)}, u32[]{:S(2)}, u32[]{:S(2)}) %all-to-all-start.3) | async-done | bytes 589856 | tf_op jit(solution)/shard_map/all_to_all | solution.py:106
  382.5 0.2 reshape.297
  382.7 0.9 convolution_convert_fusion.6
  (30 shorter events, 0.2 us)
Async XLA Ops:
  7.2 125.7 %copy-start = (bf16[1,768,256]{2,1,0:T(8,128)(2,1)S(1)}, bf16[1,768,256]{2,1,0:T(8,128)(2,1)}, u32[]{:S(2)}) copy-start(bf16[1,768,256]{2,1,0:T(8,128)(2,1)} %param.17) | copy-start | bytes 1179652
  7.2 20.1 %copy-start.9 = (s32[128,8]{0,1:T(8,128)S(1)}, s32[128,8]{0,1:T(8,128)}, u32[]{:S(2)}) copy-start(s32[128,8]{0,1:T(8,128)} %param.10) | copy-start | bytes 12292
  7.2 19.7 %copy-start.10 = (s32[64]{0:T(128)S(1)}, s32[64]{0:T(128)}, u32[]{:S(2)}) copy-start(s32[64]{0:T(128)} %param.13) | copy-start | bytes 772
  7.2 20.1 %copy-start.8 = (f32[128,8]{0,1:T(8,128)S(1)}, f32[128,8]{0,1:T(8,128)}, u32[]{:S(2)}) copy-start(f32[128,8]{0,1:T(8,128)} %param.11) | copy-start | bytes 12292
  7.2 168.0 %reduce-scatter.7.cloned.1.call-start = ((), (), s32[]{:S(2)}) async-start(), calls=%async_computation.9 | async-start | bytes 3760128
  8.3 24.8 %copy-start.6 = (bf16[128,256]{1,0:T(8,128)(2,1)S(1)}, bf16[128,256]{1,0:T(8,128)(2,1)}, u32[]{:S(2)}) copy-start(bf16[128,256]{1,0:T(8,128)(2,1)} %param.9) | copy-start | bytes 196612
  71.9 1.8 copy-start.4
  102.5 0.7 copy-start.11
  102.5 1.4 copy-start.7
  102.5 139.1 %reduce-scatter.5.cloned.1.call-start = ((), (), s32[]{:S(2)}) async-start(), calls=%async_computation.7 | async-start | bytes 1880064 | tf_op jit(solution)/shard_map/reduce_scatter | solution.py:83
  132.9 1.9 copy-start.3
  134.8 154.4 %all-gather.3.cloned.1.call-start = ((), (), s32[]{:S(2)}) async-start(), calls=%async_computation.6 | async-start | bytes 1880064 | tf_op jit(solution)/shard_map/all_gather | solution.py:76
  243.3 95.8 %all-gather.5.cloned.1.call-start = ((), (), s32[]{:S(2)}) async-start(), calls=%async_computation.8 | async-start | bytes 3760128 | tf_op jit(solution)/shard_map/all_gather | solution.py:89
  291.3 47.8 %copy-start.5 = (bf16[1,256,768]{2,1,0:T(8,128)(2,1)S(1)}, bf16[1,256,768]{2,1,0:T(8,128)(2,1)}, u32[]{:S(2)}) copy-start(bf16[1,256,768]{2,1,0:T(8,128)(2,1)} %param.15) | copy-start | bytes 1179652
  292.4 52.0 %all-to-all-start.1 = ((bf16[1,64,18,256]{3,2,0,1:T(8,128)(2,1)}), bf16[1,64,18,256]{3,2,0,1:T(8,128)(2,1)S(1)}, u32[]{:S(2)}, u32[]{:S(2)}) async-start(bf16[1,64,18,256]{3,2,0,1:T(8,128)(2,1)} %bitcast.11), calls=%async_computation.1 | async-start | bytes 1572864 | tf_op jit(solution)/shard_map/all_to_all | solution.py:92
  339.1 2.5 copy-start.1
  344.4 38.1 %all-to-all-start.3 = ((bf16[1,64,18,256]{3,2,0,1:T(8,128)(2,1)}), bf16[1,64,18,256]{3,2,0,1:T(8,128)(2,1)S(1)}, u32[]{:S(2)}, u32[]{:S(2)}) async-start(bf16[1,64,18,256]{3,2,0,1:T(8,128)(2,1)} %bitcast.18), calls=%async_computation.4 | async-start | bytes 1572864 | tf_op jit(solution)/shard_map/all_to_all | solution.py:106
  361.3 5.4 %copy-start.2 = (bf16[1,1152,2,768]{3,1,2,0:T(8,128)(2,1)S(1)}, bf16[1,1152,2,768]{3,1,2,0:T(8,128)(2,1)}, u32[]{:S(2)}) copy-start(bf16[1,1152,2,768]{3,1,2,0:T(8,128)(2,1)} %all-gather.5.cloned.1.call-done) | copy-start | bytes 10616836
Sparse Core Ops, SparseCore 0:
  102.6 72.4 reduce-scatter.6
  178.6 62.9 reduce-scatter.4
  245.2 43.8 all-gather.2
  292.7 46.3 all-gather.4
where the time goes:
time: 391 us; the launch traced here: 390 us
  waiting for transfers between devices  199 us (51%)
  blocking collectives  66.6 us (17%)
  local copies, waits for them, and re-layouts  35.6 us (9%)
  other arithmetic  27.3 us (7%)
  starting transfers between devices  25.9 us (7%)
  matrix products  21.7 us (6%)
  between operations  14.1 us (4%)
    reduce_scatter x1, waiting for transfers between devices, body(): lax.psum_scatter(grad_part.astype(jnp.bfloat16), 'dp', scatter_dimension=...  65.4 us
    all_gather x1, waiting for transfers between devices, body(): hidden_full = lax.all_gather(hidden, 'dp', axis=1, tiled=True)  44.9 us
    unnamed x5, waiting for transfers between devices  40.4 us
    all_to_all x1, blocking collectives, body(): lax.all_to_all(token_send, 'expert', split_axis=1, concat_axis=1, tiled=T...  38.3 us
    all_gather x1, waiting for transfers between devices, body(): gathered = lax.all_gather(derived, 'dp', axis=1, tiled=True)  34 us
    unnamed x28, local copies, waits for them, and re-layouts  30.5 us
    all_to_all x1, blocking collectives, body(): lax.all_to_all(grad_send, 'expert', split_axis=1, concat_axis=1, tiled=True)  28.2 us
    another operation x3, other arithmetic  18.2 us
  transfers between devices with their start and end apart: 6, of which 5 were waited for; matrix products, arithmetic and copies ran while one was open for 6% of the time, Pallas kernels for 0%

commit v1 on v0

v1 whole, which is shorter than its diff:
```python
import functools

import jax
import jax.numpy as jnp
from jax import lax
from jax.experimental import pallas as pl
from jax.experimental.pallas import tpu as pltpu
from jax.sharding import PartitionSpec as P

LOW = jnp.bfloat16
WIDE = jnp.float32


def swish_parts(gate_val):
    sigma = jax.nn.sigmoid(gate_val)
    return (gate_val * sigma, sigma * (1.0 + gate_val * (1.0 - sigma)))


def mul(left, right):
    return jnp.dot(left, right, preferred_element_type=WIDE)


def split_low(values):
    high = values.astype(LOW)
    return high, (values - high.astype(WIDE)).astype(LOW)


def dispatch_kernel(
    capacity,
    routes_ref,
    combine_ref,
    clip_ref,
    limits_ref,
    tokens_ref,
    cot_ref,
    tok_out,
    cot_out,
    rank_out,
    weight_out,
):
    top_count, tok_rows = routes_ref.shape
    experts = limits_ref.shape[0]
    labels = lax.broadcasted_iota(jnp.int32, (experts, tok_rows), 0)
    listed = jnp.zeros((experts, tok_rows), WIDE)
    weight = jnp.zeros((experts, tok_rows), WIDE)
    for entry in range(top_count):
        match = routes_ref[entry : entry + 1, :] == labels
        listed = jnp.where(match, 1.0, listed)
        weight = jnp.where(match, combine_ref[entry : entry + 1, :], weight)
    before = lax.broadcasted_iota(jnp.int32, (tok_rows, tok_rows), 0) < lax.broadcasted_iota(
        jnp.int32, (tok_rows, tok_rows), 1
    )
    rank = mul(listed.astype(LOW), jnp.where(before, 1.0, 0.0).astype(LOW))
    kept = (listed > 0.0) & (rank < limits_ref[...].astype(WIDE))
    rank = jnp.where(kept, rank, -1.0)
    rank_out[...] = rank
    weight_out[...] = weight
    slots = experts * capacity
    first = lax.broadcasted_iota(jnp.int32, (slots, experts), 1) * capacity
    offset = lax.broadcasted_iota(jnp.int32, (slots, experts), 0) - first
    owner = jnp.where((offset >= 0) & (offset < capacity), 1.0, 0.0).astype(LOW)
    place = lax.broadcasted_iota(jnp.int32, (slots, tok_rows), 0).astype(WIDE)
    place = place - capacity * jnp.floor((place + 0.5) * (1.0 / capacity))
    picked = mul(owner, rank.astype(LOW)) == place
    tok_out[...] = mul(jnp.where(picked, 1.0, 0.0).astype(LOW), tokens_ref[...]).astype(LOW)
    high, rest = split_low(weight * clip_ref[...].astype(WIDE))
    coef_high = jnp.where(picked, mul(owner, high), 0.0).astype(LOW)
    coef_rest = jnp.where(picked, mul(owner, rest), 0.0).astype(LOW)
    cot = cot_ref[...]
    cot_out[...] = (mul(coef_high, cot) + mul(coef_rest, cot)).astype(LOW)


def gather_kernel(capacity, rank_ref, weight_ref, pick_out, weight_out):
    experts, tok_rows = rank_ref.shape
    slots = experts * capacity
    first = lax.broadcasted_iota(jnp.int32, (experts, slots), 0) * capacity
    offset = lax.broadcasted_iota(jnp.int32, (experts, slots), 1) - first
    owner = jnp.where((offset >= 0) & (offset < capacity), 1.0, 0.0).astype(LOW)
    place = lax.broadcasted_iota(jnp.int32, (tok_rows, slots), 1).astype(WIDE)
    place = place - capacity * jnp.floor((place + 0.5) * (1.0 / capacity))
    picked = mul(rank_ref[...].T.astype(LOW), owner) == place
    pick_out[...] = jnp.where(picked, 1.0, 0.0).astype(LOW)
    high, rest = split_low(weight_ref[...].T)
    weight_out[0:tok_rows, :] = jnp.where(picked, mul(high, owner), 0.0).astype(LOW)
    weight_out[tok_rows:, :] = jnp.where(picked, mul(rest, owner), 0.0).astype(LOW)


def body(
    tokens, routes, combine, clip_mask, limits, cotangent, gate_weight, up_weight, down_weight
):
    tok_rows, top_count = routes.shape
    experts = limits.shape[0]
    capacity = 9 * tok_rows * top_count // (8 * experts)
    slots = experts * capacity
    half = slots // 2
    width = tokens.shape[1]
    ff = gate_weight.shape[2]
    devices = lax.axis_size("dp")
    chips = devices // 2
    core = lax.axis_index("dp") % 2
    column = [[2 * chip + which for chip in range(chips)] for which in range(2)]
    swap_pairs = [(device, device ^ 1) for device in range(devices)]

    def swap(values):
        return lax.ppermute(values, "dp", swap_pairs)

    def exchange(rows):
        return lax.all_to_all(
            rows.reshape(experts, capacity, width), "expert", split_axis=0, concat_axis=0, tiled=True
        ).reshape(slots, width)

    def halves(rows):
        keep = lax.dynamic_slice_in_dim(rows, core * half, half, axis=0)
        give = lax.dynamic_slice_in_dim(rows, (1 - core) * half, half, axis=0)
        return keep, swap(give)

    def whole(rows):
        mine, got = rows[:, :width], swap(rows[:, width:])
        return jnp.where(
            core == 0, jnp.concatenate([mine, got], axis=0), jnp.concatenate([got, mine], axis=0)
        )

    gu_own = jnp.concatenate([gate_weight[0], up_weight[0]], axis=1)
    down_own = down_weight[0]
    gu_pair = jnp.concatenate([gu_own, swap(gu_own)], axis=0)
    down_pair = jnp.concatenate([down_own, swap(down_own)], axis=1)

    token_send, grad_send, rank, weight = pl.pallas_call(
        functools.partial(dispatch_kernel, capacity),
        out_shape=(
            jax.ShapeDtypeStruct((slots, width), LOW),
            jax.ShapeDtypeStruct((slots, width), LOW),
            jax.ShapeDtypeStruct((experts, tok_rows), WIDE),
            jax.ShapeDtypeStruct((experts, tok_rows), WIDE),
        ),
        compiler_params=pltpu.CompilerParams(vmem_limit_bytes=32 * 1024 * 1024),
        name="dispatch",
    )(
        routes.T,
        combine.T,
        clip_mask.reshape(1, tok_rows),
        limits.reshape(experts, 1),
        tokens,
        cotangent,
    )
    token_keep, token_got = halves(exchange(token_send))
    token_rows = jnp.concatenate([token_keep, token_got], axis=1)
    gate_up = mul(token_rows, gu_pair).astype(LOW)
    shares = lax.psum_scatter(
        gate_up, "dp", scatter_dimension=0, tiled=True, axis_index_groups=column
    ).astype(WIDE)
    grad_keep, grad_got = halves(exchange(grad_send))
    grad_rows = jnp.concatenate([grad_keep, grad_got], axis=1)
    grad_part = (
        lax.dot_general(
            grad_rows, down_pair, (((1,), (1,)), ((), ())), preferred_element_type=WIDE
        )
        .astype(LOW)
        .reshape(chips, half // chips, ff)
    )
    grad_hidden = jnp.sum(
        lax.all_to_all(
            grad_part, "dp", split_axis=0, concat_axis=0, tiled=True, axis_index_groups=column
        ).astype(WIDE),
        axis=0,
    )
    gate_val, up_val = shares[:, :ff], shares[:, ff:]
    active, slope = swish_parts(gate_val)
    hidden = (active * up_val).astype(LOW)
    derived = jnp.concatenate(
        [(grad_hidden * up_val * slope).astype(LOW), (grad_hidden * active).astype(LOW)], axis=1
    )
    derived_full = lax.all_gather(derived, "dp", axis=0, tiled=True, axis_index_groups=column)
    hidden_full = lax.all_gather(hidden, "dp", axis=0, tiled=True, axis_index_groups=column)
    back_rows = exchange(whole(mul(hidden_full, down_pair).astype(LOW)))
    input_rows = lax.dot_general(
        derived_full, gu_pair, (((1,), (1,)), ((), ())), preferred_element_type=WIDE
    ).astype(LOW)
    grads_back = exchange(whole(input_rows))

    def outer(left, right):
        return lax.dot_general(
            left, right, (((0,), (0,)), ((), ())), preferred_element_type=WIDE
        )

    lower_got = swap(outer(hidden_full, grad_got).astype(LOW))
    down_grads = (outer(hidden_full, grad_keep) + lower_got.astype(WIDE)).astype(LOW)
    upper_got = swap(outer(token_got, derived_full).astype(LOW)).astype(WIDE)
    gate_grads = (outer(token_keep, derived_full[:, :ff]) + upper_got[:, :ff]).astype(LOW)
    up_grads = (outer(token_keep, derived_full[:, ff:]) + upper_got[:, ff:]).astype(LOW)

    picked, weights = pl.pallas_call(
        functools.partial(gather_kernel, capacity),
        out_shape=(
            jax.ShapeDtypeStruct((tok_rows, slots), LOW),
            jax.ShapeDtypeStruct((2 * tok_rows, slots), LOW),
        ),
        compiler_params=pltpu.CompilerParams(vmem_limit_bytes=32 * 1024 * 1024),
        name="gather",
    )(rank, weight)
    sums = mul(weights, back_rows)
    layer_out = (sums[:tok_rows] + sums[tok_rows:]).astype(LOW)
    token_grads = mul(picked, grads_back).astype(LOW)
    return (layer_out, token_grads, gate_grads[None], up_grads[None], down_grads[None])


def solution(mesh):
    in_specs = (
        P("expert", "dp"),
        P("expert", None),
        P("expert", None),
        P("expert"),
        P(),
        P("expert", "dp"),
        P("expert", "dp", None),
        P("expert", "dp", None),
        P("expert", None, "dp"),
    )
    out_specs = (
        P("expert", "dp"),
        P("expert", "dp"),
        P("expert", "dp", None),
        P("expert", "dp", None),
        P("expert", None, "dp"),
    )
    return jax.shard_map(body, mesh=mesh, in_specs=in_specs, out_specs=out_specs, check_vma=False)
```

time: 391 us -> 245 us (0.63)
  waiting for transfers between devices: 199 us -> 73.9 us
  local copies, waits for them, and re-layouts: 35.6 us -> 10.2 us
  starting transfers between devices: 25.9 us -> 50.7 us
  other arithmetic: 27.3 us -> 7.62 us
  matrix products: 21.7 us -> 16.4 us
    all_gather x2 -> x1, waiting for transfers between devices: 78.9 us -> 0.02 us  [body(): lax.all_gather(derived, 'dp', axis=0, tiled=True, axis_index_groups=column)]
    reduce_scatter x1, waiting for transfers between devices: 65.4 us -> 0.02 us  [body(): lax.psum_scatter(gate_up, 'dp', scatter_dimension=0, tiled=True, axis_ind...]
    all_to_all x2 -> x4, waiting for transfers between devices: 14.4 us -> 70.7 us  [exchange(): lax.all_to_all(rows.reshape(experts, capacity, width), 'expert', split_ax...]
    unnamed x5 -> x2, waiting for transfers between devices: 40.4 us -> 0.03 us
    all_gather x0 -> x1, blocking collectives: none -> 27.1 us  [body(): lax.all_gather(hidden, 'dp', axis=0, tiled=True, axis_index_groups=column)]
    unnamed x28 -> x32, local copies, waits for them, and re-layouts: 30.5 us -> 4.29 us
    all_to_all x2 -> x1, blocking collectives: 66.6 us -> 41.8 us  [body(): lax.all_to_all(grad_part, 'dp', split_axis=0, concat_axis=0, tiled=True,...]
    another operation x6 -> x0, other arithmetic: 20.9 us -> none
  transfers between devices with their start and end apart: 6 -> 14, of which waited for: 5 -> 6; matrix products, arithmetic and copies ran while one was open for 6% -> 9% of each run, Pallas kernels for 0% -> 0%
where the time goes in v1:
time: 245 us; the launch traced here: 244 us
  waiting for transfers between devices  73.9 us (30%)
  blocking collectives  68.9 us (28%)
  starting transfers between devices  50.7 us (21%)
  matrix products  16.4 us (7%)
  between operations  14.5 us (6%)
  local copies, waits for them, and re-layouts  10.2 us (4%)
  other arithmetic  7.62 us (3%)
    all_to_all x4, waiting for transfers between devices, exchange(): lax.all_to_all(rows.reshape(experts, capacity, width), 'expert', split_ax...  70.7 us
    all_to_all x1, blocking collectives, body(): lax.all_to_all(grad_part, 'dp', split_axis=0, concat_axis=0, tiled=True,...  41.8 us
    all_to_all x4, starting transfers between devices, exchange(): lax.all_to_all(rows.reshape(experts, capacity, width), 'expert', split_ax...  34.5 us
    all_gather x1, blocking collectives, body(): lax.all_gather(hidden, 'dp', axis=0, tiled=True, axis_index_groups=column)  27.1 us
    ppermute x8, starting transfers between devices, swap(): return lax.ppermute(values, 'dp', swap_pairs)  16.1 us
    dot_general x5, matrix products, outer(): lax.dot_general(left, right, (((0,), (0,)), ((), ())), preferred_element_...  7.23 us
    dot_general x4, matrix products, mul(): return jnp.dot(left, right, preferred_element_type=WIDE)  5.5 us
  transfers between devices with their start and end apart: 14, of which 6 were waited for; matrix products, arithmetic and copies ran while one was open for 9% of the time, Pallas kernels for 0%

profile of v1, /device:TPU:4, one launch (start us, length us, event | category | flops | bytes accessed | tf_op | source)
XLA Modules:
  0.0 244.1 jit_solution(781423330277823064)
XLA Ops:
  7.2 0.7 copy.15.limits_ref
  7.9 0.8 copy-done
  8.8 0.8 copy-done.1
  9.6 0.7 copy-done.2
  10.3 0.7 copy-done.3
  11.0 0.7 copy-done.4
  11.6 1.6 dispatch.1
  13.2 1.1 reshape.49
  14.3 17.3 %all-to-all-start = ((bf16[64,18,256]{2,1,0:T(8,128)(2,1)}), bf16[64,18,256]{2,1,0:T(8,128)(2,1)S(1)}, u32[]{:S(2)}, u32[]{:S(2)}) async-start(bf16[64,18,256]{2,1,0:T(8,128)(2,1)} %reshape.49), calls=%async_computation | async-start | bytes 1572864 | tf_op jit(solution)/shard_map/all_to_all | solution.py:108
  31.6 0.0 reduce-scatter.2.cloned.1.call-start
  31.7 0.1 pad_maximum_fusion.1
  31.7 1.9 collective-permute-start.1
  33.7 19.1 %all-to-all-done = bf16[64,18,256]{2,1,0:T(8,128)(2,1)S(1)} async-done(((bf16[64,18,256]{2,1,0:T(8,128)(2,1)}), bf16[64,18,256]{2,1,0:T(8,128)(2,1)S(1)}, u32[]{:S(2)}, u32[]{:S(2)}) %all-to-all-start) | async-done | bytes 589856 | tf_op jit(solution)/shard_map/all_to_all | solution.py:108
  52.8 0.2 reshape.50
  53.0 1.9 collective-permute-start
  55.0 1.5 collective-permute-done
  56.5 3.7 %convolution_convert_fusion = bf16[576,1536]{1,0:T(8,128)(2,1)} fusion(bf16[256,1536]{1,0:T(8,128)(2,1)} %collective-permute-done.1, bf16[256,768]{1,0:T(8,128)(2,1)S(1)} %bitcast.33, bf16[256,768]{1,0:T(8,128)(2,1)} %bitcast.35, bf16[576,256]{1,0:T(8,128)(2,1)S(1)} %collective-permute-done, bf16[576,256]{1,0:T(8,128)(2,1)S(1)} %get-tuple-element.27), kind=kOutput, calls=%fused_computation | convolution fusion | flops 912752640 | bytes 3932160 | tf_op jit(solution)/shard_map/dot_general | solution.py:20
  60.2 0.0 reduce-scatter.2.cloned.1.call-update
  60.2 1.0 reshape.52
  61.3 5.5 %all-to-all-start.2 = ((bf16[64,18,256]{2,1,0:T(8,128)(2,1)}), bf16[64,18,256]{2,1,0:T(8,128)(2,1)S(1)}, u32[]{:S(2)}, u32[]{:S(2)}) async-start(bf16[64,18,256]{2,1,0:T(8,128)(2,1)} %reshape.52), calls=%async_computation.3 | async-start | bytes 1572864 | tf_op jit(solution)/shard_map/all_to_all | solution.py:108
  66.8 0.0 all-gather.2.cloned.1.call-start
  66.8 1.9 collective-permute-start.2
  68.7 23.2 %all-to-all-done.2 = bf16[64,18,256]{2,1,0:T(8,128)(2,1)S(1)} async-done(((bf16[64,18,256]{2,1,0:T(8,128)(2,1)}), bf16[64,18,256]{2,1,0:T(8,128)(2,1)S(1)}, u32[]{:S(2)}, u32[]{:S(2)}) %all-to-all-start.2) | async-done | bytes 589856 | tf_op jit(solution)/shard_map/all_to_all | solution.py:108
  91.9 0.2 reshape.53
  92.1 1.9 collective-permute-start.4
  94.1 1.5 collective-permute-done.4
  95.6 0.7 convolution_convert_fusion.2
  96.3 0.0 copy-done.15
  96.3 41.8 %all_to_all.25 = bf16[8,72,768]{2,1,0:T(8,128)(2,1)S(1)} all-to-all(bf16[8,72,768]{2,1,0:T(8,128)(2,1)S(1)} %bitcast.31), channel_id=1, replica_groups={{0,128,256,384,512,640,768,896},{64,192,320,448,576,704,832,960},{1,129..., dimensions={0} | all-to-all | bytes 1769472 | tf_op jit(solution)/shard_map/all_to_all | solution.py:162
  138.1 0.1 convert_reduce_fusion
  138.3 0.0 reduce-scatter.2.cloned.1.call-done
  138.3 1.0 convert_element_type.55
  139.3 0.2 multiply_convert_fusion.1
  139.5 0.7 pad_maximum_fusion.7
  140.2 27.1 %all_gather.6 = bf16[576,768]{1,0:T(8,128)(2,1)S(1)} all-gather(bf16[72,768]{1,0:T(8,128)(2,1)S(1)} %get-tuple-element.29), channel_id=1, replica_groups={{0,128,256,384,512,640,768,896},{64,192,320,448,576,704,832,960},{1,129..., dimensions={0}, use_global_device_ids=true | all-gather | bytes 995328 | tf_op jit(solution)/shard_map/all_gather | solution.py:174
  167.3 0.6 convolution_convert_fusion.4
  168.0 1.9 collective-permute-start.3
  169.9 0.5 gather.1
  170.4 1.4 fusion.26
  171.8 1.3 maximum_select_fusion
  173.1 1.1 select_n.40
  174.1 6.3 %all-to-all-start.1 = ((bf16[64,18,256]{2,1,0:T(8,128)(2,1)}), bf16[64,18,256]{2,1,0:T(8,128)(2,1)S(1)}, u32[]{:S(2)}, u32[]{:S(2)}) async-start(bf16[64,18,256]{2,1,0:T(8,128)(2,1)} %select_n.40), calls=%async_computation.2 | async-start | bytes 1572864 | tf_op jit(solution)/shard_map/all_to_all | solution.py:108
  180.5 2.2 convolution_convert_fusion.5
  182.7 2.0 collective-permute-start.7
  184.8 0.0 all-gather.2.cloned.1.call-done
  184.8 3.0 %convolution_convert_fusion.3 = bf16[576,512]{1,0:T(8,128)(2,1)S(1)} fusion(bf16[576,1536]{1,0:T(8,128)(2,1)} %all-gather.2.cloned.1.call-done, bf16[256,1536]{1,0:T(8,128)(2,1)} %collective-permute-done.1, bf16[256,768]{1,0:T(8,128)(2,1)S(1)} %bitcast.34, bf16[256,768]{1,0:T(8,128)(2,1)} %bitcast.36), kind=kOutput, calls=%fused_computation.5 | convolution fusion | flops 910983168 | bytes 3932160 | tf_op jit(solution)/shard_map/dot_general | solution.py:176
  187.9 2.4 collective-permute-start.5
  190.3 1.7 convolution_convert_fusion.1
  192.0 2.1 collective-permute-start.6
  194.1 0.3 maximum_select_fusion.1
  194.4 1.1 select_n.42
  195.4 10.6 %all-to-all-done.1 = bf16[64,18,256]{2,1,0:T(8,128)(2,1)S(1)} async-done(((bf16[64,18,256]{2,1,0:T(8,128)(2,1)}), bf16[64,18,256]{2,1,0:T(8,128)(2,1)S(1)}, u32[]{:S(2)}, u32[]{:S(2)}) %all-to-all-start.1) | async-done | bytes 589856 | tf_op jit(solution)/shard_map/all_to_all | solution.py:108
  206.1 5.3 %all-to-all-start.4 = ((bf16[64,18,256]{2,1,0:T(8,128)(2,1)}), bf16[64,18,256]{2,1,0:T(8,128)(2,1)S(1)}, u32[]{:S(2)}, u32[]{:S(2)}) async-start(bf16[64,18,256]{2,1,0:T(8,128)(2,1)} %select_n.42), calls=%async_computation.5 | async-start | bytes 1572864 | tf_op jit(solution)/shard_map/all_to_all | solution.py:108
  211.4 2.1 fusion.12
  213.5 0.2 reshape.51
  213.7 0.3 fusion.25
  214.0 0.6 fusion.16
  214.7 0.5 copy-done.6
  215.2 0.5 fusion
  215.7 1.3 convert_element_type.66
  217.0 1.4 fusion.14
  218.4 17.8 %all-to-all-done.4 = bf16[64,18,256]{2,1,0:T(8,128)(2,1)S(1)} async-done(((bf16[64,18,256]{2,1,0:T(8,128)(2,1)}), bf16[64,18,256]{2,1,0:T(8,128)(2,1)S(1)}, u32[]{:S(2)}, u32[]{:S(2)}) %all-to-all-start.4) | async-done | bytes 589856 | tf_op jit(solution)/shard_map/all_to_all | solution.py:108
  236.2 0.2 reshape.55
  236.4 0.9 convolution_convert_fusion.6
  (36 shorter events, 0.3 us)
Async XLA Ops:
  7.9 0.8 copy-start
  8.8 0.8 copy-start.1
  9.6 0.7 copy-start.2
  10.3 0.7 copy-start.3
  11.0 0.7 copy-start.4
  11.6 20.0 %copy-start.7 = (bf16[1,256,768]{2,1,0:T(8,128)(2,1)S(1)}, bf16[1,256,768]{2,1,0:T(8,128)(2,1)}, u32[]{:S(2)}) copy-start(bf16[1,256,768]{2,1,0:T(8,128)(2,1)} %param.16) | copy-start | bytes 1179652
  11.6 20.1 %copy-start.9 = (bf16[1,256,768]{2,1,0:T(8,128)(2,1)S(1)}, bf16[1,256,768]{2,1,0:T(8,128)(2,1)}, u32[]{:S(2)}) copy-start(bf16[1,256,768]{2,1,0:T(8,128)(2,1)} %param.15) | copy-start | bytes 1179652
  14.3 38.5 %all-to-all-start = ((bf16[64,18,256]{2,1,0:T(8,128)(2,1)}), bf16[64,18,256]{2,1,0:T(8,128)(2,1)S(1)}, u32[]{:S(2)}, u32[]{:S(2)}) async-start(bf16[64,18,256]{2,1,0:T(8,128)(2,1)} %reshape.49), calls=%async_computation | async-start | bytes 1572864 | tf_op jit(solution)/shard_map/all_to_all | solution.py:108
  31.6 106.7 %reduce-scatter.2.cloned.1.call-start = ((), (), s32[]{:S(2)}) async-start(), calls=%async_computation.6 | async-start | bytes 1990656 | tf_op jit(solution)/shard_map/reduce_scatter | solution.py:149
  31.7 23.2 %collective-permute-start.1 = (bf16[256,1536]{1,0:T(8,128)(2,1)S(1)}, bf16[256,1536]{1,0:T(8,128)(2,1)}, u32[]{:S(2)}, u32[]{:S(2)}) collective-permute-start(bf16[256,1536]{1,0:T(8,128)(2,1)S(1)} %pad_maximum_fusion.1), channel_id=1, source_target_pairs={{0,64},{64,0},{128,192},{192,128},{256,320},{320,256},{384,448},{4... | collective-permute-start | bytes 2359304 | tf_op jit(solution)/shard_map/ppermute | solution.py:105
  53.0 3.5 %collective-permute-start = (bf16[576,256]{1,0:T(8,128)(2,1)S(1)}, bf16[576,256]{1,0:T(8,128)(2,1)S(1)}, u32[]{:S(2)}, u32[]{:S(2)}) collective-permute-start(bf16[576,256]{1,0:T(8,128)(2,1)S(1)} %get-tuple-element.28), channel_id=1, source_target_pairs={{0,64},{64,0},{128,192},{192,128},{256,320},{320,256},{384,448},{4... | collective-permute-start | bytes 884744 | tf_op jit(solution)/shard_map/ppermute | solution.py:105
  56.5 3.7 %copy-start.13 = (bf16[576,256]{1,0:T(8,128)(2,1)}, bf16[576,256]{1,0:T(8,128)(2,1)S(1)}, u32[]{:S(2)}) copy-start(bf16[576,256]{1,0:T(8,128)(2,1)S(1)} %collective-permute-done) | copy-start | bytes 884740
  60.2 6.6 %copy-start.10 = (bf16[1,768,256]{2,1,0:T(8,128)(2,1)S(1)}, bf16[1,768,256]{2,1,0:T(8,128)(2,1)}, u32[]{:S(2)}) copy-start(bf16[1,768,256]{2,1,0:T(8,128)(2,1)} %param.17) | copy-start | bytes 1179652
  61.3 30.6 %all-to-all-start.2 = ((bf16[64,18,256]{2,1,0:T(8,128)(2,1)}), bf16[64,18,256]{2,1,0:T(8,128)(2,1)S(1)}, u32[]{:S(2)}, u32[]{:S(2)}) async-start(bf16[64,18,256]{2,1,0:T(8,128)(2,1)} %reshape.52), calls=%async_computation.3 | async-start | bytes 1572864 | tf_op jit(solution)/shard_map/all_to_all | solution.py:108
  66.8 118.0 %all-gather.2.cloned.1.call-start = ((), (), s32[]{:S(2)}) async-start(), calls=%async_computation.7 | async-start | bytes 1990656 | tf_op jit(solution)/shard_map/all_gather | solution.py:173
  66.8 27.3 %collective-permute-start.2 = (bf16[768,256]{1,0:T(8,128)(2,1)S(1)}, bf16[768,256]{1,0:T(8,128)(2,1)S(1)}, u32[]{:S(2)}, u32[]{:S(2)}) collective-permute-start(bf16[768,256]{1,0:T(8,128)(2,1)S(1)} %bitcast.39), channel_id=1, source_target_pairs={{0,64},{64,0},{128,192},{192,128},{256,320},{320,256},{384,448},{4... | collective-permute-start | bytes 1179656 | tf_op jit(solution)/shard_map/ppermute | solution.py:105
  92.1 3.5 %collective-permute-start.4 = (bf16[576,256]{1,0:T(8,128)(2,1)S(1)}, bf16[576,256]{1,0:T(8,128)(2,1)S(1)}, u32[]{:S(2)}, u32[]{:S(2)}) collective-permute-start(bf16[576,256]{1,0:T(8,128)(2,1)S(1)} %get-tuple-element.24), channel_id=1, source_target_pairs={{0,64},{64,0},{128,192},{192,128},{256,320},{320,256},{384,448},{4... | collective-permute-start | bytes 884744 | tf_op jit(solution)/shard_map/ppermute | solution.py:105
  94.1 2.2 copy-start.11
  95.6 0.7 copy-start.15
  138.3 29.0 %copy-start.12 = (bf16[768,256]{1,0:T(8,128)(2,1)S(1)}, bf16[768,256]{1,0:T(8,128)(2,1)}, u32[]{:S(2)}) copy-start(bf16[768,256]{1,0:T(8,128)(2,1)} %copy-done.11) | copy-start | bytes 1179652
  168.0 3.8 %collective-permute-start.3 = (bf16[576,256]{1,0:T(8,128)(2,1)S(1)}, bf16[576,256]{1,0:T(8,128)(2,1)}, u32[]{:S(2)}, u32[]{:S(2)}) collective-permute-start(bf16[576,256]{1,0:T(8,128)(2,1)S(1)} %get-tuple-element.26), channel_id=1, source_target_pairs={{0,64},{64,0},{128,192},{192,128},{256,320},{320,256},{384,448},{4... | collective-permute-start | bytes 884744 | tf_op jit(solution)/shard_map/ppermute | solution.py:105
  174.1 10.6 %copy-start.8 = (bf16[1,256,768]{2,1,0:T(8,128)(2,1)S(1)}, bf16[1,256,768]{2,1,0:T(8,128)(2,1)}, u32[]{:S(2)}) copy-start(bf16[1,256,768]{2,1,0:T(8,128)(2,1)} %param.16) | copy-start | bytes 1179652
  174.1 31.9 %all-to-all-start.1 = ((bf16[64,18,256]{2,1,0:T(8,128)(2,1)}), bf16[64,18,256]{2,1,0:T(8,128)(2,1)S(1)}, u32[]{:S(2)}, u32[]{:S(2)}) async-start(bf16[64,18,256]{2,1,0:T(8,128)(2,1)} %select_n.40), calls=%async_computation.2 | async-start | bytes 1572864 | tf_op jit(solution)/shard_map/all_to_all | solution.py:108
  182.7 7.6 %copy-start.14 = (bf16[576,256]{1,0:T(8,128)(2,1)S(1)}, bf16[576,256]{1,0:T(8,128)(2,1)}, u32[]{:S(2)}) copy-start(bf16[576,256]{1,0:T(8,128)(2,1)} %copy-done.13) | copy-start | bytes 884740
  182.7 28.7 %collective-permute-start.7 = (bf16[768,256]{1,0:T(8,128)(2,1)}, bf16[768,256]{1,0:T(8,128)(2,1)}, u32[]{:S(2)}, u32[]{:S(2)}) collective-permute-start(bf16[768,256]{1,0:T(8,128)(2,1)} %convolution_convert_fusion.5), channel_id=1, source_target_pairs={{0,64},{64,0},{128,192},{192,128},{256,320},{320,256},{384,448},{4... | collective-permute-start | bytes 1179656 | tf_op jit(solution)/shard_map/ppermute | solution.py:105
  184.8 5.5 %copy-start.5 = (bf16[576,1536]{1,0:T(8,128)(2,1)S(1)}, bf16[576,1536]{1,0:T(8,128)(2,1)}, u32[]{:S(2)}) copy-start(bf16[576,1536]{1,0:T(8,128)(2,1)} %all-gather.2.cloned.1.call-done) | copy-start | bytes 5308420
  187.9 6.2 %collective-permute-start.5 = (bf16[576,256]{1,0:T(8,128)(2,1)S(1)}, bf16[576,256]{1,0:T(8,128)(2,1)S(1)}, u32[]{:S(2)}, u32[]{:S(2)}) collective-permute-start(bf16[576,256]{1,0:T(8,128)(2,1)S(1)} %get-tuple-element.22), channel_id=1, source_target_pairs={{0,64},{64,0},{128,192},{192,128},{256,320},{320,256},{384,448},{4... | collective-permute-start | bytes 884744 | tf_op jit(solution)/shard_map/ppermute | solution.py:105
  192.0 23.7 %collective-permute-start.6 = (bf16[256,1536]{1,0:T(8,128)(2,1)}, bf16[256,1536]{1,0:T(8,128)(2,1)}, u32[]{:S(2)}, u32[]{:S(2)}) collective-permute-start(bf16[256,1536]{1,0:T(8,128)(2,1)} %convolution_convert_fusion.1), channel_id=1, source_target_pairs={{0,64},{64,0},{128,192},{192,128},{256,320},{320,256},{384,448},{4... | collective-permute-start | bytes 2359304 | tf_op jit(solution)/shard_map/ppermute | solution.py:105
  206.1 30.1 %all-to-all-start.4 = ((bf16[64,18,256]{2,1,0:T(8,128)(2,1)}), bf16[64,18,256]{2,1,0:T(8,128)(2,1)S(1)}, u32[]{:S(2)}, u32[]{:S(2)}) async-start(bf16[64,18,256]{2,1,0:T(8,128)(2,1)} %select_n.42), calls=%async_computation.5 | async-start | bytes 1572864 | tf_op jit(solution)/shard_map/all_to_all | solution.py:108
  213.7 1.5 copy-start.6
Sparse Core Ops, SparseCore 0:
  60.3 51.4 reduce-scatter.1
  140.3 37.8 all-gather.1

commit v2 on v1

v2 whole, which is shorter than its diff:
```python
import functools

import jax
import jax.numpy as jnp
from jax import lax
from jax.experimental import pallas as pl
from jax.experimental.pallas import tpu as pltpu
from jax.sharding import PartitionSpec as P

LOW = jnp.bfloat16
WIDE = jnp.float32


def swish_parts(gate_val):
    sigma = jax.nn.sigmoid(gate_val)
    return (gate_val * sigma, sigma * (1.0 + gate_val * (1.0 - sigma)))


def mul(left, right):
    return jnp.dot(left, right, preferred_element_type=WIDE)


def split_low(values):
    high = values.astype(LOW)
    return high, (values - high.astype(WIDE)).astype(LOW)


def outer(left, right):
    return lax.dot_general(left, right, (((0,), (0,)), ((), ())), preferred_element_type=WIDE)


def against(left, right):
    return lax.dot_general(left, right, (((1,), (1,)), ((), ())), preferred_element_type=WIDE)


def number(shape, axis):
    return lax.broadcasted_iota(jnp.int32, shape, axis).astype(WIDE)


def low_if(condition):
    return jnp.where(condition, 1.0, 0.0).astype(LOW)


def remainder(values, step):
    return values - step * jnp.floor((values + 0.5) * (1.0 / step))


def owners(shape, slot_axis, chunk):
    offset = number(shape, slot_axis) - chunk * number(shape, 1 - slot_axis)
    return low_if((offset >= 0.0) & (offset < chunk))


def wanted(shape, slot_axis, pad):
    within = remainder(number(shape, slot_axis), 2 * pad)
    left = jnp.where(within < pad, within, -5.0)
    right = jnp.where(within >= pad, within - pad, -5.0)
    return left, right


def token_kernel(
    pad,
    routes_hbm,
    combine_hbm,
    limits_hbm,
    tokens_hbm,
    tok_out,
    rank_out,
    weight_out,
    routes_ref,
    combine_ref,
    limits_ref,
    tokens_ref,
    sems,
):
    copies = [
        pltpu.make_async_copy(source, target, sems.at[at])
        for at, (source, target) in enumerate(
            (
                (routes_hbm, routes_ref),
                (combine_hbm, combine_ref),
                (limits_hbm, limits_ref),
                (tokens_hbm, tokens_ref),
            )
        )
    ]
    for copy in copies:
        copy.start()
    top_count, tok_rows = routes_ref.shape
    experts = limits_ref.shape[1]
    chunk = 2 * pad
    slots = experts * chunk
    owner = owners((slots, experts), 0, chunk)
    left, right = wanted((slots, tok_rows), 0, pad)
    before = number((tok_rows, tok_rows), 0) < number((tok_rows, tok_rows), 1)
    square = (experts, experts)
    for copy in copies:
        copy.wait()
    labels = lax.broadcasted_iota(jnp.int32, (experts, tok_rows), 0)
    listed = jnp.zeros((experts, tok_rows), WIDE)
    weight = jnp.zeros((experts, tok_rows), WIDE)
    for entry in range(top_count):
        match = routes_ref[entry : entry + 1, :] == labels
        listed = jnp.where(match, 1.0, listed)
        weight = jnp.where(match, combine_ref[entry : entry + 1, :], weight)
    rank = mul(listed.astype(LOW), low_if(before))
    diagonal = number(square, 0) == number(square, 1)
    bounds = jnp.where(diagonal, limits_ref[...].astype(WIDE), 0.0)
    kept = (listed > 0.0) & (rank < jnp.sum(bounds, axis=1, keepdims=True))
    rank = jnp.where(kept, rank, -1.0)
    rank_out[...] = rank
    weight_out[...] = weight
    spread = mul(owner, rank.astype(LOW))
    tokens = tokens_ref[...]
    lanes = tokens.shape[1] // 2
    picked = jnp.concatenate([low_if(spread == left), low_if(spread == right)], axis=1)
    sides = jnp.concatenate([tokens[:, :lanes], tokens[:, lanes:]], axis=0)
    tok_out[...] = mul(picked, sides).reshape(experts, chunk, lanes).astype(LOW)


def grad_kernel(pad, rank_ref, weight_ref, clip_ref, cot_ref, cot_out):
    experts, tok_rows = rank_ref.shape
    chunk = 2 * pad
    slots = experts * chunk
    owner = owners((slots, experts), 0, chunk)
    left, right = wanted((slots, tok_rows), 0, pad)
    spread = mul(owner, rank_ref[...].astype(LOW))
    high, rest = split_low(weight_ref[...] * clip_ref[...].astype(WIDE))
    high, rest = mul(owner, high), mul(owner, rest)
    coefs = jnp.concatenate(
        [
            jnp.where(spread == place, part, 0.0).astype(LOW)
            for part in (high, rest)
            for place in (left, right)
        ],
        axis=1,
    )
    cot = cot_ref[...]
    lanes = cot.shape[1] // 2
    sides = jnp.concatenate([cot[:, :lanes], cot[:, lanes:]] * 2, axis=0)
    cot_out[...] = mul(coefs, sides).reshape(experts, chunk, lanes).astype(LOW)


def table_kernel(pad, rank_ref, weight_ref, pick_out, weight_out):
    experts, tok_rows = rank_ref.shape
    chunk = 2 * pad
    slots = experts * chunk
    owner = owners((experts, slots), 1, chunk)
    spread = mul(rank_ref[...].T.astype(LOW), owner)
    high, rest = split_low(weight_ref[...].T)
    high, rest = mul(high, owner), mul(rest, owner)
    for side, place in enumerate(wanted((tok_rows, slots), 1, pad)):
        picked = spread == place
        pick_out[side * tok_rows : (side + 1) * tok_rows, :] = low_if(picked)
        for at, part in enumerate((high, rest)):
            first = (2 * side + at) * tok_rows
            weight_out[first : first + tok_rows, :] = jnp.where(picked, part, 0.0).astype(LOW)


def combine_kernel(parts, table_ref, rows_ref, out_ref):
    tok_rows, width = out_ref.shape
    lanes = width // 2
    sums = mul(table_ref[...], rows_ref[...].reshape(table_ref.shape[1], lanes))
    for side in range(2):
        total = sums[parts * side * tok_rows : (parts * side + 1) * tok_rows]
        for at in range(1, parts):
            first = (parts * side + at) * tok_rows
            total = total + sums[first : first + tok_rows]
        out_ref[:, side * lanes : (side + 1) * lanes] = total.astype(LOW)


def shifts(shape, row_axis, capacity, pad, side):
    row = number(shape, row_axis)
    block = jnp.floor((row + 0.5) * (1.0 / capacity))
    return low_if(
        number(shape, 1 - row_axis) == row + (2 * pad - capacity) * block + pad * side
    )


GROUP = 8


def unpack_kernel(capacity, pad, core_ref, chunks_ref, keep_out, give_out):
    lanes = chunks_ref.shape[2]
    half = chunks_ref.shape[0] // 2
    rows, slots = GROUP * capacity, GROUP * 2 * pad
    moves = [shifts((rows, slots), 0, capacity, pad, side) for side in range(2)]
    core = core_ref[0]
    for out_ref, base in ((keep_out, core * half), (give_out, (1 - core) * half)):
        for at in range(half // GROUP):
            chunk = chunks_ref[pl.ds(base + at * GROUP, GROUP)].reshape(slots, lanes)
            for side in range(2):
                out_ref[at * rows : (at + 1) * rows, side * lanes : (side + 1) * lanes] = mul(
                    moves[side], chunk
                ).astype(LOW)


def pack_kernel(capacity, pad, core_ref, mine_ref, got_ref, chunks_out):
    lanes = chunks_out.shape[2]
    half = chunks_out.shape[0] // 2
    rows, slots = GROUP * capacity, GROUP * 2 * pad
    moves = [shifts((slots, rows), 1, capacity, pad, side) for side in range(2)]
    core = core_ref[0]
    for in_ref, base in ((mine_ref, core * half), (got_ref, (1 - core) * half)):
        for at in range(half // GROUP):
            block = in_ref[at * rows : (at + 1) * rows, :]
            chunk = mul(moves[0], block[:, :lanes]) + mul(moves[1], block[:, lanes:])
            chunks_out[pl.ds(base + at * GROUP, GROUP)] = chunk.reshape(
                GROUP, 2 * pad, lanes
            ).astype(LOW)


def gate_up_kernel(keep_ref, got_ref, gate_ref, up_ref, other_ref, out_ref):
    ff = gate_ref.shape[1]
    keep, got = keep_ref[...], got_ref[...]
    for at, own_ref in enumerate((gate_ref, up_ref)):
        cols = slice(at * ff, (at + 1) * ff)
        out_ref[:, cols] = (mul(keep, own_ref[...]) + mul(got, other_ref[:, cols])).astype(LOW)


def body(
    tokens, routes, combine, clip_mask, limits, cotangent, gate_weight, up_weight, down_weight
):
    tok_rows, top_count = routes.shape
    experts = limits.shape[0]
    capacity = 9 * tok_rows * top_count // (8 * experts)
    pad = -(-capacity // 4) * 4
    half = experts * capacity // 2
    width = tokens.shape[1]
    lanes = width // 2
    slots = experts * 2 * pad
    ff = gate_weight.shape[2]
    devices = lax.axis_size("dp")
    chips = devices // 2
    core = (lax.axis_index("dp") % 2).astype(jnp.int32).reshape(1)
    column = [[2 * chip + which for chip in range(chips)] for which in range(2)]
    swap_pairs = [(device, device ^ 1) for device in range(devices)]
    chunk_shape = jax.ShapeDtypeStruct((experts, 2 * pad, lanes), LOW)
    rank_shape = jax.ShapeDtypeStruct((experts, tok_rows), WIDE)
    half_shape = jax.ShapeDtypeStruct((half, width), LOW)
    tok_shape = jax.ShapeDtypeStruct((tok_rows, width), LOW)
    in_smem = pl.BlockSpec(memory_space=pltpu.SMEM)
    in_vmem = pl.BlockSpec(memory_space=pltpu.VMEM)
    anywhere = pl.BlockSpec(memory_space=pl.ANY)
    params = pltpu.CompilerParams(vmem_limit_bytes=40 * 1024 * 1024)

    def swap(values):
        return lax.ppermute(values, "dp", swap_pairs)

    def exchange(chunks):
        return lax.all_to_all(chunks, "expert", split_axis=0, concat_axis=0, tiled=True)

    def unpack(chunks):
        keep, give = pl.pallas_call(
            functools.partial(unpack_kernel, capacity, pad),
            out_shape=(half_shape, half_shape),
            in_specs=[in_smem, in_vmem],
            compiler_params=params,
            name="unpack",
        )(core, chunks)
        return keep, swap(give)

    def pack(mine, got):
        return pl.pallas_call(
            functools.partial(pack_kernel, capacity, pad),
            out_shape=chunk_shape,
            in_specs=[in_smem, in_vmem, in_vmem],
            compiler_params=params,
            name="pack",
        )(core, mine, got)

    def merge(parts, table, chunks):
        return pl.pallas_call(
            functools.partial(combine_kernel, parts),
            out_shape=tok_shape,
            compiler_params=params,
            name="merge",
        )(table, chunks)

    gate_own, up_own, down_own = gate_weight[0], up_weight[0], down_weight[0]
    gu_own = jnp.concatenate([gate_own, up_own], axis=1)
    gu_other = swap(gu_own)
    down_other = swap(down_own)

    token_send, rank, weight = pl.pallas_call(
        functools.partial(token_kernel, pad),
        out_shape=(chunk_shape, rank_shape, rank_shape),
        in_specs=[anywhere] * 4,
        scratch_shapes=[
            pltpu.VMEM((top_count, tok_rows), jnp.int32),
            pltpu.VMEM((top_count, tok_rows), WIDE),
            pltpu.VMEM((1, experts), jnp.int32),
            pltpu.VMEM((tok_rows, width), LOW),
            pltpu.SemaphoreType.DMA((4,)),
        ],
        compiler_params=params,
        name="token_rows",
    )(routes.T, combine.T, limits.reshape(1, experts), tokens)
    token_keep, token_got = unpack(exchange(token_send))
    gate_up = pl.pallas_call(
        gate_up_kernel,
        out_shape=jax.ShapeDtypeStruct((half, 2 * ff), LOW),
        compiler_params=params,
        name="gate_up",
    )(token_keep, token_got, gate_own, up_own, gu_other)
    shares = lax.psum_scatter(
        gate_up, "dp", scatter_dimension=0, tiled=True, axis_index_groups=column
    ).astype(WIDE)
    grad_send = pl.pallas_call(
        functools.partial(grad_kernel, pad),
        out_shape=chunk_shape,
        compiler_params=params,
        name="grad_rows",
    )(rank, weight, clip_mask.reshape(1, tok_rows), cotangent)
    grad_keep, grad_got = unpack(exchange(grad_send))
    grad_part = (
        (against(grad_keep, down_own) + against(grad_got, down_other))
        .astype(LOW)
        .reshape(chips, half // chips, ff)
    )
    grad_hidden = jnp.sum(
        lax.all_to_all(
            grad_part, "dp", split_axis=0, concat_axis=0, tiled=True, axis_index_groups=column
        ).astype(WIDE),
        axis=0,
    )
    gate_val, up_val = shares[:, :ff], shares[:, ff:]
    active, slope = swish_parts(gate_val)
    hidden = (active * up_val).astype(LOW)
    derived = jnp.concatenate(
        [(grad_hidden * up_val * slope).astype(LOW), (grad_hidden * active).astype(LOW)], axis=1
    )
    derived_full = lax.all_gather(derived, "dp", axis=0, tiled=True, axis_index_groups=column)
    hidden_full = lax.all_gather(hidden, "dp", axis=0, tiled=True, axis_index_groups=column)
    out_got = swap(mul(hidden_full, down_other).astype(LOW))
    back_rows = exchange(pack(mul(hidden_full, down_own).astype(LOW), out_got))
    input_got = swap(against(derived_full, gu_other).astype(LOW))
    grads_back = exchange(pack(against(derived_full, gu_own).astype(LOW), input_got))

    lower_got = swap(outer(hidden_full, grad_got).astype(LOW))
    down_grads = (outer(hidden_full, grad_keep) + lower_got.astype(WIDE)).astype(LOW)
    upper_got = swap(outer(token_got, derived_full).astype(LOW)).astype(WIDE)
    gate_grads = (outer(token_keep, derived_full[:, :ff]) + upper_got[:, :ff]).astype(LOW)
    up_grads = (outer(token_keep, derived_full[:, ff:]) + upper_got[:, ff:]).astype(LOW)

    picks, weights = pl.pallas_call(
        functools.partial(table_kernel, pad),
        out_shape=(
            jax.ShapeDtypeStruct((2 * tok_rows, slots), LOW),
            jax.ShapeDtypeStruct((4 * tok_rows, slots), LOW),
        ),
        compiler_params=params,
        name="tables",
    )(rank, weight)
    layer_out = merge(2, weights, back_rows)
    token_grads = merge(1, picks, grads_back)
    return (layer_out, token_grads, gate_grads[None], up_grads[None], down_grads[None])


def solution(mesh):
    in_specs = (
        P("expert", "dp"),
        P("expert", None),
        P("expert", None),
        P("expert"),
        P(),
        P("expert", "dp"),
        P("expert", "dp", None),
        P("expert", "dp", None),
        P("expert", None, "dp"),
    )
    out_specs = (
        P("expert", "dp"),
        P("expert", "dp"),
        P("expert", "dp", None),
        P("expert", "dp", None),
        P("expert", None, "dp"),
    )
    return jax.shard_map(body, mesh=mesh, in_specs=in_specs, out_specs=out_specs, check_vma=False)
```

time: 245 us -> 244 us (level)
  waiting for transfers between devices: 73.9 us -> 55.2 us
  Pallas kernels: 2.04 us -> 16.2 us
  starting transfers between devices: 50.7 us -> 57.8 us
  blocking collectives: 68.9 us -> 74.3 us
  local copies, waits for them, and re-layouts: 10.2 us -> 5.31 us
  matrix products: 16.4 us -> 13.2 us
    all_to_all x4, waiting for transfers between devices: 70.7 us -> 52.6 us  [exchange(): lax.all_to_all(chunks, 'expert', split_axis=0, concat_axis=0, tiled=True)]
    pallas_call x2 -> x10, Pallas kernels: 2.04 us -> 16.2 us  [the longest x2 3.36 us: pack(): pl.pallas_call(functools.partial(pack_kernel, capacity, pad), out_shape=c...]
    all_to_all x4, starting transfers between devices: 34.5 us -> 41.4 us  [exchange(): lax.all_to_all(chunks, 'expert', split_axis=0, concat_axis=0, tiled=True)]
    all_to_all x1, blocking collectives: 41.8 us -> 47 us  [body(): lax.all_to_all(grad_part, 'dp', split_axis=0, concat_axis=0, tiled=True,...]
    reshape x7 -> x0, local copies, waits for them, and re-layouts: 3.57 us -> none  [the longest x2 2.11 us: exchange(): rows.reshape(experts, capacity, width)]
    dot_general x4 -> x2, matrix products: 5.5 us -> 2.05 us  [mul(): return jnp.dot(left, right, preferred_element_type=WIDE)]
    dot_general x2 -> x4, matrix products: 3.66 us -> 5.01 us  [against(): lax.dot_general(left, right, (((1,), (1,)), ((), ())), preferred_element_...]
    unnamed x32 -> x40, local copies, waits for them, and re-layouts: 4.29 us -> 5.31 us
  transfers between devices with their start and end apart: 14 -> 14, of which waited for: 6 -> 8; matrix products, arithmetic and copies ran while one was open for 9% -> 7% of each run, Pallas kernels for 0% -> 5%
where the time goes in v2:
time: 244 us; the launch traced here: 242 us
  blocking collectives  74.3 us (30%)
  starting transfers between devices  57.8 us (24%)
  waiting for transfers between devices  55.2 us (23%)
  Pallas kernels  16.2 us (7%)
  between operations  14.4 us (6%)
  matrix products  13.2 us (5%)
  other arithmetic  6.02 us (2%)
  local copies, waits for them, and re-layouts  5.31 us (2%)
    all_to_all x4, waiting for transfers between devices, exchange(): lax.all_to_all(chunks, 'expert', split_axis=0, concat_axis=0, tiled=True)  52.6 us
    all_to_all x1, blocking collectives, body(): lax.all_to_all(grad_part, 'dp', split_axis=0, concat_axis=0, tiled=True,...  47 us
    all_to_all x4, starting transfers between devices, exchange(): lax.all_to_all(chunks, 'expert', split_axis=0, concat_axis=0, tiled=True)  41.4 us
    all_gather x1, blocking collectives, body(): lax.all_gather(hidden, 'dp', axis=0, tiled=True, axis_index_groups=column)  27.4 us
    ppermute x8, starting transfers between devices, swap(): return lax.ppermute(values, 'dp', swap_pairs)  16.3 us
    dot_general x5, matrix products, outer(): lax.dot_general(left, right, (((0,), (0,)), ((), ())), preferred_element_...  6.12 us
    unnamed x40, local copies, waits for them, and re-layouts  5.31 us
    dot_general x4, matrix products, against(): lax.dot_general(left, right, (((1,), (1,)), ((), ())), preferred_element_...  5.01 us
  transfers between devices with their start and end apart: 14, of which 8 were waited for; matrix products, arithmetic and copies ran while one was open for 7% of the time, Pallas kernels for 5%

profile of v2, /device:TPU:4, one launch (start us, length us, event | category | flops | bytes accessed | tf_op | source)
XLA Modules:
  0.0 242.5 jit_solution(1048825804990416031)
XLA Ops:
  7.2 0.8 copy-done.6
  8.0 0.7 copy-done.8
  8.7 0.7 copy-done.9
  9.4 0.7 copy-done.10
  10.0 2.9 %token_rows.1 = (bf16[64,40,128]{2,1,0:T(8,128)(2,1)}, f32[64,128]{1,0:T(8,128)S(1)}, f32[64,128]{1,0:T(8,128)S(1)}) custom-call(s32[8,128]{1,0:T(8,128)S(1)} %bitcast.42, f32[8,128]{1,0:T(8,128)S(1)} %bitcast.43, s32[1,64]{1,0:T(1,128)S(1)} %bitcast.44, bf16[128,256]{1,0:T(8,128)(2,1)S(1)} %copy-done.6), custom_call_target="tpu_custom_call" | custom-call | tf_op jit(solution)/shard_map/token_rows/pallas_call | solution.py:284
  13.0 0.0 copy-start.7
  13.0 0.0 copy-start.11
  13.0 17.5 %all-to-all-start = ((bf16[64,40,128]{2,1,0:T(8,128)(2,1)}), bf16[64,40,128]{2,1,0:T(8,128)(2,1)S(1)}, u32[]{:S(2)}, u32[]{:S(2)}) async-start(bf16[64,40,128]{2,1,0:T(8,128)(2,1)} %get-tuple-element.17), calls=%async_computation | async-start | bytes 1310720 | tf_op jit(solution)/shard_map/all_to_all | solution.py:250
  30.5 2.1 pad_maximum_fusion
  32.5 2.0 collective-permute-start.1
  34.6 14.3 %all-to-all-done.chunks_ref = bf16[64,40,128]{2,1,0:T(8,128)(2,1)S(1)} async-done(((bf16[64,40,128]{2,1,0:T(8,128)(2,1)}), bf16[64,40,128]{2,1,0:T(8,128)(2,1)S(1)}, u32[]{:S(2)}, u32[]{:S(2)}) %all-to-all-start) | async-done | bytes 655392 | tf_op jit(solution)/shard_map/all_to_all | solution.py:250
  48.9 0.8 unpack.2
  49.7 1.9 collective-permute-start
  51.6 2.6 %grad_rows.1 = bf16[64,40,128]{2,1,0:T(8,128)(2,1)} custom-call(f32[64,128]{1,0:T(8,128)S(1)} %get-tuple-element.14.rank_ref, f32[64,128]{1,0:T(8,128)S(1)} %get-tuple-element.15.weight_ref, s32[1,128]{1,0:T(1,128)S(1)} %bitcast.45, bf16[128,256]{1,0:T(8,128)(2,1)S(1)} %copy-done.7), custom_call_target="tpu_custom_call" | custom-call | tf_op jit(solution)/shard_map/grad_rows/pallas_call | solution.py:308
  54.2 5.5 %all-to-all-start.2 = ((bf16[64,40,128]{2,1,0:T(8,128)(2,1)}), bf16[64,40,128]{2,1,0:T(8,128)(2,1)S(1)}, u32[]{:S(2)}, u32[]{:S(2)}) async-start(bf16[64,40,128]{2,1,0:T(8,128)(2,1)} %grad_rows.1), calls=%async_computation.3 | async-start | bytes 1310720 | tf_op jit(solution)/shard_map/all_to_all | solution.py:250
  59.7 0.0 reduce-scatter.2.cloned.1.call-start
  59.8 0.0 collective-permute-done.1.other_ref
  59.8 0.0 copy-start.5
  59.8 2.3 gate_up.1
  62.1 0.0 reduce-scatter.2.cloned.1.call-update
  62.2 0.0 all-gather.2.cloned.1.call-start
  62.2 0.9 copy-done.17
  63.1 1.9 collective-permute-start.2
  65.1 17.4 %all-to-all-done.2.chunks_ref = bf16[64,40,128]{2,1,0:T(8,128)(2,1)S(1)} async-done(((bf16[64,40,128]{2,1,0:T(8,128)(2,1)}), bf16[64,40,128]{2,1,0:T(8,128)(2,1)S(1)}, u32[]{:S(2)}, u32[]{:S(2)}) %all-to-all-start.2) | async-done | bytes 655392 | tf_op jit(solution)/shard_map/all_to_all | solution.py:250
  82.5 0.8 unpack.3
  83.3 1.9 collective-permute-start.4
  85.2 0.4 fusion.10
  85.6 1.1 collective-permute-done.4
  86.8 1.5 add_convert_fusion
  88.3 47.0 %all_to_all.25 = bf16[8,72,768]{2,1,0:T(8,128)(2,1)S(1)} all-to-all(bf16[8,72,768]{2,1,0:T(8,128)(2,1)S(1)} %bitcast.46), channel_id=1, replica_groups={{0,128,256,384,512,640,768,896},{64,192,320,448,576,704,832,960},{1,129..., dimensions={0} | all-to-all | bytes 1769472 | tf_op jit(solution)/shard_map/all_to_all | solution.py:321
  135.3 0.1 convert_reduce_fusion
  135.4 0.1 reduce-scatter.2.cloned.1.call-done
  135.5 1.0 convert_element_type.51
  136.4 0.2 multiply_convert_fusion.1
  136.6 0.7 pad_maximum_fusion.1
  137.3 0.0 all-gather.2.cloned.1.call-update
  137.3 27.4 %all_gather.6 = bf16[576,768]{1,0:T(8,128)(2,1)S(1)} all-gather(bf16[72,768]{1,0:T(8,128)(2,1)S(1)} %get-tuple-element.27), channel_id=1, replica_groups={{0,128,256,384,512,640,768,896},{64,192,320,448,576,704,832,960},{1,129..., dimensions={0}, use_global_device_ids=true | all-gather | bytes 995328 | tf_op jit(solution)/shard_map/all_gather | solution.py:333
  164.7 1.7 convolution_convert_fusion.4
  166.4 1.9 collective-permute-start.3
  168.3 0.4 convolution_convert_fusion.5.mine_ref
  168.7 1.1 collective-permute-done.3.got_ref
  169.8 1.7 pack.2
  171.5 13.1 %all-to-all-start.1 = ((bf16[64,40,128]{2,1,0:T(8,128)(2,1)}), bf16[64,40,128]{2,1,0:T(8,128)(2,1)S(1)}, u32[]{:S(2)}, u32[]{:S(2)}) async-start(bf16[64,40,128]{2,1,0:T(8,128)(2,1)} %pack.2), calls=%async_computation.2 | async-start | bytes 1310720 | tf_op jit(solution)/shard_map/all_to_all | solution.py:250
  184.6 0.9 tables.1
  185.6 1.5 copy-done
  187.0 0.2 all-gather.2.cloned.1.call-done
  187.2 2.4 convolution_convert_fusion.2
  189.6 2.1 collective-permute-start.5
  191.7 1.3 convolution_convert_fusion.1
  193.0 2.4 collective-permute-start.7
  195.4 0.7 convolution_convert_fusion.3.mine_ref
  196.1 1.7 pack.3
  197.8 9.4 %all-to-all-done.1.rows_ref = bf16[64,40,128]{2,1,0:T(8,128)(2,1)S(1)} async-done(((bf16[64,40,128]{2,1,0:T(8,128)(2,1)}), bf16[64,40,128]{2,1,0:T(8,128)(2,1)S(1)}, u32[]{:S(2)}, u32[]{:S(2)}) %all-to-all-start.1) | async-done | bytes 655392 | tf_op jit(solution)/shard_map/all_to_all | solution.py:250
  207.1 5.3 %all-to-all-start.4 = ((bf16[64,40,128]{2,1,0:T(8,128)(2,1)}), bf16[64,40,128]{2,1,0:T(8,128)(2,1)S(1)}, u32[]{:S(2)}, u32[]{:S(2)}) async-start(bf16[64,40,128]{2,1,0:T(8,128)(2,1)} %pack.3), calls=%async_computation.5 | async-start | bytes 1310720 | tf_op jit(solution)/shard_map/all_to_all | solution.py:250
  212.4 2.4 %convolution_convert_fusion = bf16[256,1536]{1,0:T(8,128)(2,1)S(1)} fusion(bf16[576,256]{1,0:T(8,128)(2,1)} %copy-done.5, bf16[576,1536]{1,0:T(8,128)(2,1)} %all-gather.2.cloned.1.call-done), kind=kOutput, calls=%fused_computation | convolution fusion | flops 453378048 | bytes 2850816 | tf_op jit(solution)/shard_map/dot_general | solution.py:29
  214.9 2.2 collective-permute-start.6
  217.1 0.5 fusion.15
  217.6 1.8 fusion.6
  219.5 1.5 merge.2
  220.9 0.5 fusion
  221.5 0.2 convert_element_type.62
  221.6 1.4 fusion.8
  223.0 11.5 %all-to-all-done.4.rows_ref = bf16[64,40,128]{2,1,0:T(8,128)(2,1)S(1)} async-done(((bf16[64,40,128]{2,1,0:T(8,128)(2,1)}), bf16[64,40,128]{2,1,0:T(8,128)(2,1)S(1)}, u32[]{:S(2)}, u32[]{:S(2)}) %all-to-all-start.4) | async-done | bytes 655392 | tf_op jit(solution)/shard_map/all_to_all | solution.py:250
  234.5 1.1 merge.3
  (36 shorter events, 0.1 us)
Async XLA Ops:
  7.2 0.8 copy-start.6
  8.0 0.7 copy-start.8
  8.7 0.7 copy-start.9
  9.4 0.7 copy-start.10
  13.0 38.7 %copy-start.7 = (bf16[128,256]{1,0:T(8,128)(2,1)S(1)}, bf16[128,256]{1,0:T(8,128)(2,1)}, u32[]{:S(2)}) copy-start(bf16[128,256]{1,0:T(8,128)(2,1)} %cot_ref.1) | copy-start | bytes 196612
  13.0 38.7 %copy-start.11 = (s32[128]{0:T(128)S(1)}, s32[128]{0:T(128)}, u32[]{:S(2)}) copy-start(s32[128]{0:T(128)} %param.12) | copy-start | bytes 1540
  13.0 35.9 %all-to-all-start = ((bf16[64,40,128]{2,1,0:T(8,128)(2,1)}), bf16[64,40,128]{2,1,0:T(8,128)(2,1)S(1)}, u32[]{:S(2)}, u32[]{:S(2)}) async-start(bf16[64,40,128]{2,1,0:T(8,128)(2,1)} %get-tuple-element.17), calls=%async_computation | async-start | bytes 1310720 | tf_op jit(solution)/shard_map/all_to_all | solution.py:250
  32.5 27.3 %copy-start.2 = (bf16[1,256,768]{2,1,0:T(8,128)(2,1)S(1)}, bf16[1,256,768]{2,1,0:T(8,128)(2,1)}, u32[]{:S(2)}) copy-start(bf16[1,256,768]{2,1,0:T(8,128)(2,1)} %param.15) | copy-start | bytes 1179652
  32.5 27.3 %copy-start.3 = (bf16[1,256,768]{2,1,0:T(8,128)(2,1)S(1)}, bf16[1,256,768]{2,1,0:T(8,128)(2,1)}, u32[]{:S(2)}) copy-start(bf16[1,256,768]{2,1,0:T(8,128)(2,1)} %param.16) | copy-start | bytes 1179652
  32.5 27.2 %collective-permute-start.1 = (bf16[256,1536]{1,0:T(8,128)(2,1)}, bf16[256,1536]{1,0:T(8,128)(2,1)S(1)}, u32[]{:S(2)}, u32[]{:S(2)}) collective-permute-start(bf16[256,1536]{1,0:T(8,128)(2,1)} %pad_maximum_fusion), channel_id=1, source_target_pairs={{0,64},{64,0},{128,192},{192,128},{256,320},{320,256},{384,448},{4... | collective-permute-start | bytes 2359304 | tf_op jit(solution)/shard_map/ppermute | solution.py:247
  49.7 10.1 %collective-permute-start = (bf16[576,256]{1,0:T(8,128)(2,1)S(1)}, bf16[576,256]{1,0:T(8,128)(2,1)S(1)}, u32[]{:S(2)}, u32[]{:S(2)}) collective-permute-start(bf16[576,256]{1,0:T(8,128)(2,1)S(1)} %get-tuple-element.19), channel_id=1, source_target_pairs={{0,64},{64,0},{128,192},{192,128},{256,320},{320,256},{384,448},{4... | collective-permute-start | bytes 884744 | tf_op jit(solution)/shard_map/ppermute | solution.py:247
  54.2 28.3 %all-to-all-start.2 = ((bf16[64,40,128]{2,1,0:T(8,128)(2,1)}), bf16[64,40,128]{2,1,0:T(8,128)(2,1)S(1)}, u32[]{:S(2)}, u32[]{:S(2)}) async-start(bf16[64,40,128]{2,1,0:T(8,128)(2,1)} %grad_rows.1), calls=%async_computation.3 | async-start | bytes 1310720 | tf_op jit(solution)/shard_map/all_to_all | solution.py:250
  59.7 75.7 %reduce-scatter.2.cloned.1.call-start = ((), (), s32[]{:S(2)}) async-start(), calls=%async_computation.6 | async-start | bytes 1990656 | tf_op jit(solution)/shard_map/reduce_scatter | solution.py:305
  59.8 2.4 copy-start.4
  59.8 2.3 copy-start.5
  62.1 1.0 copy-start.17
  62.2 125.0 %all-gather.2.cloned.1.call-start = ((), (), s32[]{:S(2)}) async-start(), calls=%async_computation.7 | async-start | bytes 1990656 | tf_op jit(solution)/shard_map/all_gather | solution.py:332
  63.1 22.5 %collective-permute-start.2 = (bf16[768,256]{1,0:T(8,128)(2,1)S(1)}, bf16[768,256]{1,0:T(8,128)(2,1)}, u32[]{:S(2)}, u32[]{:S(2)}) collective-permute-start(bf16[768,256]{1,0:T(8,128)(2,1)S(1)} %bitcast.47), channel_id=1, source_target_pairs={{0,64},{64,0},{128,192},{192,128},{256,320},{320,256},{384,448},{4... | collective-permute-start | bytes 1179656 | tf_op jit(solution)/shard_map/ppermute | solution.py:247
  83.3 3.5 %collective-permute-start.4 = (bf16[576,256]{1,0:T(8,128)(2,1)S(1)}, bf16[576,256]{1,0:T(8,128)(2,1)S(1)}, u32[]{:S(2)}, u32[]{:S(2)}) collective-permute-start(bf16[576,256]{1,0:T(8,128)(2,1)S(1)} %get-tuple-element.22), channel_id=1, source_target_pairs={{0,64},{64,0},{128,192},{192,128},{256,320},{320,256},{384,448},{4... | collective-permute-start | bytes 884744 | tf_op jit(solution)/shard_map/ppermute | solution.py:247
  86.8 48.5 %copy-start.18 = (bf16[576,256]{1,0:T(8,128)(2,1)}, bf16[576,256]{1,0:T(8,128)(2,1)S(1)}, u32[]{:S(2)}) copy-start(bf16[576,256]{1,0:T(8,128)(2,1)S(1)} %collective-permute-done.4) | copy-start | bytes 884740
  164.7 3.6 %copy-start.14 = (bf16[576,768]{1,0:T(8,128)(2,1)}, bf16[576,768]{1,0:T(8,128)(2,1)S(1)}, u32[]{:S(2)}) copy-start(bf16[576,768]{1,0:T(8,128)(2,1)S(1)} %all_gather.6) | copy-start | bytes 2654212
  166.4 3.5 %collective-permute-start.3 = (bf16[576,256]{1,0:T(8,128)(2,1)S(1)}, bf16[576,256]{1,0:T(8,128)(2,1)S(1)}, u32[]{:S(2)}, u32[]{:S(2)}) collective-permute-start(bf16[576,256]{1,0:T(8,128)(2,1)S(1)} %convolution_convert_fusion.4), channel_id=1, source_target_pairs={{0,64},{64,0},{128,192},{192,128},{256,320},{320,256},{384,448},{4... | collective-permute-start | bytes 884744 | tf_op jit(solution)/shard_map/ppermute | solution.py:247
  171.5 35.6 %all-to-all-start.1 = ((bf16[64,40,128]{2,1,0:T(8,128)(2,1)}), bf16[64,40,128]{2,1,0:T(8,128)(2,1)S(1)}, u32[]{:S(2)}, u32[]{:S(2)}) async-start(bf16[64,40,128]{2,1,0:T(8,128)(2,1)} %pack.2), calls=%async_computation.2 | async-start | bytes 1310720 | tf_op jit(solution)/shard_map/all_to_all | solution.py:250
  185.5 1.5 copy-start
  187.2 4.5 %copy-start.15 = (bf16[576,768]{1,0:T(8,128)(2,1)S(1)}, bf16[576,768]{1,0:T(8,128)(2,1)}, u32[]{:S(2)}) copy-start(bf16[576,768]{1,0:T(8,128)(2,1)} %copy-done.14) | copy-start | bytes 2654212
  187.2 4.5 %copy-start.19 = (bf16[576,256]{1,0:T(8,128)(2,1)S(1)}, bf16[576,256]{1,0:T(8,128)(2,1)}, u32[]{:S(2)}) copy-start(bf16[576,256]{1,0:T(8,128)(2,1)} %copy-done.18) | copy-start | bytes 884740
  189.6 5.8 %copy-start.12 = (bf16[576,1536]{1,0:T(8,128)(2,1)S(1)}, bf16[576,1536]{1,0:T(8,128)(2,1)}, u32[]{:S(2)}) copy-start(bf16[576,1536]{1,0:T(8,128)(2,1)} %all-gather.2.cloned.1.call-done) | copy-start | bytes 5308420
  189.6 6.4 %collective-permute-start.5 = (bf16[576,256]{1,0:T(8,128)(2,1)S(1)}, bf16[576,256]{1,0:T(8,128)(2,1)S(1)}, u32[]{:S(2)}, u32[]{:S(2)}) collective-permute-start(bf16[576,256]{1,0:T(8,128)(2,1)S(1)} %convolution_convert_fusion.2), channel_id=1, source_target_pairs={{0,64},{64,0},{128,192},{192,128},{256,320},{320,256},{384,448},{4... | collective-permute-start | bytes 884744 | tf_op jit(solution)/shard_map/ppermute | solution.py:247
  193.0 24.6 %collective-permute-start.7 = (bf16[768,256]{1,0:T(8,128)(2,1)}, bf16[768,256]{1,0:T(8,128)(2,1)}, u32[]{:S(2)}, u32[]{:S(2)}) collective-permute-start(bf16[768,256]{1,0:T(8,128)(2,1)} %convolution_convert_fusion.1), channel_id=1, source_target_pairs={{0,64},{64,0},{128,192},{192,128},{256,320},{320,256},{384,448},{4... | collective-permute-start | bytes 1179656 | tf_op jit(solution)/shard_map/ppermute | solution.py:247
  207.1 27.4 %all-to-all-start.4 = ((bf16[64,40,128]{2,1,0:T(8,128)(2,1)}), bf16[64,40,128]{2,1,0:T(8,128)(2,1)S(1)}, u32[]{:S(2)}, u32[]{:S(2)}) async-start(bf16[64,40,128]{2,1,0:T(8,128)(2,1)} %pack.3), calls=%async_computation.5 | async-start | bytes 1310720 | tf_op jit(solution)/shard_map/all_to_all | solution.py:250
  212.4 4.7 %copy-start.16 = (bf16[576,768]{1,0:T(8,128)(2,1)S(1)}, bf16[576,768]{1,0:T(8,128)(2,1)}, u32[]{:S(2)}) copy-start(bf16[576,768]{1,0:T(8,128)(2,1)} %copy-done.14) | copy-start | bytes 2654212
  214.9 4.6 %copy-start.1 = (bf16[512,2560]{1,0:T(8,128)(2,1)S(1)}, bf16[512,2560]{1,0:T(8,128)(2,1)}, u32[]{:S(2)}) copy-start(bf16[512,2560]{1,0:T(8,128)(2,1)} %copy-done) | copy-start | bytes 7864324
  214.9 6.5 %collective-permute-start.6 = (bf16[256,1536]{1,0:T(8,128)(2,1)S(1)}, bf16[256,1536]{1,0:T(8,128)(2,1)S(1)}, u32[]{:S(2)}, u32[]{:S(2)}) collective-permute-start(bf16[256,1536]{1,0:T(8,128)(2,1)S(1)} %convolution_convert_fusion), channel_id=1, source_target_pairs={{0,64},{64,0},{128,192},{192,128},{256,320},{320,256},{384,448},{4... | collective-permute-start | bytes 2359304 | tf_op jit(solution)/shard_map/ppermute | solution.py:247
  219.5 1.5 copy-start.13
Sparse Core Ops, SparseCore 0:
  64.0 71.4 reduce-scatter.1
  138.7 48.4 all-gather.1

commit v3 on v2

--- a/solution.py
+++ b/solution.py
@@ -217,6 +217,17 @@
         out_ref[:, cols] = (mul(keep, own_ref[...]) + mul(got, other_ref[:, cols])).astype(LOW)
 
 
+def hidden_grad_kernel(parity_ref, keep_ref, got_ref, own_ref, other_ref, stay_out, leave_out):
+    block = stay_out.shape[1]
+    parts = against(keep_ref[...], own_ref[...]) + against(got_ref[...], other_ref[...])
+    odd = parity_ref[0] == 1
+    for at in range(stay_out.shape[0]):
+        first = parts[2 * at * block : (2 * at + 1) * block]
+        second = parts[(2 * at + 1) * block : (2 * at + 2) * block]
+        stay_out[at] = jnp.where(odd, second, first).astype(LOW)
+        leave_out[at] = jnp.where(odd, first, second).astype(LOW)
+
+
 def body(
     tokens, routes, combine, clip_mask, limits, cotangent, gate_weight, up_weight, down_weight
 ):
@@ -231,9 +242,18 @@
     ff = gate_weight.shape[2]
     devices = lax.axis_size("dp")
     chips = devices // 2
-    core = (lax.axis_index("dp") % 2).astype(jnp.int32).reshape(1)
+    spot = lax.axis_index("dp").astype(jnp.int32)
+    core = (spot % 2).reshape(1)
+    parity = (spot // 2 % 2).reshape(1)
     column = [[2 * chip + which for chip in range(chips)] for which in range(2)]
     swap_pairs = [(device, device ^ 1) for device in range(devices)]
+    near_pairs = []
+    for chip in range(chips):
+        near_pairs.append((2 * chip, 2 * (chip ^ 1)))
+        near_pairs.append((2 * chip + 1, 2 * ((((chip - 1) ^ 1) + 1) % chips) + 1))
+    alike = [
+        [2 * chip + which for chip in range(first, chips, 2)] for which in range(2) for first in range(2)
+    ]
     chunk_shape = jax.ShapeDtypeStruct((experts, 2 * pad, lanes), LOW)
     rank_shape = jax.ShapeDtypeStruct((experts, tok_rows), WIDE)
     half_shape = jax.ShapeDtypeStruct((half, width), LOW)
@@ -292,7 +312,7 @@
             pltpu.VMEM((tok_rows, width), LOW),
             pltpu.SemaphoreType.DMA((4,)),
         ],
-        compiler_params=params,
+        compiler_params=pltpu.CompilerParams(vmem_limit_bytes=63 * 1024 * 1024),
         name="token_rows",
     )(routes.T, combine.T, limits.reshape(1, experts), tokens)
     token_keep, token_got = unpack(exchange(token_send))
@@ -302,24 +322,29 @@
         compiler_params=params,
         name="gate_up",
     )(token_keep, token_got, gate_own, up_own, gu_other)
-    shares = lax.psum_scatter(
-        gate_up, "dp", scatter_dimension=0, tiled=True, axis_index_groups=column
-    ).astype(WIDE)
     grad_send = pl.pallas_call(
         functools.partial(grad_kernel, pad),
         out_shape=chunk_shape,
         compiler_params=params,
         name="grad_rows",
     )(rank, weight, clip_mask.reshape(1, tok_rows), cotangent)
+    gate_up, grad_send = lax.optimization_barrier((gate_up, grad_send))
+    shares = lax.psum_scatter(
+        gate_up, "dp", scatter_dimension=0, tiled=True, axis_index_groups=column
+    ).astype(WIDE)
     grad_keep, grad_got = unpack(exchange(grad_send))
-    grad_part = (
-        (against(grad_keep, down_own) + against(grad_got, down_other))
-        .astype(LOW)
-        .reshape(chips, half // chips, ff)
-    )
+    part_shape = jax.ShapeDtypeStruct((chips // 2, half // chips, ff), LOW)
+    stay, leave = pl.pallas_call(
+        hidden_grad_kernel,
+        out_shape=(part_shape, part_shape),
+        in_specs=[in_smem] + [in_vmem] * 4,
+        compiler_params=params,
+        name="hidden_grad",
+    )(parity, grad_keep, grad_got, down_own, down_other)
+    joined = (stay.astype(WIDE) + lax.ppermute(leave, "dp", near_pairs).astype(WIDE)).astype(LOW)
     grad_hidden = jnp.sum(
         lax.all_to_all(
-            grad_part, "dp", split_axis=0, concat_axis=0, tiled=True, axis_index_groups=column
+            joined, "dp", split_axis=0, concat_axis=0, tiled=True, axis_index_groups=alike
         ).astype(WIDE),
         axis=0,
     )

time: 244 us -> 234 us (0.959)
  blocking collectives: 74.3 us -> 54.2 us
  waiting for transfers between devices: 55.2 us -> 68.9 us
  matrix products: 13.2 us -> 9.9 us
    all_to_all x1, blocking collectives: 47 us -> 26.3 us  [body(): lax.all_to_all(joined, 'dp', split_axis=0, concat_axis=0, tiled=True, axi...]
    ppermute x0 -> x1, waiting for transfers between devices: none -> 9.77 us  [body(): lax.ppermute(leave, 'dp', near_pairs).astype(WIDE)]
    all_to_all x4, starting transfers between devices: 41.4 us -> 36 us  [exchange(): lax.all_to_all(chunks, 'expert', split_axis=0, concat_axis=0, tiled=True)]
    ppermute x0 -> x1, starting transfers between devices: none -> 4.93 us  [body(): lax.ppermute(leave, 'dp', near_pairs).astype(WIDE)]
    all_to_all x4, waiting for transfers between devices: 52.6 us -> 56.2 us  [exchange(): lax.all_to_all(chunks, 'expert', split_axis=0, concat_axis=0, tiled=True)]
    dot_general x4 -> x2, matrix products: 5.01 us -> 3.05 us  [against(): lax.dot_general(left, right, (((1,), (1,)), ((), ())), preferred_element_...]
    unnamed x40 -> x44, local copies, waits for them, and re-layouts: 5.31 us -> 3.35 us
  transfers between devices with their start and end apart: 14 -> 15, of which waited for: 8 -> 7; matrix products, arithmetic and copies ran while one was open for 7% -> 6% of each run, Pallas kernels for 5% -> 5%
where the time goes in v3:
time: 234 us; the launch traced here: 233 us
  waiting for transfers between devices  68.9 us (29%)
  starting transfers between devices  57.2 us (24%)
  blocking collectives  54.2 us (23%)
  Pallas kernels  17.5 us (7%)
  between operations  14.6 us (6%)
  matrix products  9.9 us (4%)
  other arithmetic  7.71 us (3%)
  local copies, waits for them, and re-layouts  3.35 us (1%)
    all_to_all x4, waiting for transfers between devices, exchange(): lax.all_to_all(chunks, 'expert', split_axis=0, concat_axis=0, tiled=True)  56.2 us
    all_to_all x4, starting transfers between devices, exchange(): lax.all_to_all(chunks, 'expert', split_axis=0, concat_axis=0, tiled=True)  36 us
    all_gather x1, blocking collectives, body(): lax.all_gather(hidden, 'dp', axis=0, tiled=True, axis_index_groups=column)  27.9 us
    all_to_all x1, blocking collectives, body(): lax.all_to_all(joined, 'dp', split_axis=0, concat_axis=0, tiled=True, axi...  26.3 us
    ppermute x8, starting transfers between devices, swap(): return lax.ppermute(values, 'dp', swap_pairs)  16.2 us
    ppermute x1, waiting for transfers between devices, body(): lax.ppermute(leave, 'dp', near_pairs).astype(WIDE)  9.77 us
    dot_general x5, matrix products, outer(): lax.dot_general(left, right, (((0,), (0,)), ((), ())), preferred_element_...  6.05 us
    ppermute x1, starting transfers between devices, body(): lax.ppermute(leave, 'dp', near_pairs).astype(WIDE)  4.93 us
  transfers between devices with their start and end apart: 15, of which 7 were waited for; matrix products, arithmetic and copies ran while one was open for 6% of the time, Pallas kernels for 5%

profile of v3, /device:TPU:4, one launch (start us, length us, event | category | flops | bytes accessed | tf_op | source)
XLA Modules:
  0.0 233.3 jit_solution(16969090825954193604)
XLA Ops:
  7.2 2.8 %token_rows.1 = (bf16[64,40,128]{2,1,0:T(8,128)(2,1)}, f32[64,128]{1,0:T(8,128)}, f32[64,128]{1,0:T(8,128)}) custom-call(s32[8,128]{1,0:T(8,128)} %bitcast.40, f32[8,128]{1,0:T(8,128)} %bitcast.41, s32[1,64]{1,0:T(1,128)} %bitcast.42, bf16[128,256]{1,0:T(8,128)(2,1)} %tokens_hbm.1), custom_call_target="tpu_custom_call" | custom-call | tf_op jit(solution)/shard_map/token_rows/pallas_call | solution.py:304
  10.0 0.0 copy-start.13
  10.0 0.0 copy-start.15
  10.1 0.0 copy-start.16
  10.1 17.5 %all-to-all-start = ((bf16[64,40,128]{2,1,0:T(8,128)(2,1)}), bf16[64,40,128]{2,1,0:T(8,128)(2,1)S(1)}, u32[]{:S(2)}, u32[]{:S(2)}) async-start(bf16[64,40,128]{2,1,0:T(8,128)(2,1)} %get-tuple-element.21), calls=%async_computation | async-start | bytes 1310720 | tf_op jit(solution)/shard_map/all_to_all | solution.py:270
  27.6 0.0 copy-start.3
  27.6 0.0 reduce-scatter.2.cloned.1.call-start
  27.6 2.1 pad_maximum_fusion
  29.7 1.9 collective-permute-start.1
  31.7 14.3 %all-to-all-done.chunks_ref = bf16[64,40,128]{2,1,0:T(8,128)(2,1)S(1)} async-done(((bf16[64,40,128]{2,1,0:T(8,128)(2,1)}), bf16[64,40,128]{2,1,0:T(8,128)(2,1)S(1)}, u32[]{:S(2)}, u32[]{:S(2)}) %all-to-all-start) | async-done | bytes 655392 | tf_op jit(solution)/shard_map/all_to_all | solution.py:270
  46.0 0.8 unpack.2
  46.8 1.9 collective-permute-start
  48.8 2.5 %grad_rows.1 = bf16[64,40,128]{2,1,0:T(8,128)(2,1)} custom-call(f32[64,128]{1,0:T(8,128)S(1)} %copy-done.13, f32[64,128]{1,0:T(8,128)S(1)} %copy-done.14, s32[1,128]{1,0:T(1,128)S(1)} %bitcast.39, bf16[128,256]{1,0:T(8,128)(2,1)S(1)} %copy-done.15), custom_call_target="tpu_custom_call" | custom-call | tf_op jit(solution)/shard_map/grad_rows/pallas_call | solution.py:325
  51.3 0.0 copy-start.11
  51.3 2.3 gate_up.1
  53.7 0.0 reduce-scatter.2.cloned.1.call-update
  53.7 5.6 %all-to-all-start.2 = ((bf16[64,40,128]{2,1,0:T(8,128)(2,1)}), bf16[64,40,128]{2,1,0:T(8,128)(2,1)S(1)}, u32[]{:S(2)}, u32[]{:S(2)}) async-start(bf16[64,40,128]{2,1,0:T(8,128)(2,1)} %grad_rows.1), calls=%async_computation.3 | async-start | bytes 1310720 | tf_op jit(solution)/shard_map/all_to_all | solution.py:270
  59.3 0.0 all-gather.2.cloned.1.call-start
  59.4 1.9 collective-permute-start.2
  61.3 20.8 %all-to-all-done.2.chunks_ref = bf16[64,40,128]{2,1,0:T(8,128)(2,1)S(1)} async-done(((bf16[64,40,128]{2,1,0:T(8,128)(2,1)}), bf16[64,40,128]{2,1,0:T(8,128)(2,1)S(1)}, u32[]{:S(2)}, u32[]{:S(2)}) %all-to-all-start.2) | async-done | bytes 655392 | tf_op jit(solution)/shard_map/all_to_all | solution.py:270
  82.1 1.5 unpack.3
  83.6 0.7 copy-done.6
  84.3 1.9 collective-permute-start.4
  86.3 1.7 collective-permute-done.4.got_ref
  88.0 1.1 copy-done.7
  89.1 0.7 hidden_grad.1
  89.7 4.9 %collective-permute-start.5 = (bf16[4,72,768]{2,1,0:T(8,128)(2,1)S(1)}, bf16[4,72,768]{2,1,0:T(8,128)(2,1)S(1)}, u32[]{:S(2)}, u32[]{:S(2)}) collective-permute-start(bf16[4,72,768]{2,1,0:T(8,128)(2,1)S(1)} %get-tuple-element.30), channel_id=1, source_target_pairs={{0,128},{64,960},{128,0},{192,320},{256,384},{320,192},{384,256},{... | collective-permute-start | bytes 1327112 | tf_op jit(solution)/shard_map/ppermute | solution.py:344
  94.7 9.8 %collective-permute-done.5 = bf16[4,72,768]{2,1,0:T(8,128)(2,1)S(1)} collective-permute-done((bf16[4,72,768]{2,1,0:T(8,128)(2,1)S(1)}, bf16[4,72,768]{2,1,0:T(8,128)(2,1)S(1)}, u32[]{:S(2)}, u32[]{:S(2)}) %collective-permute-start.5) | collective-permute-done | bytes 442400 | tf_op jit(solution)/shard_map/ppermute | solution.py:344
  104.5 0.1 add_convert_fusion
  104.6 26.3 %all_to_all.25 = bf16[4,72,768]{2,1,0:T(8,128)(2,1)S(1)} all-to-all(bf16[4,72,768]{2,1,0:T(8,128)(2,1)S(1)} %add_convert_fusion), channel_id=1, replica_groups={{0,256,512,768},{128,384,640,896},{64,320,576,832},{192,448,704,960},{1..., dimensions={0} | all-to-all | bytes 884736 | tf_op jit(solution)/shard_map/all_to_all | solution.py:346
  130.9 0.7 convert_reduce_fusion
  131.6 1.0 convert_element_type.57
  132.6 1.1 multiply_convert_fusion.1
  133.7 0.7 pad_maximum_fusion.1
  134.4 0.0 all-gather.2.cloned.1.call-update
  134.4 27.9 %all_gather.6 = bf16[576,768]{1,0:T(8,128)(2,1)S(1)} all-gather(bf16[72,768]{1,0:T(8,128)(2,1)S(1)} %get-tuple-element.35), channel_id=1, replica_groups={{0,128,256,384,512,640,768,896},{64,192,320,448,576,704,832,960},{1,129..., dimensions={0}, use_global_device_ids=true | all-gather | bytes 995328 | tf_op jit(solution)/shard_map/all_gather | solution.py:358
  162.3 0.4 convolution_convert_fusion.4
  162.7 1.9 collective-permute-start.3
  164.7 0.4 convolution_convert_fusion.5.mine_ref
  165.1 1.1 collective-permute-done.3.got_ref
  166.2 1.7 pack.2
  167.9 7.6 %all-to-all-start.1 = ((bf16[64,40,128]{2,1,0:T(8,128)(2,1)}), bf16[64,40,128]{2,1,0:T(8,128)(2,1)S(1)}, u32[]{:S(2)}, u32[]{:S(2)}) async-start(bf16[64,40,128]{2,1,0:T(8,128)(2,1)} %pack.2), calls=%async_computation.2 | async-start | bytes 1310720 | tf_op jit(solution)/shard_map/all_to_all | solution.py:270
  175.5 0.9 tables.1
  176.4 1.5 copy-done
  177.9 2.4 %convolution_convert_fusion.2 = bf16[576,256]{1,0:T(8,128)(2,1)S(1)} fusion(bf16[576,1536]{1,0:T(8,128)(2,1)} %all-gather.2.cloned.1.call-done, bf16[256,1536]{1,0:T(8,128)(2,1)} %copy-done.4), kind=kOutput, calls=%fused_computation.2 | convolution fusion | flops 453132288 | bytes 2850816 | tf_op jit(solution)/shard_map/dot_general | solution.py:33
  180.3 2.1 collective-permute-start.6
  182.3 1.3 convolution_convert_fusion.1
  183.6 2.4 %collective-permute-start.8 = (bf16[768,256]{1,0:T(8,128)(2,1)}, bf16[768,256]{1,0:T(8,128)(2,1)}, u32[]{:S(2)}, u32[]{:S(2)}) collective-permute-start(bf16[768,256]{1,0:T(8,128)(2,1)} %convolution_convert_fusion.1), channel_id=1, source_target_pairs={{0,64},{64,0},{128,192},{192,128},{256,320},{320,256},{384,448},{4... | collective-permute-start | bytes 1179656 | tf_op jit(solution)/shard_map/ppermute | solution.py:267
  186.0 0.7 convolution_convert_fusion.3.mine_ref
  186.7 0.0 copy-start.12
  186.7 1.7 pack.3
  188.4 9.5 %all-to-all-done.1.rows_ref = bf16[64,40,128]{2,1,0:T(8,128)(2,1)S(1)} async-done(((bf16[64,40,128]{2,1,0:T(8,128)(2,1)}), bf16[64,40,128]{2,1,0:T(8,128)(2,1)S(1)}, u32[]{:S(2)}, u32[]{:S(2)}) %all-to-all-start.1) | async-done | bytes 655392 | tf_op jit(solution)/shard_map/all_to_all | solution.py:270
  197.9 5.3 %all-to-all-start.4 = ((bf16[64,40,128]{2,1,0:T(8,128)(2,1)}), bf16[64,40,128]{2,1,0:T(8,128)(2,1)S(1)}, u32[]{:S(2)}, u32[]{:S(2)}) async-start(bf16[64,40,128]{2,1,0:T(8,128)(2,1)} %pack.3), calls=%async_computation.5 | async-start | bytes 1310720 | tf_op jit(solution)/shard_map/all_to_all | solution.py:270
  203.3 0.0 copy-start.8
  203.3 2.4 %convolution_convert_fusion = bf16[256,1536]{1,0:T(8,128)(2,1)S(1)} fusion(bf16[576,256]{1,0:T(8,128)(2,1)S(1)} %copy-done.12, bf16[576,1536]{1,0:T(8,128)(2,1)} %all-gather.2.cloned.1.call-done), kind=kOutput, calls=%fused_computation | convolution fusion | flops 453378048 | bytes 2850816 | tf_op jit(solution)/shard_map/dot_general | solution.py:29
  205.7 2.2 collective-permute-start.7
  207.9 0.5 fusion.13
  208.4 1.8 fusion.6
  210.2 1.5 merge.2
  211.7 0.5 fusion
  212.2 0.2 convert_element_type.70
  212.4 1.4 fusion.8
  213.8 11.5 %all-to-all-done.4.rows_ref = bf16[64,40,128]{2,1,0:T(8,128)(2,1)S(1)} async-done(((bf16[64,40,128]{2,1,0:T(8,128)(2,1)}), bf16[64,40,128]{2,1,0:T(8,128)(2,1)S(1)}, u32[]{:S(2)}, u32[]{:S(2)}) %all-to-all-start.4) | async-done | bytes 655392 | tf_op jit(solution)/shard_map/all_to_all | solution.py:270
  225.3 1.1 merge.3
  (42 shorter events, 0.1 us)
Async XLA Ops:
  10.0 38.7 %copy-start.13 = (f32[64,128]{1,0:T(8,128)S(1)}, f32[64,128]{1,0:T(8,128)}, u32[]{:S(2)}) copy-start(f32[64,128]{1,0:T(8,128)} %get-tuple-element.18.rank_ref) | copy-start | bytes 98308
  10.0 38.7 %copy-start.14 = (f32[64,128]{1,0:T(8,128)S(1)}, f32[64,128]{1,0:T(8,128)}, u32[]{:S(2)}) copy-start(f32[64,128]{1,0:T(8,128)} %get-tuple-element.19.weight_ref) | copy-start | bytes 98308
  10.0 38.7 %copy-start.15 = (bf16[128,256]{1,0:T(8,128)(2,1)S(1)}, bf16[128,256]{1,0:T(8,128)(2,1)}, u32[]{:S(2)}) copy-start(bf16[128,256]{1,0:T(8,128)(2,1)} %cot_ref.1) | copy-start | bytes 196612
  10.1 38.7 %copy-start.16 = (s32[128]{0:T(128)S(1)}, s32[128]{0:T(128)}, u32[]{:S(2)}) copy-start(s32[128]{0:T(128)} %param.12) | copy-start | bytes 1540
  10.1 35.9 %all-to-all-start = ((bf16[64,40,128]{2,1,0:T(8,128)(2,1)}), bf16[64,40,128]{2,1,0:T(8,128)(2,1)S(1)}, u32[]{:S(2)}, u32[]{:S(2)}) async-start(bf16[64,40,128]{2,1,0:T(8,128)(2,1)} %get-tuple-element.21), calls=%async_computation | async-start | bytes 1310720 | tf_op jit(solution)/shard_map/all_to_all | solution.py:270
  27.6 23.8 %copy-start.2 = (bf16[1,256,768]{2,1,0:T(8,128)(2,1)S(1)}, bf16[1,256,768]{2,1,0:T(8,128)(2,1)}, u32[]{:S(2)}) copy-start(bf16[1,256,768]{2,1,0:T(8,128)(2,1)} %param.15) | copy-start | bytes 1179652
  27.6 23.8 %copy-start.3 = (bf16[1,256,768]{2,1,0:T(8,128)(2,1)S(1)}, bf16[1,256,768]{2,1,0:T(8,128)(2,1)}, u32[]{:S(2)}) copy-start(bf16[1,256,768]{2,1,0:T(8,128)(2,1)} %param.16) | copy-start | bytes 1179652
  27.6 104.1 %reduce-scatter.2.cloned.1.call-start = ((), (), s32[]{:S(2)}) async-start(), calls=%async_computation.6 | async-start | bytes 1990656 | tf_op jit(solution)/shard_map/reduce_scatter | solution.py:332
  29.7 21.6 %collective-permute-start.1 = (bf16[256,1536]{1,0:T(8,128)(2,1)}, bf16[256,1536]{1,0:T(8,128)(2,1)S(1)}, u32[]{:S(2)}, u32[]{:S(2)}) collective-permute-start(bf16[256,1536]{1,0:T(8,128)(2,1)} %pad_maximum_fusion), channel_id=1, source_target_pairs={{0,64},{64,0},{128,192},{192,128},{256,320},{320,256},{384,448},{4... | collective-permute-start | bytes 2359304 | tf_op jit(solution)/shard_map/ppermute | solution.py:267
  46.8 4.5 %collective-permute-start = (bf16[576,256]{1,0:T(8,128)(2,1)S(1)}, bf16[576,256]{1,0:T(8,128)(2,1)S(1)}, u32[]{:S(2)}, u32[]{:S(2)}) collective-permute-start(bf16[576,256]{1,0:T(8,128)(2,1)S(1)} %get-tuple-element.23), channel_id=1, source_target_pairs={{0,64},{64,0},{128,192},{192,128},{256,320},{320,256},{384,448},{4... | collective-permute-start | bytes 884744 | tf_op jit(solution)/shard_map/ppermute | solution.py:267
  51.3 79.6 %copy-start.4 = (bf16[256,1536]{1,0:T(8,128)(2,1)}, bf16[256,1536]{1,0:T(8,128)(2,1)S(1)}, u32[]{:S(2)}) copy-start(bf16[256,1536]{1,0:T(8,128)(2,1)S(1)} %collective-permute-done.1.other_ref) | copy-start | bytes 2359300
  51.3 2.4 %copy-start.11 = (bf16[576,256]{1,0:T(8,128)(2,1)}, bf16[576,256]{1,0:T(8,128)(2,1)S(1)}, u32[]{:S(2)}) copy-start(bf16[576,256]{1,0:T(8,128)(2,1)S(1)} %collective-permute-done.got_ref) | copy-start | bytes 884740
  53.7 5.7 %copy-start.5 = (bf16[1,768,256]{2,1,0:T(8,128)(2,1)S(1)}, bf16[1,768,256]{2,1,0:T(8,128)(2,1)}, u32[]{:S(2)}) copy-start(bf16[1,768,256]{2,1,0:T(8,128)(2,1)} %param.17) | copy-start | bytes 1179652
  53.7 28.4 %all-to-all-start.2 = ((bf16[64,40,128]{2,1,0:T(8,128)(2,1)}), bf16[64,40,128]{2,1,0:T(8,128)(2,1)S(1)}, u32[]{:S(2)}, u32[]{:S(2)}) async-start(bf16[64,40,128]{2,1,0:T(8,128)(2,1)} %grad_rows.1), calls=%async_computation.3 | async-start | bytes 1310720 | tf_op jit(solution)/shard_map/all_to_all | solution.py:270
  59.3 118.5 %all-gather.2.cloned.1.call-start = ((), (), s32[]{:S(2)}) async-start(), calls=%async_computation.7 | async-start | bytes 1990656 | tf_op jit(solution)/shard_map/all_gather | solution.py:357
  59.4 26.9 %collective-permute-start.2 = (bf16[768,256]{1,0:T(8,128)(2,1)S(1)}, bf16[768,256]{1,0:T(8,128)(2,1)S(1)}, u32[]{:S(2)}, u32[]{:S(2)}) collective-permute-start(bf16[768,256]{1,0:T(8,128)(2,1)S(1)} %bitcast.37), channel_id=1, source_target_pairs={{0,64},{64,0},{128,192},{192,128},{256,320},{320,256},{384,448},{4... | collective-permute-start | bytes 1179656 | tf_op jit(solution)/shard_map/ppermute | solution.py:267
  83.6 0.7 copy-start.6
  84.3 3.7 %collective-permute-start.4 = (bf16[576,256]{1,0:T(8,128)(2,1)}, bf16[576,256]{1,0:T(8,128)(2,1)S(1)}, u32[]{:S(2)}, u32[]{:S(2)}) collective-permute-start(bf16[576,256]{1,0:T(8,128)(2,1)} %get-tuple-element.28), channel_id=1, source_target_pairs={{0,64},{64,0},{128,192},{192,128},{256,320},{320,256},{384,448},{4... | collective-permute-start | bytes 884744 | tf_op jit(solution)/shard_map/ppermute | solution.py:267
  88.0 42.9 %copy-start.9 = (bf16[576,256]{1,0:T(8,128)(2,1)}, bf16[576,256]{1,0:T(8,128)(2,1)S(1)}, u32[]{:S(2)}) copy-start(bf16[576,256]{1,0:T(8,128)(2,1)S(1)} %collective-permute-done.4.got_ref) | copy-start | bytes 884740
  88.0 1.1 copy-start.7
  89.7 14.7 %collective-permute-start.5 = (bf16[4,72,768]{2,1,0:T(8,128)(2,1)S(1)}, bf16[4,72,768]{2,1,0:T(8,128)(2,1)S(1)}, u32[]{:S(2)}, u32[]{:S(2)}) collective-permute-start(bf16[4,72,768]{2,1,0:T(8,128)(2,1)S(1)} %get-tuple-element.30), channel_id=1, source_target_pairs={{0,128},{64,960},{128,0},{192,320},{256,384},{320,192},{384,256},{... | collective-permute-start | bytes 1327112 | tf_op jit(solution)/shard_map/ppermute | solution.py:344
  162.3 2.7 %copy-start.19 = (bf16[576,768]{1,0:T(8,128)(2,1)}, bf16[576,768]{1,0:T(8,128)(2,1)S(1)}, u32[]{:S(2)}) copy-start(bf16[576,768]{1,0:T(8,128)(2,1)S(1)} %all_gather.6) | copy-start | bytes 2654212
  162.7 3.5 %collective-permute-start.3 = (bf16[576,256]{1,0:T(8,128)(2,1)S(1)}, bf16[576,256]{1,0:T(8,128)(2,1)S(1)}, u32[]{:S(2)}, u32[]{:S(2)}) collective-permute-start(bf16[576,256]{1,0:T(8,128)(2,1)S(1)} %convolution_convert_fusion.4), channel_id=1, source_target_pairs={{0,64},{64,0},{128,192},{192,128},{256,320},{320,256},{384,448},{4... | collective-permute-start | bytes 884744 | tf_op jit(solution)/shard_map/ppermute | solution.py:267
  167.9 30.1 %all-to-all-start.1 = ((bf16[64,40,128]{2,1,0:T(8,128)(2,1)}), bf16[64,40,128]{2,1,0:T(8,128)(2,1)S(1)}, u32[]{:S(2)}, u32[]{:S(2)}) async-start(bf16[64,40,128]{2,1,0:T(8,128)(2,1)} %pack.2), calls=%async_computation.2 | async-start | bytes 1310720 | tf_op jit(solution)/shard_map/all_to_all | solution.py:270
  175.4 6.9 %copy-start.10 = (bf16[576,256]{1,0:T(8,128)(2,1)S(1)}, bf16[576,256]{1,0:T(8,128)(2,1)}, u32[]{:S(2)}) copy-start(bf16[576,256]{1,0:T(8,128)(2,1)} %copy-done.9) | copy-start | bytes 884740
  176.4 1.5 copy-start
  177.9 4.5 %copy-start.20 = (bf16[576,768]{1,0:T(8,128)(2,1)S(1)}, bf16[576,768]{1,0:T(8,128)(2,1)}, u32[]{:S(2)}) copy-start(bf16[576,768]{1,0:T(8,128)(2,1)} %copy-done.19) | copy-start | bytes 2654212
  180.3 5.8 %copy-start.17 = (bf16[576,1536]{1,0:T(8,128)(2,1)S(1)}, bf16[576,1536]{1,0:T(8,128)(2,1)}, u32[]{:S(2)}) copy-start(bf16[576,1536]{1,0:T(8,128)(2,1)} %all-gather.2.cloned.1.call-done) | copy-start | bytes 5308420
  180.3 6.4 %collective-permute-start.6 = (bf16[576,256]{1,0:T(8,128)(2,1)S(1)}, bf16[576,256]{1,0:T(8,128)(2,1)S(1)}, u32[]{:S(2)}, u32[]{:S(2)}) collective-permute-start(bf16[576,256]{1,0:T(8,128)(2,1)S(1)} %convolution_convert_fusion.2), channel_id=1, source_target_pairs={{0,64},{64,0},{128,192},{192,128},{256,320},{320,256},{384,448},{4... | collective-permute-start | bytes 884744 | tf_op jit(solution)/shard_map/ppermute | solution.py:267
  183.6 24.8 %collective-permute-start.8 = (bf16[768,256]{1,0:T(8,128)(2,1)}, bf16[768,256]{1,0:T(8,128)(2,1)}, u32[]{:S(2)}, u32[]{:S(2)}) collective-permute-start(bf16[768,256]{1,0:T(8,128)(2,1)} %convolution_convert_fusion.1), channel_id=1, source_target_pairs={{0,64},{64,0},{128,192},{192,128},{256,320},{320,256},{384,448},{4... | collective-permute-start | bytes 1179656 | tf_op jit(solution)/shard_map/ppermute | solution.py:267
  186.7 16.6 %copy-start.12 = (bf16[576,256]{1,0:T(8,128)(2,1)S(1)}, bf16[576,256]{1,0:T(8,128)(2,1)}, u32[]{:S(2)}) copy-start(bf16[576,256]{1,0:T(8,128)(2,1)} %copy-done.11) | copy-start | bytes 884740
  197.9 27.4 %all-to-all-start.4 = ((bf16[64,40,128]{2,1,0:T(8,128)(2,1)}), bf16[64,40,128]{2,1,0:T(8,128)(2,1)S(1)}, u32[]{:S(2)}, u32[]{:S(2)}) async-start(bf16[64,40,128]{2,1,0:T(8,128)(2,1)} %pack.3), calls=%async_computation.5 | async-start | bytes 1310720 | tf_op jit(solution)/shard_map/all_to_all | solution.py:270
  203.3 4.6 %copy-start.8 = (bf16[576,256]{1,0:T(8,128)(2,1)S(1)}, bf16[576,256]{1,0:T(8,128)(2,1)}, u32[]{:S(2)}) copy-start(bf16[576,256]{1,0:T(8,128)(2,1)} %copy-done.6) | copy-start | bytes 884740
  203.3 4.6 %copy-start.21 = (bf16[576,768]{1,0:T(8,128)(2,1)S(1)}, bf16[576,768]{1,0:T(8,128)(2,1)}, u32[]{:S(2)}) copy-start(bf16[576,768]{1,0:T(8,128)(2,1)} %copy-done.19) | copy-start | bytes 2654212
  205.6 4.6 %copy-start.1 = (bf16[512,2560]{1,0:T(8,128)(2,1)S(1)}, bf16[512,2560]{1,0:T(8,128)(2,1)}, u32[]{:S(2)}) copy-start(bf16[512,2560]{1,0:T(8,128)(2,1)} %copy-done) | copy-start | bytes 7864324
  205.7 6.6 %collective-permute-start.7 = (bf16[256,1536]{1,0:T(8,128)(2,1)S(1)}, bf16[256,1536]{1,0:T(8,128)(2,1)S(1)}, u32[]{:S(2)}, u32[]{:S(2)}) collective-permute-start(bf16[256,1536]{1,0:T(8,128)(2,1)S(1)} %convolution_convert_fusion), channel_id=1, source_target_pairs={{0,64},{64,0},{128,192},{192,128},{256,320},{320,256},{384,448},{4... | collective-permute-start | bytes 2359304 | tf_op jit(solution)/shard_map/ppermute | solution.py:267
  210.2 1.5 copy-start.18
Sparse Core Ops, SparseCore 0:
  53.8 51.5 reduce-scatter.1
  134.5 39.7 all-gather.1

commit v4 on v2

--- a/solution.py
+++ b/solution.py
@@ -57,19 +57,36 @@
     return left, right
 
 
-def token_kernel(
-    pad,
+def places(group, capacity, transposed):
+    size = 4 * group * capacity
+    chunked = number((1, size) if transposed else (size, 1), 1 if transposed else 0)
+    expert = jnp.floor((chunked + 0.5) * (1.0 / (4 * capacity)))
+    within = chunked - 4 * capacity * expert
+    piece = jnp.floor((within + 0.5) * (1.0 / capacity))
+    stacked = within - capacity * piece + capacity * (expert + group * piece)
+    return low_if(number((size, size), 0 if transposed else 1) == stacked)
+
+
+GROUP = 8
+
+
+def dispatch_kernel(
+    capacity,
     routes_hbm,
     combine_hbm,
+    clip_hbm,
     limits_hbm,
     tokens_hbm,
-    tok_out,
+    cot_hbm,
+    chunks_out,
     rank_out,
     weight_out,
     routes_ref,
     combine_ref,
+    clip_ref,
     limits_ref,
     tokens_ref,
+    cot_ref,
     sems,
 ):
     copies = [
@@ -78,8 +95,10 @@
             (
                 (routes_hbm, routes_ref),
                 (combine_hbm, combine_ref),
+                (clip_hbm, clip_ref),
                 (limits_hbm, limits_ref),
                 (tokens_hbm, tokens_ref),
+                (cot_hbm, cot_ref),
             )
         )
     ]
@@ -87,10 +106,9 @@
         copy.start()
     top_count, tok_rows = routes_ref.shape
     experts = limits_ref.shape[1]
-    chunk = 2 * pad
-    slots = experts * chunk
-    owner = owners((slots, experts), 0, chunk)
-    left, right = wanted((slots, tok_rows), 0, pad)
+    slots = experts * capacity
+    owner = owners((slots, experts), 0, capacity)
+    place = remainder(number((slots, 1), 0), capacity)
     before = number((tok_rows, tok_rows), 0) < number((tok_rows, tok_rows), 1)
     square = (experts, experts)
     for copy in copies:
@@ -109,35 +127,33 @@
     rank = jnp.where(kept, rank, -1.0)
     rank_out[...] = rank
     weight_out[...] = weight
-    spread = mul(owner, rank.astype(LOW))
-    tokens = tokens_ref[...]
-    lanes = tokens.shape[1] // 2
-    picked = jnp.concatenate([low_if(spread == left), low_if(spread == right)], axis=1)
-    sides = jnp.concatenate([tokens[:, :lanes], tokens[:, lanes:]], axis=0)
-    tok_out[...] = mul(picked, sides).reshape(experts, chunk, lanes).astype(LOW)
-
-
-def grad_kernel(pad, rank_ref, weight_ref, clip_ref, cot_ref, cot_out):
-    experts, tok_rows = rank_ref.shape
-    chunk = 2 * pad
-    slots = experts * chunk
-    owner = owners((slots, experts), 0, chunk)
-    left, right = wanted((slots, tok_rows), 0, pad)
-    spread = mul(owner, rank_ref[...].astype(LOW))
-    high, rest = split_low(weight_ref[...] * clip_ref[...].astype(WIDE))
-    high, rest = mul(owner, high), mul(owner, rest)
+    picked = mul(owner, rank.astype(LOW)) == place
+    tok_rows_all = mul(low_if(picked), tokens_ref[...]).astype(LOW)
     coefs = jnp.concatenate(
         [
-            jnp.where(spread == place, part, 0.0).astype(LOW)
-            for part in (high, rest)
-            for place in (left, right)
+            jnp.where(picked, mul(owner, part), 0.0).astype(LOW)
+            for part in split_low(weight * clip_ref[...].astype(WIDE))
         ],
         axis=1,
     )
     cot = cot_ref[...]
+    cot_rows_all = mul(coefs, jnp.concatenate([cot, cot], axis=0)).astype(LOW)
     lanes = cot.shape[1] // 2
-    sides = jnp.concatenate([cot[:, :lanes], cot[:, lanes:]] * 2, axis=0)
-    cot_out[...] = mul(coefs, sides).reshape(experts, chunk, lanes).astype(LOW)
+    moves = places(GROUP, capacity, False)
+    rows = GROUP * capacity
+    for at in range(experts // GROUP):
+        block = slice(at * rows, (at + 1) * rows)
+        stacked = jnp.concatenate(
+            [
+                part[block, side * lanes : (side + 1) * lanes]
+                for part in (tok_rows_all, cot_rows_all)
+                for side in range(2)
+            ],
+            axis=0,
+        )
+        chunks_out[at * GROUP : (at + 1) * GROUP] = (
+            mul(moves, stacked).reshape(GROUP, 4 * capacity, lanes).astype(LOW)
+        )
 
 
 def table_kernel(pad, rank_ref, weight_ref, pick_out, weight_out):
@@ -176,22 +192,24 @@
     )
 
 
-GROUP = 8
-
-
-def unpack_kernel(capacity, pad, core_ref, chunks_ref, keep_out, give_out):
+def unpack_kernel(capacity, core_ref, chunks_ref, tok_out, cot_out, give_out):
     lanes = chunks_ref.shape[2]
     half = chunks_ref.shape[0] // 2
-    rows, slots = GROUP * capacity, GROUP * 2 * pad
-    moves = [shifts((rows, slots), 0, capacity, pad, side) for side in range(2)]
+    rows = GROUP * capacity
+    moves = places(GROUP, capacity, True)
     core = core_ref[0]
-    for out_ref, base in ((keep_out, core * half), (give_out, (1 - core) * half)):
+    for (first_out, first), (second_out, second), base in (
+        ((tok_out, 0), (cot_out, 0), core * half),
+        ((give_out, 0), (give_out, half * capacity), (1 - core) * half),
+    ):
         for at in range(half // GROUP):
-            chunk = chunks_ref[pl.ds(base + at * GROUP, GROUP)].reshape(slots, lanes)
-            for side in range(2):
-                out_ref[at * rows : (at + 1) * rows, side * lanes : (side + 1) * lanes] = mul(
-                    moves[side], chunk
-                ).astype(LOW)
+            chunk = chunks_ref[pl.ds(base + at * GROUP, GROUP)].reshape(4 * rows, lanes)
+            pieces = mul(moves, chunk).astype(LOW)
+            for piece in range(4):
+                out_ref, start = ((first_out, first), (second_out, second))[piece // 2]
+                start = start + at * rows
+                cols = slice(piece % 2 * lanes, (piece % 2 + 1) * lanes)
+                out_ref[start : start + rows, cols] = pieces[piece * rows : (piece + 1) * rows]
 
 
 def pack_kernel(capacity, pad, core_ref, mine_ref, got_ref, chunks_out):
@@ -210,11 +228,31 @@
 
 
 def gate_up_kernel(keep_ref, got_ref, gate_ref, up_ref, other_ref, out_ref):
-    ff = gate_ref.shape[1]
-    keep, got = keep_ref[...], got_ref[...]
+    half, ff = keep_ref.shape[0], gate_ref.shape[1]
+    keep, got = keep_ref[...], got_ref[0:half, :]
     for at, own_ref in enumerate((gate_ref, up_ref)):
         cols = slice(at * ff, (at + 1) * ff)
         out_ref[:, cols] = (mul(keep, own_ref[...]) + mul(got, other_ref[:, cols])).astype(LOW)
+
+
+def hidden_grad_kernel(keep_ref, got_ref, own_ref, other_ref, out_ref):
+    half = keep_ref.shape[0]
+    out_ref[...] = (
+        against(keep_ref[...], own_ref[...]) + against(got_ref[half:, :], other_ref[...])
+    ).astype(LOW)
+
+
+def activate_kernel(shares_ref, parts_ref, hidden_out, derived_out):
+    ff = hidden_out.shape[1]
+    gate_val = shares_ref[:, :ff].astype(WIDE)
+    up_val = shares_ref[:, ff:].astype(WIDE)
+    grad_hidden = parts_ref[0].astype(WIDE)
+    for at in range(1, parts_ref.shape[0]):
+        grad_hidden = grad_hidden + parts_ref[at].astype(WIDE)
+    active, slope = swish_parts(gate_val)
+    hidden_out[...] = (active * up_val).astype(LOW)
+    derived_out[:, :ff] = (grad_hidden * up_val * slope).astype(LOW)
+    derived_out[:, ff:] = (grad_hidden * active).astype(LOW)
 
 
 def body(
@@ -249,16 +287,6 @@
     def exchange(chunks):
         return lax.all_to_all(chunks, "expert", split_axis=0, concat_axis=0, tiled=True)
 
-    def unpack(chunks):
-        keep, give = pl.pallas_call(
-            functools.partial(unpack_kernel, capacity, pad),
-            out_shape=(half_shape, half_shape),
-            in_specs=[in_smem, in_vmem],
-            compiler_params=params,
-            name="unpack",
-        )(core, chunks)
-        return keep, swap(give)
-
     def pack(mine, got):
         return pl.pallas_call(
             functools.partial(pack_kernel, capacity, pad),
@@ -281,54 +309,75 @@
     gu_other = swap(gu_own)
     down_other = swap(down_own)
 
-    token_send, rank, weight = pl.pallas_call(
-        functools.partial(token_kernel, pad),
-        out_shape=(chunk_shape, rank_shape, rank_shape),
-        in_specs=[anywhere] * 4,
+    sent, rank, weight = pl.pallas_call(
+        functools.partial(dispatch_kernel, capacity),
+        out_shape=(
+            jax.ShapeDtypeStruct((experts, 4 * capacity, lanes), LOW),
+            rank_shape,
+            rank_shape,
+        ),
+        in_specs=[anywhere] * 6,
         scratch_shapes=[
             pltpu.VMEM((top_count, tok_rows), jnp.int32),
             pltpu.VMEM((top_count, tok_rows), WIDE),
+            pltpu.VMEM((1, tok_rows), jnp.int32),
             pltpu.VMEM((1, experts), jnp.int32),
             pltpu.VMEM((tok_rows, width), LOW),
-            pltpu.SemaphoreType.DMA((4,)),
+            pltpu.VMEM((tok_rows, width), LOW),
+            pltpu.SemaphoreType.DMA((6,)),
         ],
+        compiler_params=pltpu.CompilerParams(vmem_limit_bytes=63 * 1024 * 1024),
+        name="dispatch",
+    )(
+        routes.T,
+        combine.T,
+        clip_mask.reshape(1, tok_rows),
+        limits.reshape(1, experts),
+        tokens,
+        cotangent,
+    )
+    token_keep, grad_keep, give = pl.pallas_call(
+        functools.partial(unpack_kernel, capacity),
+        out_shape=(half_shape, half_shape, jax.ShapeDtypeStruct((2 * half, width), LOW)),
+        in_specs=[in_smem, in_vmem],
         compiler_params=params,
-        name="token_rows",
-    )(routes.T, combine.T, limits.reshape(1, experts), tokens)
-    token_keep, token_got = unpack(exchange(token_send))
+        name="unpack",
+    )(core, exchange(sent))
+    got = swap(give)
+    token_got, grad_got = got[:half], got[half:]
     gate_up = pl.pallas_call(
         gate_up_kernel,
         out_shape=jax.ShapeDtypeStruct((half, 2 * ff), LOW),
         compiler_params=params,
         name="gate_up",
-    )(token_keep, token_got, gate_own, up_own, gu_other)
+    )(token_keep, got, gate_own, up_own, gu_other)
+    gate_up, grad_ready = lax.optimization_barrier((gate_up, grad_keep))
     shares = lax.psum_scatter(
         gate_up, "dp", scatter_dimension=0, tiled=True, axis_index_groups=column
-    ).astype(WIDE)
-    grad_send = pl.pallas_call(
-        functools.partial(grad_kernel, pad),
-        out_shape=chunk_shape,
+    )
+    grad_part = pl.pallas_call(
+        hidden_grad_kernel,
+        out_shape=jax.ShapeDtypeStruct((half, ff), LOW),
         compiler_params=params,
-        name="grad_rows",
-    )(rank, weight, clip_mask.reshape(1, tok_rows), cotangent)
-    grad_keep, grad_got = unpack(exchange(grad_send))
-    grad_part = (
-        (against(grad_keep, down_own) + against(grad_got, down_other))
-        .astype(LOW)
-        .reshape(chips, half // chips, ff)
-    )
-    grad_hidden = jnp.sum(
-        lax.all_to_all(
-            grad_part, "dp", split_axis=0, concat_axis=0, tiled=True, axis_index_groups=column
-        ).astype(WIDE),
-        axis=0,
-    )
-    gate_val, up_val = shares[:, :ff], shares[:, ff:]
-    active, slope = swish_parts(gate_val)
-    hidden = (active * up_val).astype(LOW)
-    derived = jnp.concatenate(
-        [(grad_hidden * up_val * slope).astype(LOW), (grad_hidden * active).astype(LOW)], axis=1
-    )
+        name="hidden_grad",
+    )(grad_ready, got, down_own, down_other)
+    grad_parts = lax.all_to_all(
+        grad_part.reshape(chips, half // chips, ff),
+        "dp",
+        split_axis=0,
+        concat_axis=0,
+        tiled=True,
+        axis_index_groups=column,
+    )
+    hidden, derived = pl.pallas_call(
+        activate_kernel,
+        out_shape=(
+            jax.ShapeDtypeStruct((half // chips, ff), LOW),
+            jax.ShapeDtypeStruct((half // chips, 2 * ff), LOW),
+        ),
+        compiler_params=params,
+        name="activate",
+    )(shares, grad_parts)
     derived_full = lax.all_gather(derived, "dp", axis=0, tiled=True, axis_index_groups=column)
     hidden_full = lax.all_gather(hidden, "dp", axis=0, tiled=True, axis_index_groups=column)
     out_got = swap(mul(hidden_full, down_other).astype(LOW))

time: 244 us -> 237 us (0.971)
  starting transfers between devices: 57.8 us -> 44.5 us
  blocking collectives: 74.3 us -> 79.5 us
  waiting for transfers between devices: 55.2 us -> 59.3 us
  other arithmetic: 6.02 us -> 2.95 us
    all_to_all x4 -> x3, starting transfers between devices: 41.4 us -> 29.8 us  [exchange(): lax.all_to_all(chunks, 'expert', split_axis=0, concat_axis=0, tiled=True)]
    reduce_scatter x1, waiting for transfers between devices: 0.07 us -> 8.38 us  [body(): lax.psum_scatter(gate_up, 'dp', scatter_dimension=0, tiled=True, axis_ind...]
    all_to_all x4 -> x3, waiting for transfers between devices: 52.6 us -> 46.2 us  [exchange(): lax.all_to_all(chunks, 'expert', split_axis=0, concat_axis=0, tiled=True)]
    all_to_all x1, blocking collectives: 47 us -> 51.5 us  [body(): lax.all_to_all(grad_part.reshape(chips, half // chips, ff), 'dp', split_a...]
    dot_general x4 -> x2, matrix products: 5.01 us -> 3.04 us  [against(): lax.dot_general(left, right, (((1,), (1,)), ((), ())), preferred_element_...]
    ppermute x8 -> x7, starting transfers between devices: 16.3 us -> 14.6 us  [swap(): return lax.ppermute(values, 'dp', swap_pairs)]
    unnamed x40 -> x38, local copies, waits for them, and re-layouts: 5.31 us -> 5.91 us
  transfers between devices with their start and end apart: 14 -> 12, of which waited for: 8 -> 7; matrix products, arithmetic and copies ran while one was open for 7% -> 6% of each run, Pallas kernels for 5% -> 3%
where the time goes in v4:
time: 237 us; the launch traced here: 236 us
  blocking collectives  79.5 us (34%)
  waiting for transfers between devices  59.3 us (25%)
  starting transfers between devices  44.5 us (19%)
  Pallas kernels  18.4 us (8%)
  between operations  14.4 us (6%)
  matrix products  11.1 us (5%)
  local copies, waits for them, and re-layouts  5.91 us (2%)
  other arithmetic  2.95 us (1%)
    all_to_all x1, blocking collectives, body(): lax.all_to_all(grad_part.reshape(chips, half // chips, ff), 'dp', split_a...  51.5 us
    all_to_all x3, waiting for transfers between devices, exchange(): lax.all_to_all(chunks, 'expert', split_axis=0, concat_axis=0, tiled=True)  46.2 us
    all_to_all x3, starting transfers between devices, exchange(): lax.all_to_all(chunks, 'expert', split_axis=0, concat_axis=0, tiled=True)  29.8 us
    all_gather x1, blocking collectives, body(): lax.all_gather(hidden, 'dp', axis=0, tiled=True, axis_index_groups=column)  28 us
    ppermute x7, starting transfers between devices, swap(): return lax.ppermute(values, 'dp', swap_pairs)  14.6 us
    reduce_scatter x1, waiting for transfers between devices, body(): lax.psum_scatter(gate_up, 'dp', scatter_dimension=0, tiled=True, axis_ind...  8.38 us
    dot_general x5, matrix products, outer(): lax.dot_general(left, right, (((0,), (0,)), ((), ())), preferred_element_...  6.04 us
    unnamed x38, local copies, waits for them, and re-layouts  5.91 us
  transfers between devices with their start and end apart: 12, of which 7 were waited for; matrix products, arithmetic and copies ran while one was open for 6% of the time, Pallas kernels for 3%

profile of v4, /device:TPU:4, one launch (start us, length us, event | category | flops | bytes accessed | tf_op | source)
XLA Modules:
  0.0 236.1 jit_solution(12612528574834344463)
XLA Ops:
  7.2 0.0 copy-start.3
  7.2 0.0 copy-start.2
  7.2 4.8 %dispatch.1 = (bf16[64,72,128]{2,1,0:T(8,128)(2,1)}, f32[64,128]{1,0:T(8,128)}, f32[64,128]{1,0:T(8,128)}) custom-call(s32[8,128]{1,0:T(8,128)} %bitcast.38, f32[8,128]{1,0:T(8,128)} %bitcast.39, s32[1,128]{1,0:T(1,128)} %bitcast.40, s32[1,64]{1,0:T(1,128)} %bitcast.41, bf16[128,256]{1,0:T(8,128)(2,1)} %tokens_hbm.1, bf16[128,256]{1,0:T(8,128)(2,1)} %cot_hbm.1), custom_call_target="tpu_custom_call" | custom-call | tf_op jit(solution)/shard_map/dispatch/pallas_call | solution.py:312
  12.0 17.4 %all-to-all-start = ((bf16[64,72,128]{2,1,0:T(8,128)(2,1)}), bf16[64,72,128]{2,1,0:T(8,128)(2,1)S(1)}, u32[]{:S(2)}, u32[]{:S(2)}) async-start(bf16[64,72,128]{2,1,0:T(8,128)(2,1)} %get-tuple-element.20), calls=%async_computation | async-start | bytes 2359296 | tf_op jit(solution)/shard_map/all_to_all | solution.py:288
  29.4 0.0 reduce-scatter.2.cloned.1.call-start
  29.5 0.0 copy-done.3
  29.5 0.0 copy-done.2
  29.5 0.9 pad_maximum_fusion
  30.4 1.9 collective-permute-start.1
  32.4 26.4 %all-to-all-done.chunks_ref = bf16[64,72,128]{2,1,0:T(8,128)(2,1)S(1)} async-done(((bf16[64,72,128]{2,1,0:T(8,128)(2,1)}), bf16[64,72,128]{2,1,0:T(8,128)(2,1)S(1)}, u32[]{:S(2)}, u32[]{:S(2)}) %all-to-all-start) | async-done | bytes 1179680 | tf_op jit(solution)/shard_map/all_to_all | solution.py:288
  58.7 1.7 unpack.1
  60.4 0.0 copy-start.8
  60.4 0.7 copy-done.8
  61.1 1.9 collective-permute-start
  63.0 0.0 collective-permute-done.1.other_ref
  63.1 2.0 collective-permute-done.got_ref
  65.0 3.4 %gate_up.1 = bf16[576,1536]{1,0:T(8,128)(2,1)} custom-call(bf16[576,256]{1,0:T(8,128)(2,1)S(1)} %get-tuple-element.21.keep_ref, bf16[1152,256]{1,0:T(8,128)(2,1)S(1)} %collective-permute-done.got_ref, bf16[256,768]{1,0:T(8,128)(2,1)S(1)} %bitcast.31, bf16[256,768]{1,0:T(8,128)(2,1)S(1)} %bitcast.34, bf16[256,1536]{1,0:T(8,128)(2,1)} %collective-permute-done.1.other_ref), custom_call_target="tpu_custom_call" | custom-call | tf_op jit(solution)/shard_map/gate_up/pallas_call | solution.py:348
  68.5 0.0 reduce-scatter.2.cloned.1.call-update
  68.5 0.0 all-gather.2.cloned.1.call-start
  68.5 0.9 copy-done.6
  69.5 2.0 collective-permute-start.2
  71.5 1.6 collective-permute-done.2.other_ref
  73.1 0.7 hidden_grad.1
  73.7 0.1 copy-done.7
  73.8 51.5 %all_to_all.20.parts_ref = bf16[8,72,768]{2,1,0:T(8,128)(2,1)S(1)} all-to-all(bf16[8,72,768]{2,1,0:T(8,128)(2,1)S(1)} %bitcast.29), channel_id=1, replica_groups={{0,128,256,384,512,640,768,896},{64,192,320,448,576,704,832,960},{1,129..., dimensions={0} | all-to-all | bytes 1769472 | tf_op jit(solution)/shard_map/all_to_all | solution.py:364
  125.3 8.4 %reduce-scatter.2.cloned.1.call-done.shares_ref = bf16[72,1536]{1,0:T(8,128)(2,1)} async-done(((bf16[576,1536]{1,0:T(8,128)(2,1)}), bf16[72,1536]{1,0:T(8,128)(2,1)}) %reduce-scatter.2.cloned.1.call-update) | async-done | bytes 221200 | tf_op jit(solution)/shard_map/reduce_scatter | solution.py:355
  133.7 0.9 copy-done.10
  134.6 0.9 activate.1
  135.5 0.6 copy-done.11
  136.2 0.0 all-gather.2.cloned.1.call-update
  136.2 28.0 %all_gather.6 = bf16[576,768]{1,0:T(8,128)(2,1)S(1)} all-gather(bf16[72,768]{1,0:T(8,128)(2,1)} %copy-done.11), channel_id=1, replica_groups={{0,128,256,384,512,640,768,896},{64,192,320,448,576,704,832,960},{1,129..., dimensions={0}, use_global_device_ids=true | all-gather | bytes 995328 | tf_op jit(solution)/shard_map/all_gather | solution.py:382
  164.2 1.7 convolution_convert_fusion.4
  165.9 0.0 copy-start.12
  165.9 0.0 copy-start.13
  165.9 1.9 collective-permute-start.3
  167.8 0.4 convolution_convert_fusion.5.mine_ref
  168.2 1.1 collective-permute-done.3.got_ref
  169.4 1.7 pack.2
  171.1 7.1 %all-to-all-start.2 = ((bf16[64,40,128]{2,1,0:T(8,128)(2,1)}), bf16[64,40,128]{2,1,0:T(8,128)(2,1)S(1)}, u32[]{:S(2)}, u32[]{:S(2)}) async-start(bf16[64,40,128]{2,1,0:T(8,128)(2,1)} %pack.2), calls=%async_computation.3 | async-start | bytes 1310720 | tf_op jit(solution)/shard_map/all_to_all | solution.py:288
  178.3 0.9 tables.1
  179.2 1.5 copy-done
  180.7 1.1 copy-done.4
  181.8 2.4 %convolution_convert_fusion.2 = bf16[576,256]{1,0:T(8,128)(2,1)S(1)} fusion(bf16[576,1536]{1,0:T(8,128)(2,1)} %all-gather.2.cloned.1.call-done, bf16[256,1536]{1,0:T(8,128)(2,1)} %collective-permute-done.1.other_ref), kind=kOutput, calls=%fused_computation.2 | convolution fusion | flops 453132288 | bytes 2850816 | tf_op jit(solution)/shard_map/dot_general | solution.py:33
  184.2 2.2 collective-permute-start.4
  186.4 0.0 copy-done.17
  186.4 1.3 convolution_convert_fusion.1
  187.7 2.4 %collective-permute-start.6 = (bf16[768,256]{1,0:T(8,128)(2,1)}, bf16[768,256]{1,0:T(8,128)(2,1)}, u32[]{:S(2)}, u32[]{:S(2)}) collective-permute-start(bf16[768,256]{1,0:T(8,128)(2,1)} %convolution_convert_fusion.1), channel_id=1, source_target_pairs={{0,64},{64,0},{128,192},{192,128},{256,320},{320,256},{384,448},{4... | collective-permute-start | bytes 1179656 | tf_op jit(solution)/shard_map/ppermute | solution.py:285
  190.1 0.7 convolution_convert_fusion.3.mine_ref
  190.8 0.0 collective-permute-done.4.got_ref
  190.8 1.7 pack.3
  192.4 8.3 %all-to-all-done.2.rows_ref = bf16[64,40,128]{2,1,0:T(8,128)(2,1)S(1)} async-done(((bf16[64,40,128]{2,1,0:T(8,128)(2,1)}), bf16[64,40,128]{2,1,0:T(8,128)(2,1)S(1)}, u32[]{:S(2)}, u32[]{:S(2)}) %all-to-all-start.2) | async-done | bytes 655392 | tf_op jit(solution)/shard_map/all_to_all | solution.py:288
  200.7 5.3 %all-to-all-start.3 = ((bf16[64,40,128]{2,1,0:T(8,128)(2,1)}), bf16[64,40,128]{2,1,0:T(8,128)(2,1)S(1)}, u32[]{:S(2)}, u32[]{:S(2)}) async-start(bf16[64,40,128]{2,1,0:T(8,128)(2,1)} %pack.3), calls=%async_computation.4 | async-start | bytes 1310720 | tf_op jit(solution)/shard_map/all_to_all | solution.py:288
  206.1 2.3 convolution_convert_fusion
  208.4 2.2 collective-permute-start.5
  210.6 0.5 fusion.14
  211.2 0.0 collective-permute-done.6
  211.2 1.8 fusion.6
  213.0 1.5 merge.2
  214.5 0.5 fusion
  215.0 0.0 collective-permute-done.5
  215.0 0.2 convert_element_type.38
  215.2 1.4 fusion.8
  216.6 11.6 %all-to-all-done.3.rows_ref = bf16[64,40,128]{2,1,0:T(8,128)(2,1)S(1)} async-done(((bf16[64,40,128]{2,1,0:T(8,128)(2,1)}), bf16[64,40,128]{2,1,0:T(8,128)(2,1)S(1)}, u32[]{:S(2)}, u32[]{:S(2)}) %all-to-all-start.3) | async-done | bytes 655392 | tf_op jit(solution)/shard_map/all_to_all | solution.py:288
  228.2 1.1 merge.3
  (24 shorter events, 0.0 us)
Async XLA Ops:
  7.2 22.3 %copy-start.3 = (bf16[1,256,768]{2,1,0:T(8,128)(2,1)S(1)}, bf16[1,256,768]{2,1,0:T(8,128)(2,1)}, u32[]{:S(2)}) copy-start(bf16[1,256,768]{2,1,0:T(8,128)(2,1)} %param.16) | copy-start | bytes 1179652
  7.2 22.3 %copy-start.2 = (bf16[1,256,768]{2,1,0:T(8,128)(2,1)S(1)}, bf16[1,256,768]{2,1,0:T(8,128)(2,1)}, u32[]{:S(2)}) copy-start(bf16[1,256,768]{2,1,0:T(8,128)(2,1)} %param.15) | copy-start | bytes 1179652
  12.0 46.7 %all-to-all-start = ((bf16[64,72,128]{2,1,0:T(8,128)(2,1)}), bf16[64,72,128]{2,1,0:T(8,128)(2,1)S(1)}, u32[]{:S(2)}, u32[]{:S(2)}) async-start(bf16[64,72,128]{2,1,0:T(8,128)(2,1)} %get-tuple-element.20), calls=%async_computation | async-start | bytes 2359296 | tf_op jit(solution)/shard_map/all_to_all | solution.py:288
  29.4 104.3 %reduce-scatter.2.cloned.1.call-start = ((), (), s32[]{:S(2)}) async-start(), calls=%async_computation.5 | async-start | bytes 1990656 | tf_op jit(solution)/shard_map/reduce_scatter | solution.py:355
  30.4 32.6 %collective-permute-start.1 = (bf16[256,1536]{1,0:T(8,128)(2,1)}, bf16[256,1536]{1,0:T(8,128)(2,1)}, u32[]{:S(2)}, u32[]{:S(2)}) collective-permute-start(bf16[256,1536]{1,0:T(8,128)(2,1)} %pad_maximum_fusion), channel_id=1, source_target_pairs={{0,64},{64,0},{128,192},{192,128},{256,320},{320,256},{384,448},{4... | collective-permute-start | bytes 2359304 | tf_op jit(solution)/shard_map/ppermute | solution.py:285
  60.4 0.7 copy-start.8
  61.1 3.9 %collective-permute-start = (bf16[1152,256]{1,0:T(8,128)(2,1)S(1)}, bf16[1152,256]{1,0:T(8,128)(2,1)S(1)}, u32[]{:S(2)}, u32[]{:S(2)}) collective-permute-start(bf16[1152,256]{1,0:T(8,128)(2,1)S(1)} %get-tuple-element.22), channel_id=1, source_target_pairs={{0,64},{64,0},{128,192},{192,128},{256,320},{320,256},{384,448},{4... | collective-permute-start | bytes 1769480 | tf_op jit(solution)/shard_map/ppermute | solution.py:285
  68.5 1.0 copy-start.6
  68.5 4.6 %copy-start.9 = (bf16[576,256]{1,0:T(8,128)(2,1)S(1)}, bf16[576,256]{1,0:T(8,128)(2,1)}, u32[]{:S(2)}) copy-start(bf16[576,256]{1,0:T(8,128)(2,1)} %copy-done.8) | copy-start | bytes 884740
  68.5 113.3 %all-gather.2.cloned.1.call-start = ((), (), s32[]{:S(2)}) async-start(), calls=%async_computation.6 | async-start | bytes 1990656 | tf_op jit(solution)/shard_map/all_gather | solution.py:381
  69.5 3.6 %collective-permute-start.2 = (bf16[768,256]{1,0:T(8,128)(2,1)S(1)}, bf16[768,256]{1,0:T(8,128)(2,1)S(1)}, u32[]{:S(2)}, u32[]{:S(2)}) collective-permute-start(bf16[768,256]{1,0:T(8,128)(2,1)S(1)} %bitcast.36), channel_id=1, source_target_pairs={{0,64},{64,0},{128,192},{192,128},{256,320},{320,256},{384,448},{4... | collective-permute-start | bytes 1179656 | tf_op jit(solution)/shard_map/ppermute | solution.py:285
  73.1 0.7 copy-start.7
  133.7 0.9 copy-start.10
  135.5 0.6 copy-start.11
  164.2 4.0 %copy-start.16 = (bf16[576,768]{1,0:T(8,128)(2,1)}, bf16[576,768]{1,0:T(8,128)(2,1)S(1)}, u32[]{:S(2)}) copy-start(bf16[576,768]{1,0:T(8,128)(2,1)S(1)} %all_gather.6) | copy-start | bytes 2654212
  165.9 12.4 %copy-start.12 = (f32[64,128]{1,0:T(8,128)S(1)}, f32[64,128]{1,0:T(8,128)}, u32[]{:S(2)}) copy-start(f32[64,128]{1,0:T(8,128)} %get-tuple-element.17.rank_ref) | copy-start | bytes 98308
  165.9 12.4 %copy-start.13 = (f32[64,128]{1,0:T(8,128)S(1)}, f32[64,128]{1,0:T(8,128)}, u32[]{:S(2)}) copy-start(f32[64,128]{1,0:T(8,128)} %get-tuple-element.18.weight_ref) | copy-start | bytes 98308
  165.9 3.5 %collective-permute-start.3 = (bf16[576,256]{1,0:T(8,128)(2,1)S(1)}, bf16[576,256]{1,0:T(8,128)(2,1)S(1)}, u32[]{:S(2)}, u32[]{:S(2)}) collective-permute-start(bf16[576,256]{1,0:T(8,128)(2,1)S(1)} %convolution_convert_fusion.4), channel_id=1, source_target_pairs={{0,64},{64,0},{128,192},{192,128},{256,320},{320,256},{384,448},{4... | collective-permute-start | bytes 884744 | tf_op jit(solution)/shard_map/ppermute | solution.py:285
  171.1 29.6 %all-to-all-start.2 = ((bf16[64,40,128]{2,1,0:T(8,128)(2,1)}), bf16[64,40,128]{2,1,0:T(8,128)(2,1)S(1)}, u32[]{:S(2)}, u32[]{:S(2)}) async-start(bf16[64,40,128]{2,1,0:T(8,128)(2,1)} %pack.2), calls=%async_computation.3 | async-start | bytes 1310720 | tf_op jit(solution)/shard_map/all_to_all | solution.py:288
  179.2 1.5 copy-start
  180.7 1.1 copy-start.4
  181.8 4.7 %copy-start.17 = (bf16[576,768]{1,0:T(8,128)(2,1)S(1)}, bf16[576,768]{1,0:T(8,128)(2,1)}, u32[]{:S(2)}) copy-start(bf16[576,768]{1,0:T(8,128)(2,1)} %copy-done.16) | copy-start | bytes 2654212
  184.2 5.9 %copy-start.14 = (bf16[576,1536]{1,0:T(8,128)(2,1)S(1)}, bf16[576,1536]{1,0:T(8,128)(2,1)}, u32[]{:S(2)}) copy-start(bf16[576,1536]{1,0:T(8,128)(2,1)} %all-gather.2.cloned.1.call-done) | copy-start | bytes 5308420
  184.2 6.6 %collective-permute-start.4 = (bf16[576,256]{1,0:T(8,128)(2,1)S(1)}, bf16[576,256]{1,0:T(8,128)(2,1)S(1)}, u32[]{:S(2)}, u32[]{:S(2)}) collective-permute-start(bf16[576,256]{1,0:T(8,128)(2,1)S(1)} %convolution_convert_fusion.2), channel_id=1, source_target_pairs={{0,64},{64,0},{128,192},{192,128},{256,320},{320,256},{384,448},{4... | collective-permute-start | bytes 884744 | tf_op jit(solution)/shard_map/ppermute | solution.py:285
  187.7 23.5 %collective-permute-start.6 = (bf16[768,256]{1,0:T(8,128)(2,1)}, bf16[768,256]{1,0:T(8,128)(2,1)}, u32[]{:S(2)}, u32[]{:S(2)}) collective-permute-start(bf16[768,256]{1,0:T(8,128)(2,1)} %convolution_convert_fusion.1), channel_id=1, source_target_pairs={{0,64},{64,0},{128,192},{192,128},{256,320},{320,256},{384,448},{4... | collective-permute-start | bytes 1179656 | tf_op jit(solution)/shard_map/ppermute | solution.py:285
  200.7 27.4 %all-to-all-start.3 = ((bf16[64,40,128]{2,1,0:T(8,128)(2,1)}), bf16[64,40,128]{2,1,0:T(8,128)(2,1)S(1)}, u32[]{:S(2)}, u32[]{:S(2)}) async-start(bf16[64,40,128]{2,1,0:T(8,128)(2,1)} %pack.3), calls=%async_computation.4 | async-start | bytes 1310720 | tf_op jit(solution)/shard_map/all_to_all | solution.py:288
  206.1 4.6 %copy-start.18 = (bf16[576,768]{1,0:T(8,128)(2,1)S(1)}, bf16[576,768]{1,0:T(8,128)(2,1)}, u32[]{:S(2)}) copy-start(bf16[576,768]{1,0:T(8,128)(2,1)} %copy-done.16) | copy-start | bytes 2654212
  208.4 4.6 %copy-start.1 = (bf16[512,2560]{1,0:T(8,128)(2,1)S(1)}, bf16[512,2560]{1,0:T(8,128)(2,1)}, u32[]{:S(2)}) copy-start(bf16[512,2560]{1,0:T(8,128)(2,1)} %copy-done) | copy-start | bytes 7864324
  208.4 6.5 %collective-permute-start.5 = (bf16[256,1536]{1,0:T(8,128)(2,1)S(1)}, bf16[256,1536]{1,0:T(8,128)(2,1)S(1)}, u32[]{:S(2)}, u32[]{:S(2)}) collective-permute-start(bf16[256,1536]{1,0:T(8,128)(2,1)S(1)} %convolution_convert_fusion), channel_id=1, source_target_pairs={{0,64},{64,0},{128,192},{192,128},{256,320},{320,256},{384,448},{4... | collective-permute-start | bytes 2359304 | tf_op jit(solution)/shard_map/ppermute | solution.py:285
  213.0 1.5 copy-start.15
  215.2 13.0 %copy-start.5 = (bf16[256,2560]{1,0:T(8,128)(2,1)S(1)}, bf16[256,2560]{1,0:T(8,128)(2,1)}, u32[]{:S(2)}) copy-start(bf16[256,2560]{1,0:T(8,128)(2,1)} %copy-done.4) | copy-start | bytes 3932164
Sparse Core Ops, SparseCore 0:
  68.6 65.0 reduce-scatter.1
  136.9 42.7 all-gather.1

commit v5 on v3

--- a/solution.py
+++ b/solution.py
@@ -140,32 +140,27 @@
     cot_out[...] = mul(coefs, sides).reshape(experts, chunk, lanes).astype(LOW)
 
 
-def table_kernel(pad, rank_ref, weight_ref, pick_out, weight_out):
+def table_kernel(capacity, rank_ref, weight_ref, pick_out, weight_out):
     experts, tok_rows = rank_ref.shape
-    chunk = 2 * pad
-    slots = experts * chunk
-    owner = owners((experts, slots), 1, chunk)
-    spread = mul(rank_ref[...].T.astype(LOW), owner)
-    high, rest = split_low(weight_ref[...].T)
-    high, rest = mul(high, owner), mul(rest, owner)
-    for side, place in enumerate(wanted((tok_rows, slots), 1, pad)):
-        picked = spread == place
-        pick_out[side * tok_rows : (side + 1) * tok_rows, :] = low_if(picked)
-        for at, part in enumerate((high, rest)):
-            first = (2 * side + at) * tok_rows
-            weight_out[first : first + tok_rows, :] = jnp.where(picked, part, 0.0).astype(LOW)
-
-
-def combine_kernel(parts, table_ref, rows_ref, out_ref):
-    tok_rows, width = out_ref.shape
-    lanes = width // 2
-    sums = mul(table_ref[...], rows_ref[...].reshape(table_ref.shape[1], lanes))
-    for side in range(2):
-        total = sums[parts * side * tok_rows : (parts * side + 1) * tok_rows]
-        for at in range(1, parts):
-            first = (parts * side + at) * tok_rows
-            total = total + sums[first : first + tok_rows]
-        out_ref[:, side * lanes : (side + 1) * lanes] = total.astype(LOW)
+    slots = experts * capacity
+    owner = owners((experts, slots), 1, capacity)
+    place = remainder(number((1, slots), 1), capacity)
+    picked = mul(rank_ref[...].T.astype(LOW), owner) == place
+    pick_out[...] = low_if(picked)
+    for at, part in enumerate(split_low(weight_ref[...].T)):
+        weight_out[at * tok_rows : (at + 1) * tok_rows, :] = jnp.where(
+            picked, mul(part, owner), 0.0
+        ).astype(LOW)
+
+
+def places(group, capacity, transposed):
+    size = 4 * group * capacity
+    chunked = number((1, size) if transposed else (size, 1), 1 if transposed else 0)
+    expert = jnp.floor((chunked + 0.5) * (1.0 / (4 * capacity)))
+    within = chunked - 4 * capacity * expert
+    piece = jnp.floor((within + 0.5) * (1.0 / capacity))
+    stacked = within - capacity * piece + capacity * (expert + group * piece)
+    return low_if(number((size, size), 0 if transposed else 1) == stacked)
 
 
 def shifts(shape, row_axis, capacity, pad, side):
@@ -194,19 +189,59 @@
                 ).astype(LOW)
 
 
-def pack_kernel(capacity, pad, core_ref, mine_ref, got_ref, chunks_out):
+def pack_kernel(
+    capacity,
+    core_ref,
+    parity_ref,
+    out_mine_ref,
+    out_got_ref,
+    same_mine_ref,
+    same_got_ref,
+    near_mine_ref,
+    near_got_ref,
+    chunks_out,
+):
     lanes = chunks_out.shape[2]
     half = chunks_out.shape[0] // 2
-    rows, slots = GROUP * capacity, GROUP * 2 * pad
-    moves = [shifts((slots, rows), 1, capacity, pad, side) for side in range(2)]
+    rows = GROUP * capacity
+    moves = places(GROUP, capacity, False)
     core = core_ref[0]
-    for in_ref, base in ((mine_ref, core * half), (got_ref, (1 - core) * half)):
+    odd = parity_ref[0] == 1
+    for out_ref, same_ref, near_ref, base in (
+        (out_mine_ref, same_mine_ref, near_mine_ref, core * half),
+        (out_got_ref, same_got_ref, near_got_ref, (1 - core) * half),
+    ):
         for at in range(half // GROUP):
-            block = in_ref[at * rows : (at + 1) * rows, :]
-            chunk = mul(moves[0], block[:, :lanes]) + mul(moves[1], block[:, lanes:])
-            chunks_out[pl.ds(base + at * GROUP, GROUP)] = chunk.reshape(
-                GROUP, 2 * pad, lanes
+            same, near = same_ref[at].astype(WIDE), near_ref[at].astype(WIDE)
+            grads = jnp.concatenate(
+                [jnp.where(odd, near, same), jnp.where(odd, same, near)], axis=0
             ).astype(LOW)
+            outs = out_ref[at * rows : (at + 1) * rows, :]
+            stacked = jnp.concatenate(
+                [outs[:, :lanes], outs[:, lanes:], grads[:, :lanes], grads[:, lanes:]], axis=0
+            )
+            chunks_out[pl.ds(base + at * GROUP, GROUP)] = (
+                mul(moves, stacked).reshape(GROUP, 4 * capacity, lanes).astype(LOW)
+            )
+
+
+def merge_kernel(
+    capacity, chunks_ref, pick_ref, weight_ref, layer_out, token_out, out_rows, grad_rows
+):
+    experts, _, lanes = chunks_ref.shape
+    tok_rows = layer_out.shape[0]
+    rows = GROUP * capacity
+    moves = places(GROUP, capacity, True)
+    for at in range(experts // GROUP):
+        chunk = chunks_ref[at * GROUP : (at + 1) * GROUP].reshape(4 * rows, lanes)
+        pieces = mul(moves, chunk).astype(LOW)
+        for piece in range(4):
+            target = (out_rows, grad_rows)[piece // 2]
+            cols = slice(piece % 2 * lanes, (piece % 2 + 1) * lanes)
+            target[at * rows : (at + 1) * rows, cols] = pieces[piece * rows : (piece + 1) * rows]
+    sums = mul(weight_ref[...], out_rows[...])
+    layer_out[...] = (sums[:tok_rows] + sums[tok_rows:]).astype(LOW)
+    token_out[...] = mul(pick_ref[...], grad_rows[...]).astype(LOW)
 
 
 def gate_up_kernel(keep_ref, got_ref, gate_ref, up_ref, other_ref, out_ref):
@@ -226,6 +261,30 @@
         second = parts[(2 * at + 1) * block : (2 * at + 2) * block]
         stay_out[at] = jnp.where(odd, second, first).astype(LOW)
         leave_out[at] = jnp.where(odd, first, second).astype(LOW)
+
+
+def hidden_kernel(shares_ref, hidden_out):
+    ff = shares_ref.shape[1] // 2
+    active, _ = swish_parts(shares_ref[:, :ff].astype(WIDE))
+    hidden_out[:, :ff] = (active * shares_ref[:, ff:].astype(WIDE)).astype(LOW)
+    hidden_out[:, ff:] = jnp.zeros((shares_ref.shape[0], hidden_out.shape[1] - ff), LOW)
+
+
+def derived_kernel(shares_ref, parts_ref, derived_out):
+    ff = parts_ref.shape[2]
+    up_val = shares_ref[:, ff:].astype(WIDE)
+    grad_hidden = parts_ref[0].astype(WIDE)
+    for at in range(1, parts_ref.shape[0]):
+        grad_hidden = grad_hidden + parts_ref[at].astype(WIDE)
+    active, slope = swish_parts(shares_ref[:, :ff].astype(WIDE))
+    derived_out[:, :ff] = (grad_hidden * up_val * slope).astype(LOW)
+    derived_out[:, ff:] = (grad_hidden * active).astype(LOW)
+
+
+def input_kernel(rows_ref, own_ref, other_ref, mine_out, give_out):
+    rows = rows_ref[...]
+    give_out[...] = against(rows, other_ref[...]).reshape(give_out.shape).astype(LOW)
+    mine_out[...] = against(rows, own_ref[...]).reshape(mine_out.shape).astype(LOW)
 
 
 def body(
@@ -238,7 +297,7 @@
     half = experts * capacity // 2
     width = tokens.shape[1]
     lanes = width // 2
-    slots = experts * 2 * pad
+    slots = experts * capacity
     ff = gate_weight.shape[2]
     devices = lax.axis_size("dp")
     chips = devices // 2
@@ -279,23 +338,6 @@
         )(core, chunks)
         return keep, swap(give)
 
-    def pack(mine, got):
-        return pl.pallas_call(
-            functools.partial(pack_kernel, capacity, pad),
-            out_shape=chunk_shape,
-            in_specs=[in_smem, in_vmem, in_vmem],
-            compiler_params=params,
-            name="pack",
-        )(core, mine, got)
-
-    def merge(parts, table, chunks):
-        return pl.pallas_call(
-            functools.partial(combine_kernel, parts),
-            out_shape=tok_shape,
-            compiler_params=params,
-            name="merge",
-        )(table, chunks)
-
     gate_own, up_own, down_own = gate_weight[0], up_weight[0], down_weight[0]
     gu_own = jnp.concatenate([gate_own, up_own], axis=1)
     gu_other = swap(gu_own)
@@ -315,23 +357,24 @@
         compiler_params=pltpu.CompilerParams(vmem_limit_bytes=63 * 1024 * 1024),
         name="token_rows",
     )(routes.T, combine.T, limits.reshape(1, experts), tokens)
-    token_keep, token_got = unpack(exchange(token_send))
+    grad_send = pl.pallas_call(
+        functools.partial(grad_kernel, pad),
+        out_shape=chunk_shape,
+        compiler_params=params,
+        name="grad_rows",
+    )(rank, weight, clip_mask.reshape(1, tok_rows), cotangent)
+    token_chunks, grad_send = lax.optimization_barrier((exchange(token_send), grad_send))
+    token_keep, token_got = unpack(token_chunks)
     gate_up = pl.pallas_call(
         gate_up_kernel,
         out_shape=jax.ShapeDtypeStruct((half, 2 * ff), LOW),
         compiler_params=params,
         name="gate_up",
     )(token_keep, token_got, gate_own, up_own, gu_other)
-    grad_send = pl.pallas_call(
-        functools.partial(grad_kernel, pad),
-        out_shape=chunk_shape,
-        compiler_params=params,
-        name="grad_rows",
-    )(rank, weight, clip_mask.reshape(1, tok_rows), cotangent)
     gate_up, grad_send = lax.optimization_barrier((gate_up, grad_send))
     shares = lax.psum_scatter(
         gate_up, "dp", scatter_dimension=0, tiled=True, axis_index_groups=column
-    ).astype(WIDE)
+    )
     grad_keep, grad_got = unpack(exchange(grad_send))
     part_shape = jax.ShapeDtypeStruct((chips // 2, half // chips, ff), LOW)
     stay, leave = pl.pallas_call(
@@ -342,25 +385,60 @@
         name="hidden_grad",
     )(parity, grad_keep, grad_got, down_own, down_other)
     joined = (stay.astype(WIDE) + lax.ppermute(leave, "dp", near_pairs).astype(WIDE)).astype(LOW)
-    grad_hidden = jnp.sum(
-        lax.all_to_all(
-            joined, "dp", split_axis=0, concat_axis=0, tiled=True, axis_index_groups=alike
-        ).astype(WIDE),
-        axis=0,
-    )
-    gate_val, up_val = shares[:, :ff], shares[:, ff:]
-    active, slope = swish_parts(gate_val)
-    hidden = (active * up_val).astype(LOW)
-    derived = jnp.concatenate(
-        [(grad_hidden * up_val * slope).astype(LOW), (grad_hidden * active).astype(LOW)], axis=1
-    )
-    derived_full = lax.all_gather(derived, "dp", axis=0, tiled=True, axis_index_groups=column)
-    hidden_full = lax.all_gather(hidden, "dp", axis=0, tiled=True, axis_index_groups=column)
+    share_rows = half // chips
+    hidden = pl.pallas_call(
+        hidden_kernel,
+        out_shape=jax.ShapeDtypeStruct((share_rows, 4 * ff // 3), LOW),
+        compiler_params=params,
+        name="hidden",
+    )(shares)
+    hidden, joined = lax.optimization_barrier((hidden, joined))
+    hidden_full = lax.all_gather(
+        hidden, "dp", axis=0, tiled=True, axis_index_groups=column
+    )[:, :ff]
+    grad_parts = lax.all_to_all(
+        joined, "dp", split_axis=0, concat_axis=0, tiled=True, axis_index_groups=alike
+    )
+    derived = pl.pallas_call(
+        derived_kernel,
+        out_shape=jax.ShapeDtypeStruct((share_rows, 2 * ff), LOW),
+        compiler_params=params,
+        name="derived",
+    )(shares, grad_parts)
+    same_rows = lax.all_gather(derived, "dp", axis=0, tiled=True, axis_index_groups=alike)
+    near_rows = lax.ppermute(same_rows, "dp", near_pairs)
+    block_shape = jax.ShapeDtypeStruct((chips // 2, share_rows, width), LOW)
+
+    def input_rows(rows):
+        mine, give = pl.pallas_call(
+            input_kernel,
+            out_shape=(block_shape, block_shape),
+            compiler_params=params,
+            name="input_rows",
+        )(rows, gu_own, gu_other)
+        return mine, swap(give)
+
+    same_mine, same_got = input_rows(same_rows)
+    near_mine, near_got = input_rows(near_rows)
     out_got = swap(mul(hidden_full, down_other).astype(LOW))
-    back_rows = exchange(pack(mul(hidden_full, down_own).astype(LOW), out_got))
-    input_got = swap(against(derived_full, gu_other).astype(LOW))
-    grads_back = exchange(pack(against(derived_full, gu_own).astype(LOW), input_got))
-
+    out_mine = mul(hidden_full, down_own).astype(LOW)
+    back = exchange(
+        pl.pallas_call(
+            functools.partial(pack_kernel, capacity),
+            out_shape=jax.ShapeDtypeStruct((experts, 4 * capacity, lanes), LOW),
+            in_specs=[in_smem] * 2 + [in_vmem] * 6,
+            compiler_params=params,
+            name="pack",
+        )(core, parity, out_mine, out_got, same_mine, same_got, near_mine, near_got)
+    )
+
+    same_blocks = same_rows.reshape(chips // 2, share_rows, 2 * ff)
+    near_blocks = near_rows.reshape(chips // 2, share_rows, 2 * ff)
+    derived_full = jnp.where(
+        parity[0] == 0,
+        jnp.stack([same_blocks, near_blocks], axis=1),
+        jnp.stack([near_blocks, same_blocks], axis=1),
+    ).reshape(half, 2 * ff)
     lower_got = swap(outer(hidden_full, grad_got).astype(LOW))
     down_grads = (outer(hidden_full, grad_keep) + lower_got.astype(WIDE)).astype(LOW)
     upper_got = swap(outer(token_got, derived_full).astype(LOW)).astype(WIDE)
@@ -368,16 +446,22 @@
     up_grads = (outer(token_keep, derived_full[:, ff:]) + upper_got[:, ff:]).astype(LOW)
 
     picks, weights = pl.pallas_call(
-        functools.partial(table_kernel, pad),
+        functools.partial(table_kernel, capacity),
         out_shape=(
+            jax.ShapeDtypeStruct((tok_rows, slots), LOW),
             jax.ShapeDtypeStruct((2 * tok_rows, slots), LOW),
-            jax.ShapeDtypeStruct((4 * tok_rows, slots), LOW),
         ),
         compiler_params=params,
         name="tables",
     )(rank, weight)
-    layer_out = merge(2, weights, back_rows)
-    token_grads = merge(1, picks, grads_back)
+    rows_scratch = pltpu.VMEM((slots, width), LOW)
+    layer_out, token_grads = pl.pallas_call(
+        functools.partial(merge_kernel, capacity),
+        out_shape=(tok_shape, tok_shape),
+        scratch_shapes=[rows_scratch, rows_scratch],
+        compiler_params=params,
+        name="merge",
+    )(back, picks, weights)
     return (layer_out, token_grads, gate_grads[None], up_grads[None], down_grads[None])
 
 

time: 234 us -> 230 us (0.983)
  waiting for transfers between devices: 68.9 us -> 76.6 us
  other arithmetic: 7.71 us -> 1.39 us
  blocking collectives: 54.2 us -> 47.9 us
  matrix products: 9.9 us -> 6.39 us
    all_to_all x4 -> x3, starting transfers between devices: 36 us -> 30.9 us  [exchange(): lax.all_to_all(chunks, 'expert', split_axis=0, concat_axis=0, tiled=True)]
    ppermute x0 -> x1, waiting for transfers between devices: none -> 4.5 us  [body(): near_rows = lax.ppermute(same_rows, 'dp', near_pairs)]
    all_gather x1, blocking collectives: 27.9 us -> 24.4 us  [body(): lax.all_gather(derived, 'dp', axis=0, tiled=True, axis_index_groups=alike)]
    ppermute x0 -> x1, starting transfers between devices: none -> 3.57 us  [body(): near_rows = lax.ppermute(same_rows, 'dp', near_pairs)]
    dot_general x2 -> x0, matrix products: 3.05 us -> none  [against(): lax.dot_general(left, right, (((1,), (1,)), ((), ())), preferred_element_...]
    all_to_all x1, blocking collectives: 26.3 us -> 23.5 us  [body(): lax.all_to_all(joined, 'dp', split_axis=0, concat_axis=0, tiled=True, axi...]
    ppermute x8 -> x9, starting transfers between devices: 16.2 us -> 18.7 us  [swap(): return lax.ppermute(values, 'dp', swap_pairs)]
    unnamed x44 -> x46, local copies, waits for them, and re-layouts: 3.35 us -> 4.82 us
  transfers between devices with their start and end apart: 15 -> 16, of which waited for: 7 -> 9; matrix products, arithmetic and copies ran while one was open for 6% -> 3% of each run, Pallas kernels for 5% -> 3%
where the time goes in v5:
time: 230 us; the launch traced here: 229 us
  waiting for transfers between devices  76.6 us (33%)
  starting transfers between devices  58.2 us (25%)
  blocking collectives  47.9 us (21%)
  Pallas kernels  18.7 us (8%)
  between operations  14.6 us (6%)
  matrix products  6.39 us (3%)
  local copies, waits for them, and re-layouts  4.82 us (2%)
    all_to_all x3, waiting for transfers between devices, exchange(): lax.all_to_all(chunks, 'expert', split_axis=0, concat_axis=0, tiled=True)  55.5 us
    all_to_all x3, starting transfers between devices, exchange(): lax.all_to_all(chunks, 'expert', split_axis=0, concat_axis=0, tiled=True)  30.9 us
    all_gather x1, blocking collectives, body(): lax.all_gather(derived, 'dp', axis=0, tiled=True, axis_index_groups=alike)  24.4 us
    all_to_all x1, blocking collectives, body(): lax.all_to_all(joined, 'dp', split_axis=0, concat_axis=0, tiled=True, axi...  23.5 us
    ppermute x9, starting transfers between devices, swap(): return lax.ppermute(values, 'dp', swap_pairs)  18.7 us
    ppermute x1, waiting for transfers between devices, body(): lax.ppermute(leave, 'dp', near_pairs).astype(WIDE)  10.9 us
    ppermute x1, starting transfers between devices, body(): lax.ppermute(leave, 'dp', near_pairs).astype(WIDE)  4.93 us
    unnamed x46, local copies, waits for them, and re-layouts  4.82 us
  transfers between devices with their start and end apart: 16, of which 9 were waited for; matrix products, arithmetic and copies ran while one was open for 3% of the time, Pallas kernels for 3%

profile of v5, /device:TPU:4, one launch (start us, length us, event | category | flops | bytes accessed | tf_op | source)
XLA Modules:
  0.0 228.6 jit_solution(9526441376765417814)
XLA Ops:
  7.2 2.8 %token_rows.1 = (bf16[64,40,128]{2,1,0:T(8,128)(2,1)}, f32[64,128]{1,0:T(8,128)}, f32[64,128]{1,0:T(8,128)}) custom-call(s32[8,128]{1,0:T(8,128)} %bitcast.45, f32[8,128]{1,0:T(8,128)} %bitcast.46, s32[1,64]{1,0:T(1,128)} %bitcast.47, bf16[128,256]{1,0:T(8,128)(2,1)} %tokens_hbm.1), custom_call_target="tpu_custom_call" | custom-call | tf_op jit(solution)/shard_map/token_rows/pallas_call | solution.py:346
  10.1 0.0 copy-start.15
  10.1 17.3 %all-to-all-start = ((bf16[64,40,128]{2,1,0:T(8,128)(2,1)}), bf16[64,40,128]{2,1,0:T(8,128)(2,1)S(1)}, u32[]{:S(2)}, u32[]{:S(2)}) async-start(bf16[64,40,128]{2,1,0:T(8,128)(2,1)} %get-tuple-element.28), calls=%async_computation | async-start | bytes 1310720 | tf_op jit(solution)/shard_map/all_to_all | solution.py:329
  27.4 0.0 reduce-scatter.2.cloned.1.call-start
  27.5 0.1 pad_maximum_fusion.own_ref
  27.6 1.9 collective-permute-start.1
  29.5 2.5 %grad_rows.1 = bf16[64,40,128]{2,1,0:T(8,128)(2,1)} custom-call(f32[64,128]{1,0:T(8,128)S(1)} %copy-done.15, f32[64,128]{1,0:T(8,128)S(1)} %copy-done.17, s32[1,128]{1,0:T(1,128)S(1)} %bitcast.41, bf16[128,256]{1,0:T(8,128)(2,1)S(1)} %copy-done.19), custom_call_target="tpu_custom_call" | custom-call | tf_op jit(solution)/shard_map/grad_rows/pallas_call | solution.py:360
  32.1 13.8 %all-to-all-done.chunks_ref = bf16[64,40,128]{2,1,0:T(8,128)(2,1)S(1)} async-done(((bf16[64,40,128]{2,1,0:T(8,128)(2,1)}), bf16[64,40,128]{2,1,0:T(8,128)(2,1)S(1)}, u32[]{:S(2)}, u32[]{:S(2)}) %all-to-all-start) | async-done | bytes 655392 | tf_op jit(solution)/shard_map/all_to_all | solution.py:329
  45.9 0.8 unpack.2
  46.7 1.9 collective-permute-start
  48.6 1.5 collective-permute-done.got_ref
  50.1 2.3 %gate_up.1 = bf16[576,1536]{1,0:T(8,128)(2,1)} custom-call(bf16[576,256]{1,0:T(8,128)(2,1)S(1)} %get-tuple-element.32.keep_ref, bf16[576,256]{1,0:T(8,128)(2,1)S(1)} %collective-permute-done.got_ref, bf16[256,768]{1,0:T(8,128)(2,1)S(1)} %bitcast.36, bf16[256,768]{1,0:T(8,128)(2,1)S(1)} %bitcast.38, bf16[256,1536]{1,0:T(8,128)(2,1)S(1)} %collective-permute-done.1.other_ref), custom_call_target="tpu_custom_call" | custom-call | tf_op jit(solution)/shard_map/gate_up/pallas_call | solution.py:368
  52.5 0.7 copy-done
  53.2 0.7 copy-done.13
  53.9 0.0 reduce-scatter.2.cloned.1.call-update
  53.9 5.6 %all-to-all-start.1 = ((bf16[64,40,128]{2,1,0:T(8,128)(2,1)}), bf16[64,40,128]{2,1,0:T(8,128)(2,1)S(1)}, u32[]{:S(2)}, u32[]{:S(2)}) async-start(bf16[64,40,128]{2,1,0:T(8,128)(2,1)} %grad_rows.1), calls=%async_computation.2 | async-start | bytes 1310720 | tf_op jit(solution)/shard_map/all_to_all | solution.py:329
  59.6 0.0 all-gather.2.cloned.1.call-start
  59.6 1.9 collective-permute-start.3
  61.6 20.5 %all-to-all-done.1.chunks_ref = bf16[64,40,128]{2,1,0:T(8,128)(2,1)S(1)} async-done(((bf16[64,40,128]{2,1,0:T(8,128)(2,1)}), bf16[64,40,128]{2,1,0:T(8,128)(2,1)S(1)}, u32[]{:S(2)}, u32[]{:S(2)}) %all-to-all-start.1) | async-done | bytes 655392 | tf_op jit(solution)/shard_map/all_to_all | solution.py:329
  82.1 1.5 unpack.3
  83.6 1.9 collective-permute-start.2
  85.5 1.7 collective-permute-done.2.got_ref
  87.2 0.7 hidden_grad.1
  87.9 4.9 %collective-permute-start.4 = (bf16[4,72,768]{2,1,0:T(8,128)(2,1)S(1)}, bf16[4,72,768]{2,1,0:T(8,128)(2,1)S(1)}, u32[]{:S(2)}, u32[]{:S(2)}) collective-permute-start(bf16[4,72,768]{2,1,0:T(8,128)(2,1)S(1)} %get-tuple-element.40), channel_id=1, source_target_pairs={{0,128},{64,960},{128,0},{192,320},{256,384},{320,192},{384,256},{... | collective-permute-start | bytes 1327112 | tf_op jit(solution)/shard_map/ppermute | solution.py:387
  92.8 10.9 %collective-permute-done.4 = bf16[4,72,768]{2,1,0:T(8,128)(2,1)S(1)} collective-permute-done((bf16[4,72,768]{2,1,0:T(8,128)(2,1)S(1)}, bf16[4,72,768]{2,1,0:T(8,128)(2,1)S(1)}, u32[]{:S(2)}, u32[]{:S(2)}) %collective-permute-start.4) | collective-permute-done | bytes 442400 | tf_op jit(solution)/shard_map/ppermute | solution.py:387
  103.8 0.1 add_convert_fusion
  103.9 1.6 reduce-scatter.2.cloned.1.call-done.shares_ref
  105.5 0.9 copy-done.4
  106.5 0.7 hidden.1
  107.2 0.0 all-gather.2.cloned.1.call-update
  107.2 23.5 %all_to_all.20.parts_ref = bf16[4,72,768]{2,1,0:T(8,128)(2,1)S(1)} all-to-all(bf16[4,72,768]{2,1,0:T(8,128)(2,1)S(1)} %add_convert_fusion), channel_id=1, replica_groups={{0,256,512,768},{128,384,640,896},{64,320,576,832},{192,448,704,960},{1..., dimensions={0} | all-to-all | bytes 884736 | tf_op jit(solution)/shard_map/all_to_all | solution.py:399
  130.8 0.9 copy-done.5
  131.7 0.2 derived.1
  131.9 24.4 %all_gather.7.rows_ref = bf16[288,1536]{1,0:T(8,128)(2,1)S(1)} all-gather(bf16[72,1536]{1,0:T(8,128)(2,1)S(1)} %derived.1), channel_id=1, replica_groups={{0,256,512,768},{128,384,640,896},{64,320,576,832},{192,448,704,960},{1..., dimensions={0}, use_global_device_ids=true | all-gather | bytes 1105920 | tf_op jit(solution)/shard_map/all_gather | solution.py:408
  156.2 3.6 %collective-permute-start.7 = (bf16[288,1536]{1,0:T(8,128)(2,1)S(1)}, bf16[288,1536]{1,0:T(8,128)(2,1)S(1)}, u32[]{:S(2)}, u32[]{:S(2)}) collective-permute-start(bf16[288,1536]{1,0:T(8,128)(2,1)S(1)} %all_gather.7.rows_ref), channel_id=1, source_target_pairs={{0,128},{64,960},{128,0},{192,320},{256,384},{320,192},{384,256},{... | collective-permute-start | bytes 2654216 | tf_op jit(solution)/shard_map/ppermute | solution.py:409
  159.8 0.0 all-gather.2.cloned.1.call-done
  159.8 1.7 convolution_convert_fusion.2
  161.5 1.9 collective-permute-start.5
  163.4 0.6 input_rows.2
  164.1 2.5 %collective-permute-start.6 = (bf16[4,72,256]{2,1,0:T(8,128)(2,1)S(1)}, bf16[4,72,256]{2,1,0:T(8,128)(2,1)S(1)}, u32[]{:S(2)}, u32[]{:S(2)}) collective-permute-start(bf16[4,72,256]{2,1,0:T(8,128)(2,1)S(1)} %get-tuple-element.44), channel_id=1, source_target_pairs={{0,64},{64,0},{128,192},{192,128},{256,320},{320,256},{384,448},{4... | collective-permute-start | bytes 442376 | tf_op jit(solution)/shard_map/ppermute | solution.py:326
  166.7 4.5 %collective-permute-done.7.rows_ref = bf16[288,1536]{1,0:T(8,128)(2,1)S(1)} collective-permute-done((bf16[288,1536]{1,0:T(8,128)(2,1)S(1)}, bf16[288,1536]{1,0:T(8,128)(2,1)S(1)}, u32[]{:S(2)}, u32[]{:S(2)}) %collective-permute-start.7) | collective-permute-done | bytes 884768 | tf_op jit(solution)/shard_map/ppermute | solution.py:409
  171.2 0.7 input_rows.3
  171.8 2.1 collective-permute-start.8
  174.0 0.4 convolution_convert_fusion.3.out_mine_ref
  174.4 0.7 collective-permute-done.8.near_got_ref
  175.1 2.9 %pack.1 = bf16[64,72,128]{2,1,0:T(8,128)(2,1)} custom-call(s32[1]{0:T(128)} %bitcast.core_ref, s32[1]{0:T(128)} %bitcast.1.parity_ref, bf16[576,256]{1,0:T(8,128)(2,1)S(1)} %convolution_convert_fusion.3.out_mine_ref, bf16[576,256]{1,0:T(8,128)(2,1)S(1)} %collective-permute-done.5.out_got_ref, bf16[4,72,256]{2,1,0:T(8,128)(2,1)S(1)} %get-tuple-element.43.same_mine_ref, ...), custom_call_target="tpu_custom_call" | custom-call | tf_op jit(solution)/shard_map/pack/pallas_call | solution.py:426
  178.0 7.9 %all-to-all-start.3 = ((bf16[64,72,128]{2,1,0:T(8,128)(2,1)}), bf16[64,72,128]{2,1,0:T(8,128)(2,1)S(1)}, u32[]{:S(2)}, u32[]{:S(2)}) async-start(bf16[64,72,128]{2,1,0:T(8,128)(2,1)} %pack.1), calls=%async_computation.4 | async-start | bytes 2359296 | tf_op jit(solution)/shard_map/all_to_all | solution.py:329
  185.9 0.2 maximum_select_fusion
  186.1 0.0 copy-start.18
  186.1 0.0 copy-start.12
  186.2 0.7 copy-done.14
  186.8 0.8 convolution_convert_fusion
  187.6 2.1 collective-permute-start.9
  189.7 0.5 tables.1
  190.2 0.5 convolution_convert_fusion.1
  190.7 2.4 %collective-permute-start.10 = (bf16[768,256]{1,0:T(8,128)(2,1)S(1)}, bf16[768,256]{1,0:T(8,128)(2,1)S(1)}, u32[]{:S(2)}, u32[]{:S(2)}) collective-permute-start(bf16[768,256]{1,0:T(8,128)(2,1)S(1)} %convolution_convert_fusion.1), channel_id=1, source_target_pairs={{0,64},{64,0},{128,192},{192,128},{256,320},{320,256},{384,448},{4... | collective-permute-start | bytes 1179656 | tf_op jit(solution)/shard_map/ppermute | solution.py:326
  193.2 0.5 fusion.23
  193.7 0.2 convert_element_type.42
  193.9 0.8 copy-done.1
  194.6 1.3 fusion.8
  195.9 1.3 fusion.19
  197.2 0.8 fusion.27
  198.0 21.2 %all-to-all-done.3.chunks_ref = bf16[64,72,128]{2,1,0:T(8,128)(2,1)S(1)} async-done(((bf16[64,72,128]{2,1,0:T(8,128)(2,1)}), bf16[64,72,128]{2,1,0:T(8,128)(2,1)S(1)}, u32[]{:S(2)}, u32[]{:S(2)}) %all-to-all-start.3) | async-done | bytes 1179680 | tf_op jit(solution)/shard_map/all_to_all | solution.py:329
  219.2 2.6 %merge.1 = (bf16[128,256]{1,0:T(8,128)(2,1)}, bf16[128,256]{1,0:T(8,128)(2,1)}) custom-call(bf16[64,72,128]{2,1,0:T(8,128)(2,1)S(1)} %all-to-all-done.3.chunks_ref, bf16[128,1152]{1,0:T(8,128)(2,1)S(1)} %get-tuple-element.47.pick_ref, bf16[256,1152]{1,0:T(8,128)(2,1)S(1)} %get-tuple-element.48.weight_ref), custom_call_target="tpu_custom_call" | custom-call | tf_op jit(solution)/shard_map/merge/pallas_call | solution.py:458
  (43 shorter events, 0.1 us)
Async XLA Ops:
  7.2 20.3 %copy-start.3 = (bf16[1,256,768]{2,1,0:T(8,128)(2,1)S(1)}, bf16[1,256,768]{2,1,0:T(8,128)(2,1)}, u32[]{:S(2)}) copy-start(bf16[1,256,768]{2,1,0:T(8,128)(2,1)} %param.16) | copy-start | bytes 1179652
  7.2 20.3 %copy-start.2 = (bf16[1,256,768]{2,1,0:T(8,128)(2,1)S(1)}, bf16[1,256,768]{2,1,0:T(8,128)(2,1)}, u32[]{:S(2)}) copy-start(bf16[1,256,768]{2,1,0:T(8,128)(2,1)} %param.15) | copy-start | bytes 1179652
  7.2 22.3 %copy-start.19 = (bf16[128,256]{1,0:T(8,128)(2,1)S(1)}, bf16[128,256]{1,0:T(8,128)(2,1)}, u32[]{:S(2)}) copy-start(bf16[128,256]{1,0:T(8,128)(2,1)} %cot_ref.1) | copy-start | bytes 196612
  7.2 22.3 %copy-start.20 = (s32[128]{0:T(128)S(1)}, s32[128]{0:T(128)}, u32[]{:S(2)}) copy-start(s32[128]{0:T(128)} %param.12) | copy-start | bytes 1540
  10.1 19.5 %copy-start.15 = (f32[64,128]{1,0:T(8,128)S(1)}, f32[64,128]{1,0:T(8,128)}, u32[]{:S(2)}) copy-start(f32[64,128]{1,0:T(8,128)} %get-tuple-element.29.rank_ref) | copy-start | bytes 98308
  10.1 19.5 %copy-start.17 = (f32[64,128]{1,0:T(8,128)S(1)}, f32[64,128]{1,0:T(8,128)}, u32[]{:S(2)}) copy-start(f32[64,128]{1,0:T(8,128)} %get-tuple-element.30.weight_ref) | copy-start | bytes 98308
  10.1 35.8 %all-to-all-start = ((bf16[64,40,128]{2,1,0:T(8,128)(2,1)}), bf16[64,40,128]{2,1,0:T(8,128)(2,1)S(1)}, u32[]{:S(2)}, u32[]{:S(2)}) async-start(bf16[64,40,128]{2,1,0:T(8,128)(2,1)} %get-tuple-element.28), calls=%async_computation | async-start | bytes 1310720 | tf_op jit(solution)/shard_map/all_to_all | solution.py:329
  27.4 78.1 %reduce-scatter.2.cloned.1.call-start = ((), (), s32[]{:S(2)}) async-start(), calls=%async_computation.5 | async-start | bytes 1990656 | tf_op jit(solution)/shard_map/reduce_scatter | solution.py:375
  27.6 21.0 %collective-permute-start.1 = (bf16[256,1536]{1,0:T(8,128)(2,1)S(1)}, bf16[256,1536]{1,0:T(8,128)(2,1)S(1)}, u32[]{:S(2)}, u32[]{:S(2)}) collective-permute-start(bf16[256,1536]{1,0:T(8,128)(2,1)S(1)} %pad_maximum_fusion.own_ref), channel_id=1, source_target_pairs={{0,64},{64,0},{128,192},{192,128},{256,320},{320,256},{384,448},{4... | collective-permute-start | bytes 2359304 | tf_op jit(solution)/shard_map/ppermute | solution.py:326
  46.7 3.5 %collective-permute-start = (bf16[576,256]{1,0:T(8,128)(2,1)S(1)}, bf16[576,256]{1,0:T(8,128)(2,1)S(1)}, u32[]{:S(2)}, u32[]{:S(2)}) collective-permute-start(bf16[576,256]{1,0:T(8,128)(2,1)S(1)} %get-tuple-element.33), channel_id=1, source_target_pairs={{0,64},{64,0},{128,192},{192,128},{256,320},{320,256},{384,448},{4... | collective-permute-start | bytes 884744 | tf_op jit(solution)/shard_map/ppermute | solution.py:326
  52.5 0.7 copy-start
  53.2 0.7 copy-start.13
  53.9 5.7 %copy-start.6 = (bf16[1,768,256]{2,1,0:T(8,128)(2,1)S(1)}, bf16[1,768,256]{2,1,0:T(8,128)(2,1)}, u32[]{:S(2)}) copy-start(bf16[1,768,256]{2,1,0:T(8,128)(2,1)} %param.17) | copy-start | bytes 1179652
  53.9 28.1 %all-to-all-start.1 = ((bf16[64,40,128]{2,1,0:T(8,128)(2,1)}), bf16[64,40,128]{2,1,0:T(8,128)(2,1)S(1)}, u32[]{:S(2)}, u32[]{:S(2)}) async-start(bf16[64,40,128]{2,1,0:T(8,128)(2,1)} %grad_rows.1), calls=%async_computation.2 | async-start | bytes 1310720 | tf_op jit(solution)/shard_map/all_to_all | solution.py:329
  59.6 100.3 %all-gather.2.cloned.1.call-start = ((), (), s32[]{:S(2)}) async-start(), calls=%async_computation.6 | async-start | bytes 1327104 | tf_op jit(solution)/shard_map/all_gather | solution.py:396
  59.6 25.9 %collective-permute-start.3 = (bf16[768,256]{1,0:T(8,128)(2,1)S(1)}, bf16[768,256]{1,0:T(8,128)(2,1)S(1)}, u32[]{:S(2)}, u32[]{:S(2)}) collective-permute-start(bf16[768,256]{1,0:T(8,128)(2,1)S(1)} %bitcast.39), channel_id=1, source_target_pairs={{0,64},{64,0},{128,192},{192,128},{256,320},{320,256},{384,448},{4... | collective-permute-start | bytes 1179656 | tf_op jit(solution)/shard_map/ppermute | solution.py:326
  83.6 23.6 %copy-start.9 = (bf16[576,256]{1,0:T(8,128)(2,1)}, bf16[576,256]{1,0:T(8,128)(2,1)S(1)}, u32[]{:S(2)}) copy-start(bf16[576,256]{1,0:T(8,128)(2,1)S(1)} %get-tuple-element.37.keep_ref) | copy-start | bytes 884740
  83.6 3.7 %collective-permute-start.2 = (bf16[576,256]{1,0:T(8,128)(2,1)}, bf16[576,256]{1,0:T(8,128)(2,1)S(1)}, u32[]{:S(2)}, u32[]{:S(2)}) collective-permute-start(bf16[576,256]{1,0:T(8,128)(2,1)} %get-tuple-element.38), channel_id=1, source_target_pairs={{0,64},{64,0},{128,192},{192,128},{256,320},{320,256},{384,448},{4... | collective-permute-start | bytes 884744 | tf_op jit(solution)/shard_map/ppermute | solution.py:326
  85.5 46.4 %copy-start.8 = (bf16[768,256]{1,0:T(8,128)(2,1)}, bf16[768,256]{1,0:T(8,128)(2,1)S(1)}, u32[]{:S(2)}) copy-start(bf16[768,256]{1,0:T(8,128)(2,1)S(1)} %collective-permute-done.3.other_ref) | copy-start | bytes 1179652
  87.2 20.0 %copy-start.11 = (bf16[576,256]{1,0:T(8,128)(2,1)}, bf16[576,256]{1,0:T(8,128)(2,1)S(1)}, u32[]{:S(2)}) copy-start(bf16[576,256]{1,0:T(8,128)(2,1)S(1)} %collective-permute-done.2.got_ref) | copy-start | bytes 884740
  87.9 15.9 %collective-permute-start.4 = (bf16[4,72,768]{2,1,0:T(8,128)(2,1)S(1)}, bf16[4,72,768]{2,1,0:T(8,128)(2,1)S(1)}, u32[]{:S(2)}, u32[]{:S(2)}) collective-permute-start(bf16[4,72,768]{2,1,0:T(8,128)(2,1)S(1)} %get-tuple-element.40), channel_id=1, source_target_pairs={{0,128},{64,960},{128,0},{192,320},{256,384},{320,192},{384,256},{... | collective-permute-start | bytes 1327112 | tf_op jit(solution)/shard_map/ppermute | solution.py:387
  105.5 0.9 copy-start.4
  130.8 0.9 copy-start.5
  156.2 14.9 %collective-permute-start.7 = (bf16[288,1536]{1,0:T(8,128)(2,1)S(1)}, bf16[288,1536]{1,0:T(8,128)(2,1)S(1)}, u32[]{:S(2)}, u32[]{:S(2)}) collective-permute-start(bf16[288,1536]{1,0:T(8,128)(2,1)S(1)} %all_gather.7.rows_ref), channel_id=1, source_target_pairs={{0,128},{64,960},{128,0},{192,320},{256,384},{320,192},{384,256},{... | collective-permute-start | bytes 2654216 | tf_op jit(solution)/shard_map/ppermute | solution.py:409
  161.5 13.6 %collective-permute-start.5 = (bf16[576,256]{1,0:T(8,128)(2,1)S(1)}, bf16[576,256]{1,0:T(8,128)(2,1)S(1)}, u32[]{:S(2)}, u32[]{:S(2)}) collective-permute-start(bf16[576,256]{1,0:T(8,128)(2,1)S(1)} %convolution_convert_fusion.2), channel_id=1, source_target_pairs={{0,64},{64,0},{128,192},{192,128},{256,320},{320,256},{384,448},{4... | collective-permute-start | bytes 884744 | tf_op jit(solution)/shard_map/ppermute | solution.py:326
  164.1 9.8 %copy-start.7 = (bf16[1,768,256]{2,1,0:T(8,128)(2,1)S(1)}, bf16[1,768,256]{2,1,0:T(8,128)(2,1)}, u32[]{:S(2)}) copy-start(bf16[1,768,256]{2,1,0:T(8,128)(2,1)} %param.17) | copy-start | bytes 1179652
  164.1 9.8 %copy-start.21 = (bf16[576,1024]{1,0:T(8,128)(2,1)S(1)}, bf16[576,1024]{1,0:T(8,128)(2,1)}, u32[]{:S(2)}) copy-start(bf16[576,1024]{1,0:T(8,128)(2,1)} %all-gather.2.cloned.1.call-done) | copy-start | bytes 3538948
  164.1 10.2 %collective-permute-start.6 = (bf16[4,72,256]{2,1,0:T(8,128)(2,1)S(1)}, bf16[4,72,256]{2,1,0:T(8,128)(2,1)S(1)}, u32[]{:S(2)}, u32[]{:S(2)}) collective-permute-start(bf16[4,72,256]{2,1,0:T(8,128)(2,1)S(1)} %get-tuple-element.44), channel_id=1, source_target_pairs={{0,64},{64,0},{128,192},{192,128},{256,320},{320,256},{384,448},{4... | collective-permute-start | bytes 442376 | tf_op jit(solution)/shard_map/ppermute | solution.py:326
  171.8 3.3 %collective-permute-start.8 = (bf16[4,72,256]{2,1,0:T(8,128)(2,1)S(1)}, bf16[4,72,256]{2,1,0:T(8,128)(2,1)S(1)}, u32[]{:S(2)}, u32[]{:S(2)}) collective-permute-start(bf16[4,72,256]{2,1,0:T(8,128)(2,1)S(1)} %get-tuple-element.46), channel_id=1, source_target_pairs={{0,64},{64,0},{128,192},{192,128},{256,320},{320,256},{384,448},{4... | collective-permute-start | bytes 442376 | tf_op jit(solution)/shard_map/ppermute | solution.py:326
  178.0 41.2 %all-to-all-start.3 = ((bf16[64,72,128]{2,1,0:T(8,128)(2,1)}), bf16[64,72,128]{2,1,0:T(8,128)(2,1)S(1)}, u32[]{:S(2)}, u32[]{:S(2)}) async-start(bf16[64,72,128]{2,1,0:T(8,128)(2,1)} %pack.1), calls=%async_computation.4 | async-start | bytes 2359296 | tf_op jit(solution)/shard_map/all_to_all | solution.py:329
  185.9 1.0 copy-start.14
  186.1 3.6 %copy-start.16 = (f32[64,128]{1,0:T(8,128)S(1)}, f32[64,128]{1,0:T(8,128)}, u32[]{:S(2)}) copy-start(f32[64,128]{1,0:T(8,128)} %get-tuple-element.29.rank_ref) | copy-start | bytes 98308
  186.1 3.6 %copy-start.18 = (f32[64,128]{1,0:T(8,128)S(1)}, f32[64,128]{1,0:T(8,128)}, u32[]{:S(2)}) copy-start(f32[64,128]{1,0:T(8,128)} %get-tuple-element.30.weight_ref) | copy-start | bytes 98308
  186.1 4.0 %copy-start.12 = (bf16[576,256]{1,0:T(8,128)(2,1)S(1)}, bf16[576,256]{1,0:T(8,128)(2,1)}, u32[]{:S(2)}) copy-start(bf16[576,256]{1,0:T(8,128)(2,1)} %copy-done.11) | copy-start | bytes 884740
  186.2 4.0 %copy-start.22 = (bf16[576,1024]{1,0:T(8,128)(2,1)S(1)}, bf16[576,1024]{1,0:T(8,128)(2,1)}, u32[]{:S(2)}) copy-start(bf16[576,1024]{1,0:T(8,128)(2,1)} %all-gather.2.cloned.1.call-done) | copy-start | bytes 3538948
  187.6 5.5 %copy-start.10 = (bf16[576,256]{1,0:T(8,128)(2,1)S(1)}, bf16[576,256]{1,0:T(8,128)(2,1)}, u32[]{:S(2)}) copy-start(bf16[576,256]{1,0:T(8,128)(2,1)} %copy-done.9) | copy-start | bytes 884740
  187.6 6.0 %collective-permute-start.9 = (bf16[256,1536]{1,0:T(8,128)(2,1)S(1)}, bf16[256,1536]{1,0:T(8,128)(2,1)S(1)}, u32[]{:S(2)}, u32[]{:S(2)}) collective-permute-start(bf16[256,1536]{1,0:T(8,128)(2,1)S(1)} %convolution_convert_fusion), channel_id=1, source_target_pairs={{0,64},{64,0},{128,192},{192,128},{256,320},{320,256},{384,448},{4... | collective-permute-start | bytes 2359304 | tf_op jit(solution)/shard_map/ppermute | solution.py:326
  190.7 6.4 %collective-permute-start.10 = (bf16[768,256]{1,0:T(8,128)(2,1)S(1)}, bf16[768,256]{1,0:T(8,128)(2,1)S(1)}, u32[]{:S(2)}, u32[]{:S(2)}) collective-permute-start(bf16[768,256]{1,0:T(8,128)(2,1)S(1)} %convolution_convert_fusion.1), channel_id=1, source_target_pairs={{0,64},{64,0},{128,192},{192,128},{256,320},{320,256},{384,448},{4... | collective-permute-start | bytes 1179656 | tf_op jit(solution)/shard_map/ppermute | solution.py:326
  193.7 1.0 copy-start.1
Sparse Core Ops, SparseCore 0:
  54.0 51.4 reduce-scatter.1
  108.2 50.0 all-gather.1

commit v6 on v5

--- a/solution.py
+++ b/solution.py
@@ -189,36 +189,21 @@
                 ).astype(LOW)
 
 
-def pack_kernel(
-    capacity,
-    core_ref,
-    parity_ref,
-    out_mine_ref,
-    out_got_ref,
-    same_mine_ref,
-    same_got_ref,
-    near_mine_ref,
-    near_got_ref,
-    chunks_out,
-):
+def pack_kernel(capacity, core_ref, mine_ref, got_ref, chunks_out):
     lanes = chunks_out.shape[2]
     half = chunks_out.shape[0] // 2
     rows = GROUP * capacity
     moves = places(GROUP, capacity, False)
     core = core_ref[0]
-    odd = parity_ref[0] == 1
-    for out_ref, same_ref, near_ref, base in (
-        (out_mine_ref, same_mine_ref, near_mine_ref, core * half),
-        (out_got_ref, same_got_ref, near_got_ref, (1 - core) * half),
-    ):
+    for in_ref, base in ((mine_ref, core * half), (got_ref, (1 - core) * half)):
         for at in range(half // GROUP):
-            same, near = same_ref[at].astype(WIDE), near_ref[at].astype(WIDE)
-            grads = jnp.concatenate(
-                [jnp.where(odd, near, same), jnp.where(odd, same, near)], axis=0
-            ).astype(LOW)
-            outs = out_ref[at * rows : (at + 1) * rows, :]
             stacked = jnp.concatenate(
-                [outs[:, :lanes], outs[:, lanes:], grads[:, :lanes], grads[:, lanes:]], axis=0
+                [
+                    in_ref[first + at * rows : first + (at + 1) * rows, cols]
+                    for first in (0, half * capacity)
+                    for cols in (slice(0, lanes), slice(lanes, 2 * lanes))
+                ],
+                axis=0,
             )
             chunks_out[pl.ds(base + at * GROUP, GROUP)] = (
                 mul(moves, stacked).reshape(GROUP, 4 * capacity, lanes).astype(LOW)
@@ -263,28 +248,35 @@
         leave_out[at] = jnp.where(odd, first, second).astype(LOW)
 
 
-def hidden_kernel(shares_ref, hidden_out):
-    ff = shares_ref.shape[1] // 2
-    active, _ = swish_parts(shares_ref[:, :ff].astype(WIDE))
-    hidden_out[:, :ff] = (active * shares_ref[:, ff:].astype(WIDE)).astype(LOW)
-    hidden_out[:, ff:] = jnp.zeros((shares_ref.shape[0], hidden_out.shape[1] - ff), LOW)
-
-
-def derived_kernel(shares_ref, parts_ref, derived_out):
-    ff = parts_ref.shape[2]
-    up_val = shares_ref[:, ff:].astype(WIDE)
-    grad_hidden = parts_ref[0].astype(WIDE)
+def total_kernel(parts_ref, out_ref):
+    total = parts_ref[0].astype(WIDE)
     for at in range(1, parts_ref.shape[0]):
-        grad_hidden = grad_hidden + parts_ref[at].astype(WIDE)
-    active, slope = swish_parts(shares_ref[:, :ff].astype(WIDE))
-    derived_out[:, :ff] = (grad_hidden * up_val * slope).astype(LOW)
-    derived_out[:, ff:] = (grad_hidden * active).astype(LOW)
-
-
-def input_kernel(rows_ref, own_ref, other_ref, mine_out, give_out):
-    rows = rows_ref[...]
-    give_out[...] = against(rows, other_ref[...]).reshape(give_out.shape).astype(LOW)
-    mine_out[...] = against(rows, own_ref[...]).reshape(mine_out.shape).astype(LOW)
+        total = total + parts_ref[at].astype(WIDE)
+    out_ref[...] = total.astype(LOW)
+
+
+def give_kernel(
+    shares_ref, grad_ref, gu_ref, down_ref, hidden_out, derived_out, give_out
+):
+    half, ff = grad_ref.shape
+    step = GROUP * (half // 4 // GROUP)
+    for start in range(0, half, step):
+        rows = slice(start, start + step)
+        gate_val = shares_ref[rows, :ff].astype(WIDE)
+        up_val = shares_ref[rows, ff:].astype(WIDE)
+        grad_hidden = grad_ref[rows, :].astype(WIDE)
+        active, slope = swish_parts(gate_val)
+        hidden_out[rows, :] = (active * up_val).astype(LOW)
+        derived_out[rows, :ff] = (grad_hidden * up_val * slope).astype(LOW)
+        derived_out[rows, ff:] = (grad_hidden * active).astype(LOW)
+    give_out[:half, :] = mul(hidden_out[...], down_ref[...]).astype(LOW)
+    give_out[half:, :] = against(derived_out[...], gu_ref[...]).astype(LOW)
+
+
+def mine_kernel(hidden_ref, derived_ref, gu_ref, down_ref, mine_out):
+    half = hidden_ref.shape[0]
+    mine_out[:half, :] = mul(hidden_ref[...], down_ref[...]).astype(LOW)
+    mine_out[half:, :] = against(derived_ref[...], gu_ref[...]).astype(LOW)
 
 
 def body(
@@ -385,60 +377,45 @@
         name="hidden_grad",
     )(parity, grad_keep, grad_got, down_own, down_other)
     joined = (stay.astype(WIDE) + lax.ppermute(leave, "dp", near_pairs).astype(WIDE)).astype(LOW)
-    share_rows = half // chips
-    hidden = pl.pallas_call(
-        hidden_kernel,
-        out_shape=jax.ShapeDtypeStruct((share_rows, 4 * ff // 3), LOW),
-        compiler_params=params,
-        name="hidden",
-    )(shares)
-    hidden, joined = lax.optimization_barrier((hidden, joined))
-    hidden_full = lax.all_gather(
-        hidden, "dp", axis=0, tiled=True, axis_index_groups=column
-    )[:, :ff]
+    shares, joined = lax.optimization_barrier((shares, joined))
+    shares_full = lax.all_gather(shares, "dp", axis=0, tiled=True, axis_index_groups=column)
     grad_parts = lax.all_to_all(
         joined, "dp", split_axis=0, concat_axis=0, tiled=True, axis_index_groups=alike
     )
-    derived = pl.pallas_call(
-        derived_kernel,
-        out_shape=jax.ShapeDtypeStruct((share_rows, 2 * ff), LOW),
-        compiler_params=params,
-        name="derived",
-    )(shares, grad_parts)
-    same_rows = lax.all_gather(derived, "dp", axis=0, tiled=True, axis_index_groups=alike)
-    near_rows = lax.ppermute(same_rows, "dp", near_pairs)
-    block_shape = jax.ShapeDtypeStruct((chips // 2, share_rows, width), LOW)
-
-    def input_rows(rows):
-        mine, give = pl.pallas_call(
-            input_kernel,
-            out_shape=(block_shape, block_shape),
-            compiler_params=params,
-            name="input_rows",
-        )(rows, gu_own, gu_other)
-        return mine, swap(give)
-
-    same_mine, same_got = input_rows(same_rows)
-    near_mine, near_got = input_rows(near_rows)
-    out_got = swap(mul(hidden_full, down_other).astype(LOW))
-    out_mine = mul(hidden_full, down_own).astype(LOW)
+    grad_total = pl.pallas_call(
+        total_kernel,
+        out_shape=jax.ShapeDtypeStruct((half // chips, ff), LOW),
+        compiler_params=params,
+        name="total",
+    )(grad_parts)
+    grad_full = lax.all_gather(grad_total, "dp", axis=0, tiled=True, axis_index_groups=column)
+    pair_shape = jax.ShapeDtypeStruct((2 * half, width), LOW)
+    hidden_full, derived_full, give = pl.pallas_call(
+        give_kernel,
+        out_shape=(
+            jax.ShapeDtypeStruct((half, ff), LOW),
+            jax.ShapeDtypeStruct((half, 2 * ff), LOW),
+            pair_shape,
+        ),
+        compiler_params=params,
+        name="give_rows",
+    )(shares_full, grad_full, gu_other, down_other)
+    mine = pl.pallas_call(
+        mine_kernel,
+        out_shape=pair_shape,
+        compiler_params=params,
+        name="mine_rows",
+    )(hidden_full, derived_full, gu_own, down_own)
     back = exchange(
         pl.pallas_call(
             functools.partial(pack_kernel, capacity),
             out_shape=jax.ShapeDtypeStruct((experts, 4 * capacity, lanes), LOW),
-            in_specs=[in_smem] * 2 + [in_vmem] * 6,
+            in_specs=[in_smem] + [in_vmem] * 2,
             compiler_params=params,
             name="pack",
-        )(core, parity, out_mine, out_got, same_mine, same_got, near_mine, near_got)
-    )
-
-    same_blocks = same_rows.reshape(chips // 2, share_rows, 2 * ff)
-    near_blocks = near_rows.reshape(chips // 2, share_rows, 2 * ff)
-    derived_full = jnp.where(
-        parity[0] == 0,
-        jnp.stack([same_blocks, near_blocks], axis=1),
-        jnp.stack([near_blocks, same_blocks], axis=1),
-    ).reshape(half, 2 * ff)
+        )(core, mine, swap(give))
+    )
+
     lower_got = swap(outer(hidden_full, grad_got).astype(LOW))
     down_grads = (outer(hidden_full, grad_keep) + lower_got.astype(WIDE)).astype(LOW)
     upper_got = swap(outer(token_got, derived_full).astype(LOW)).astype(WIDE)

time: 230 us -> 226 us (0.983)
  starting transfers between devices: 58.2 us -> 54.5 us
  blocking collectives: 47.9 us -> 50.8 us
    ppermute x1 -> x0, waiting for transfers between devices: 4.5 us -> none  [body(): near_rows = lax.ppermute(same_rows, 'dp', near_pairs)]
    ppermute x9 -> x7, starting transfers between devices: 18.7 us -> 14.2 us  [swap(): return lax.ppermute(values, 'dp', swap_pairs)]
    all_to_all x3, starting transfers between devices: 30.9 us -> 35.2 us  [exchange(): lax.all_to_all(chunks, 'expert', split_axis=0, concat_axis=0, tiled=True)]
    all_gather x1, blocking collectives: 24.4 us -> 28.2 us  [body(): lax.all_gather(grad_total, 'dp', axis=0, tiled=True, axis_index_groups=co...]
    ppermute x1 -> x0, starting transfers between devices: 3.57 us -> none  [body(): near_rows = lax.ppermute(same_rows, 'dp', near_pairs)]
    unnamed x46 -> x54, local copies, waits for them, and re-layouts: 4.82 us -> 6.09 us
    ppermute x9 -> x7, waiting for transfers between devices: 3.98 us -> 4.76 us  [swap(): return lax.ppermute(values, 'dp', swap_pairs)]
  transfers between devices with their start and end apart: 16 -> 13, of which waited for: 9 -> 10; matrix products, arithmetic and copies ran while one was open for 3% -> 3% of each run, Pallas kernels for 3% -> 3%
where the time goes in v6:
time: 226 us; the launch traced here: 225 us
  waiting for transfers between devices  74.8 us (33%)
  starting transfers between devices  54.5 us (24%)
  blocking collectives  50.8 us (22%)
  Pallas kernels  18.2 us (8%)
  between operations  14.5 us (6%)
  local copies, waits for them, and re-layouts  6.09 us (3%)
  matrix products  5.09 us (2%)
    all_to_all x3, waiting for transfers between devices, exchange(): lax.all_to_all(chunks, 'expert', split_axis=0, concat_axis=0, tiled=True)  55.2 us
    all_to_all x3, starting transfers between devices, exchange(): lax.all_to_all(chunks, 'expert', split_axis=0, concat_axis=0, tiled=True)  35.2 us
    all_gather x1, blocking collectives, body(): lax.all_gather(grad_total, 'dp', axis=0, tiled=True, axis_index_groups=co...  28.2 us
    all_to_all x1, blocking collectives, body(): lax.all_to_all(joined, 'dp', split_axis=0, concat_axis=0, tiled=True, axi...  22.6 us
    ppermute x7, starting transfers between devices, swap(): return lax.ppermute(values, 'dp', swap_pairs)  14.2 us
    ppermute x1, waiting for transfers between devices, body(): lax.ppermute(leave, 'dp', near_pairs).astype(WIDE)  11.4 us
    unnamed x54, local copies, waits for them, and re-layouts  6.09 us
    dot_general x5, matrix products, outer(): lax.dot_general(left, right, (((0,), (0,)), ((), ())), preferred_element_...  5.09 us
  transfers between devices with their start and end apart: 13, of which 10 were waited for; matrix products, arithmetic and copies ran while one was open for 3% of the time, Pallas kernels for 3%

profile of v6, /device:TPU:4, one launch (start us, length us, event | category | flops | bytes accessed | tf_op | source)
XLA Modules:
  0.0 225.5 jit_solution(15768552717260855092)
XLA Ops:
  7.2 2.8 %token_rows.1 = (bf16[64,40,128]{2,1,0:T(8,128)(2,1)}, f32[64,128]{1,0:T(8,128)}, f32[64,128]{1,0:T(8,128)}) custom-call(s32[8,128]{1,0:T(8,128)} %bitcast.31, f32[8,128]{1,0:T(8,128)} %bitcast.32, s32[1,64]{1,0:T(1,128)} %bitcast.33, bf16[128,256]{1,0:T(8,128)(2,1)} %tokens_hbm.1), custom_call_target="tpu_custom_call" | custom-call | tf_op jit(solution)/shard_map/token_rows/pallas_call | solution.py:338
  10.0 0.0 copy-start.21
  10.0 0.0 copy-start.23
  10.1 17.3 %all-to-all-start = ((bf16[64,40,128]{2,1,0:T(8,128)(2,1)}), bf16[64,40,128]{2,1,0:T(8,128)(2,1)S(1)}, u32[]{:S(2)}, u32[]{:S(2)}) async-start(bf16[64,40,128]{2,1,0:T(8,128)(2,1)} %get-tuple-element.27), calls=%async_computation | async-start | bytes 1310720 | tf_op jit(solution)/shard_map/all_to_all | solution.py:321
  27.4 0.0 copy-start.9
  27.4 0.0 copy-start.10
  27.4 0.0 reduce-scatter.2.cloned.1.call-start
  27.5 1.2 pad_maximum_fusion.gu_ref
  28.7 1.9 collective-permute-start.1
  30.7 2.5 %grad_rows.1 = bf16[64,40,128]{2,1,0:T(8,128)(2,1)} custom-call(f32[64,128]{1,0:T(8,128)S(1)} %copy-done.21, f32[64,128]{1,0:T(8,128)S(1)} %copy-done.23, s32[1,128]{1,0:T(1,128)S(1)} %bitcast.30, bf16[128,256]{1,0:T(8,128)(2,1)S(1)} %copy-done.25), custom_call_target="tpu_custom_call" | custom-call | tf_op jit(solution)/shard_map/grad_rows/pallas_call | solution.py:352
  33.2 12.6 %all-to-all-done.chunks_ref = bf16[64,40,128]{2,1,0:T(8,128)(2,1)S(1)} async-done(((bf16[64,40,128]{2,1,0:T(8,128)(2,1)}), bf16[64,40,128]{2,1,0:T(8,128)(2,1)S(1)}, u32[]{:S(2)}, u32[]{:S(2)}) %all-to-all-start) | async-done | bytes 655392 | tf_op jit(solution)/shard_map/all_to_all | solution.py:321
  45.9 0.8 unpack.2
  46.6 1.9 collective-permute-start
  48.6 0.0 collective-permute-done.1.other_ref.gu_ref
  48.6 1.5 collective-permute-done.got_ref
  50.1 2.3 %gate_up.1 = bf16[576,1536]{1,0:T(8,128)(2,1)} custom-call(bf16[576,256]{1,0:T(8,128)(2,1)S(1)} %get-tuple-element.31.keep_ref, bf16[576,256]{1,0:T(8,128)(2,1)S(1)} %collective-permute-done.got_ref, bf16[256,768]{1,0:T(8,128)(2,1)S(1)} %bitcast.27, bf16[256,768]{1,0:T(8,128)(2,1)S(1)} %bitcast.29, bf16[256,1536]{1,0:T(8,128)(2,1)S(1)} %collective-permute-done.1.other_ref.gu_ref), custom_call_target="tpu_custom_call" | custom-call | tf_op jit(solution)/shard_map/gate_up/pallas_call | solution.py:360
  52.5 0.7 copy-done.2
  53.2 0.7 copy-done.19
  53.9 0.0 reduce-scatter.2.cloned.1.call-update
  53.9 5.6 %all-to-all-start.1 = ((bf16[64,40,128]{2,1,0:T(8,128)(2,1)}), bf16[64,40,128]{2,1,0:T(8,128)(2,1)S(1)}, u32[]{:S(2)}, u32[]{:S(2)}) async-start(bf16[64,40,128]{2,1,0:T(8,128)(2,1)} %grad_rows.1), calls=%async_computation.2 | async-start | bytes 1310720 | tf_op jit(solution)/shard_map/all_to_all | solution.py:321
  59.6 0.0 all-gather.2.cloned.1.call-start
  59.6 1.9 collective-permute-start.3
  61.6 20.5 %all-to-all-done.1.chunks_ref = bf16[64,40,128]{2,1,0:T(8,128)(2,1)S(1)} async-done(((bf16[64,40,128]{2,1,0:T(8,128)(2,1)}), bf16[64,40,128]{2,1,0:T(8,128)(2,1)S(1)}, u32[]{:S(2)}, u32[]{:S(2)}) %all-to-all-start.1) | async-done | bytes 655392 | tf_op jit(solution)/shard_map/all_to_all | solution.py:321
  82.1 0.8 unpack.3
  82.8 1.9 collective-permute-start.2
  84.8 0.0 collective-permute-done.3.other_ref.down_ref
  84.8 0.0 copy-start.7
  84.8 1.5 collective-permute-done.2.got_ref
  86.3 0.7 hidden_grad.1
  87.0 4.9 %collective-permute-start.4 = (bf16[4,72,768]{2,1,0:T(8,128)(2,1)S(1)}, bf16[4,72,768]{2,1,0:T(8,128)(2,1)S(1)}, u32[]{:S(2)}, u32[]{:S(2)}) collective-permute-start(bf16[4,72,768]{2,1,0:T(8,128)(2,1)S(1)} %get-tuple-element.39), channel_id=1, source_target_pairs={{0,128},{64,960},{128,0},{192,320},{256,384},{320,192},{384,256},{... | collective-permute-start | bytes 1327112 | tf_op jit(solution)/shard_map/ppermute | solution.py:379
  91.9 11.4 %collective-permute-done.4 = bf16[4,72,768]{2,1,0:T(8,128)(2,1)S(1)} collective-permute-done((bf16[4,72,768]{2,1,0:T(8,128)(2,1)S(1)}, bf16[4,72,768]{2,1,0:T(8,128)(2,1)S(1)}, u32[]{:S(2)}, u32[]{:S(2)}) %collective-permute-start.4) | collective-permute-done | bytes 442400 | tf_op jit(solution)/shard_map/ppermute | solution.py:379
  103.4 0.1 add_convert_fusion
  103.5 2.0 reduce-scatter.2.cloned.1.call-done
  105.5 0.0 all-gather.2.cloned.1.call-update
  105.5 22.6 %all_to_all.20.parts_ref = bf16[4,72,768]{2,1,0:T(8,128)(2,1)S(1)} all-to-all(bf16[4,72,768]{2,1,0:T(8,128)(2,1)S(1)} %add_convert_fusion), channel_id=1, replica_groups={{0,256,512,768},{128,384,640,896},{64,320,576,832},{192,448,704,960},{1..., dimensions={0} | all-to-all | bytes 884736 | tf_op jit(solution)/shard_map/all_to_all | solution.py:382
  128.2 0.1 total.1
  128.2 28.2 %all_gather.7.grad_ref = bf16[576,768]{1,0:T(8,128)(2,1)S(1)} all-gather(bf16[72,768]{1,0:T(8,128)(2,1)S(1)} %total.1), channel_id=1, replica_groups={{0,128,256,384,512,640,768,896},{64,192,320,448,576,704,832,960},{1,129..., dimensions={0}, use_global_device_ids=true | all-gather | bytes 995328 | tf_op jit(solution)/shard_map/all_gather | solution.py:391
  156.4 1.3 all-gather.2.cloned.1.call-done.shares_ref
  157.7 1.1 copy-done.1
  158.9 1.5 copy-done.4
  160.3 1.0 copy-done.8
  161.3 1.4 give_rows.1
  162.8 2.1 collective-permute-start.5
  164.9 0.9 mine_rows.1.mine_ref
  165.8 0.9 collective-permute-done.5.got_ref
  166.7 2.9 %pack.1 = bf16[64,72,128]{2,1,0:T(8,128)(2,1)} custom-call(s32[1]{0:T(128)} %bitcast.core_ref, bf16[1152,256]{1,0:T(8,128)(2,1)S(1)} %mine_rows.1.mine_ref, bf16[1152,256]{1,0:T(8,128)(2,1)S(1)} %collective-permute-done.5.got_ref), custom_call_target="tpu_custom_call" | custom-call | tf_op jit(solution)/shard_map/pack/pallas_call | solution.py:410
  169.6 12.2 %all-to-all-start.3 = ((bf16[64,72,128]{2,1,0:T(8,128)(2,1)}), bf16[64,72,128]{2,1,0:T(8,128)(2,1)S(1)}, u32[]{:S(2)}, u32[]{:S(2)}) async-start(bf16[64,72,128]{2,1,0:T(8,128)(2,1)} %pack.1), calls=%async_computation.4 | async-start | bytes 2359296 | tf_op jit(solution)/shard_map/all_to_all | solution.py:321
  181.8 0.8 convolution_convert_fusion
  182.6 0.0 copy-start.22
  182.6 0.0 copy-start.24
  182.7 2.1 collective-permute-start.6
  184.7 0.5 convolution_convert_fusion.1
  185.3 2.4 %collective-permute-start.7 = (bf16[768,256]{1,0:T(8,128)(2,1)S(1)}, bf16[768,256]{1,0:T(8,128)(2,1)S(1)}, u32[]{:S(2)}, u32[]{:S(2)}) collective-permute-start(bf16[768,256]{1,0:T(8,128)(2,1)S(1)} %convolution_convert_fusion.1), channel_id=1, source_target_pairs={{0,64},{64,0},{128,192},{192,128},{256,320},{320,256},{384,448},{4... | collective-permute-start | bytes 1179656 | tf_op jit(solution)/shard_map/ppermute | solution.py:318
  187.7 0.5 tables.1
  188.2 0.0 copy-start.3
  188.2 0.8 collective-permute-done.7
  189.0 1.3 fusion.3
  190.3 0.0 collective-permute-done.6
  190.3 0.2 convert_element_type.34
  190.5 1.3 fusion.4
  191.7 1.3 fusion.5
  193.0 22.1 %all-to-all-done.3.chunks_ref = bf16[64,72,128]{2,1,0:T(8,128)(2,1)S(1)} async-done(((bf16[64,72,128]{2,1,0:T(8,128)(2,1)}), bf16[64,72,128]{2,1,0:T(8,128)(2,1)S(1)}, u32[]{:S(2)}, u32[]{:S(2)}) %all-to-all-start.3) | async-done | bytes 1179680 | tf_op jit(solution)/shard_map/all_to_all | solution.py:321
  215.1 1.0 copy-done.18
  216.0 2.6 %merge.1 = (bf16[128,256]{1,0:T(8,128)(2,1)}, bf16[128,256]{1,0:T(8,128)(2,1)}) custom-call(bf16[64,72,128]{2,1,0:T(8,128)(2,1)S(1)} %all-to-all-done.3.chunks_ref, bf16[128,1152]{1,0:T(8,128)(2,1)S(1)} %copy-done.18, bf16[256,1152]{1,0:T(8,128)(2,1)S(1)} %get-tuple-element.46.weight_ref), custom_call_target="tpu_custom_call" | custom-call | tf_op jit(solution)/shard_map/merge/pallas_call | solution.py:435
  (40 shorter events, 0.1 us)
Async XLA Ops:
  7.2 23.5 %copy-start.26 = (s32[128]{0:T(128)S(1)}, s32[128]{0:T(128)}, u32[]{:S(2)}) copy-start(s32[128]{0:T(128)} %param.12) | copy-start | bytes 1540
  7.2 23.5 %copy-start.25 = (bf16[128,256]{1,0:T(8,128)(2,1)S(1)}, bf16[128,256]{1,0:T(8,128)(2,1)}, u32[]{:S(2)}) copy-start(bf16[128,256]{1,0:T(8,128)(2,1)} %cot_ref.1) | copy-start | bytes 196612
  10.0 20.6 %copy-start.21 = (f32[64,128]{1,0:T(8,128)S(1)}, f32[64,128]{1,0:T(8,128)}, u32[]{:S(2)}) copy-start(f32[64,128]{1,0:T(8,128)} %get-tuple-element.28.rank_ref) | copy-start | bytes 98308
  10.0 20.6 %copy-start.23 = (f32[64,128]{1,0:T(8,128)S(1)}, f32[64,128]{1,0:T(8,128)}, u32[]{:S(2)}) copy-start(f32[64,128]{1,0:T(8,128)} %get-tuple-element.29.weight_ref) | copy-start | bytes 98308
  10.1 35.8 %all-to-all-start = ((bf16[64,40,128]{2,1,0:T(8,128)(2,1)}), bf16[64,40,128]{2,1,0:T(8,128)(2,1)S(1)}, u32[]{:S(2)}, u32[]{:S(2)}) async-start(bf16[64,40,128]{2,1,0:T(8,128)(2,1)} %get-tuple-element.27), calls=%async_computation | async-start | bytes 1310720 | tf_op jit(solution)/shard_map/all_to_all | solution.py:321
  27.4 22.7 %copy-start.9 = (bf16[1,256,768]{2,1,0:T(8,128)(2,1)S(1)}, bf16[1,256,768]{2,1,0:T(8,128)(2,1)}, u32[]{:S(2)}) copy-start(bf16[1,256,768]{2,1,0:T(8,128)(2,1)} %param.15) | copy-start | bytes 1179652
  27.4 22.7 %copy-start.10 = (bf16[1,256,768]{2,1,0:T(8,128)(2,1)S(1)}, bf16[1,256,768]{2,1,0:T(8,128)(2,1)}, u32[]{:S(2)}) copy-start(bf16[1,256,768]{2,1,0:T(8,128)(2,1)} %param.16) | copy-start | bytes 1179652
  27.4 78.1 %reduce-scatter.2.cloned.1.call-start = ((), (), s32[]{:S(2)}) async-start(), calls=%async_computation.5 | async-start | bytes 1990656 | tf_op jit(solution)/shard_map/reduce_scatter | solution.py:367
  28.7 19.9 %collective-permute-start.1 = (bf16[256,1536]{1,0:T(8,128)(2,1)S(1)}, bf16[256,1536]{1,0:T(8,128)(2,1)S(1)}, u32[]{:S(2)}, u32[]{:S(2)}) collective-permute-start(bf16[256,1536]{1,0:T(8,128)(2,1)S(1)} %pad_maximum_fusion.gu_ref), channel_id=1, source_target_pairs={{0,64},{64,0},{128,192},{192,128},{256,320},{320,256},{384,448},{4... | collective-permute-start | bytes 2359304 | tf_op jit(solution)/shard_map/ppermute | solution.py:318
  46.6 3.5 %collective-permute-start = (bf16[576,256]{1,0:T(8,128)(2,1)S(1)}, bf16[576,256]{1,0:T(8,128)(2,1)S(1)}, u32[]{:S(2)}, u32[]{:S(2)}) collective-permute-start(bf16[576,256]{1,0:T(8,128)(2,1)S(1)} %get-tuple-element.32), channel_id=1, source_target_pairs={{0,64},{64,0},{128,192},{192,128},{256,320},{320,256},{384,448},{4... | collective-permute-start | bytes 884744 | tf_op jit(solution)/shard_map/ppermute | solution.py:318
  48.6 3.9 %copy-start = (bf16[256,1536]{1,0:T(8,128)(2,1)}, bf16[256,1536]{1,0:T(8,128)(2,1)S(1)}, u32[]{:S(2)}) copy-start(bf16[256,1536]{1,0:T(8,128)(2,1)S(1)} %collective-permute-done.1.other_ref.gu_ref) | copy-start | bytes 2359300
  52.5 0.7 copy-start.2
  53.2 0.7 copy-start.19
  53.9 5.7 %copy-start.5 = (bf16[1,768,256]{2,1,0:T(8,128)(2,1)S(1)}, bf16[1,768,256]{2,1,0:T(8,128)(2,1)}, u32[]{:S(2)}) copy-start(bf16[1,768,256]{2,1,0:T(8,128)(2,1)} %param.17) | copy-start | bytes 1179652
  53.9 28.1 %all-to-all-start.1 = ((bf16[64,40,128]{2,1,0:T(8,128)(2,1)}), bf16[64,40,128]{2,1,0:T(8,128)(2,1)S(1)}, u32[]{:S(2)}, u32[]{:S(2)}) async-start(bf16[64,40,128]{2,1,0:T(8,128)(2,1)} %grad_rows.1), calls=%async_computation.2 | async-start | bytes 1310720 | tf_op jit(solution)/shard_map/all_to_all | solution.py:321
  59.6 98.2 %all-gather.2.cloned.1.call-start = ((), (), s32[]{:S(2)}) async-start(), calls=%async_computation.6 | async-start | bytes 1990656 | tf_op jit(solution)/shard_map/all_gather | solution.py:381
  59.6 25.2 %collective-permute-start.3 = (bf16[768,256]{1,0:T(8,128)(2,1)S(1)}, bf16[768,256]{1,0:T(8,128)(2,1)S(1)}, u32[]{:S(2)}, u32[]{:S(2)}) collective-permute-start(bf16[768,256]{1,0:T(8,128)(2,1)S(1)} %bitcast.23), channel_id=1, source_target_pairs={{0,64},{64,0},{128,192},{192,128},{256,320},{320,256},{384,448},{4... | collective-permute-start | bytes 1179656 | tf_op jit(solution)/shard_map/ppermute | solution.py:318
  82.8 45.3 %copy-start.13 = (bf16[576,256]{1,0:T(8,128)(2,1)}, bf16[576,256]{1,0:T(8,128)(2,1)S(1)}, u32[]{:S(2)}) copy-start(bf16[576,256]{1,0:T(8,128)(2,1)S(1)} %get-tuple-element.36.keep_ref) | copy-start | bytes 884740
  82.8 3.5 %collective-permute-start.2 = (bf16[576,256]{1,0:T(8,128)(2,1)S(1)}, bf16[576,256]{1,0:T(8,128)(2,1)S(1)}, u32[]{:S(2)}, u32[]{:S(2)}) collective-permute-start(bf16[576,256]{1,0:T(8,128)(2,1)S(1)} %get-tuple-element.37), channel_id=1, source_target_pairs={{0,64},{64,0},{128,192},{192,128},{256,320},{320,256},{384,448},{4... | collective-permute-start | bytes 884744 | tf_op jit(solution)/shard_map/ppermute | solution.py:318
  84.8 43.4 %copy-start.7 = (bf16[768,256]{1,0:T(8,128)(2,1)}, bf16[768,256]{1,0:T(8,128)(2,1)S(1)}, u32[]{:S(2)}) copy-start(bf16[768,256]{1,0:T(8,128)(2,1)S(1)} %collective-permute-done.3.other_ref.down_ref) | copy-start | bytes 1179652
  86.3 41.9 %copy-start.15 = (bf16[576,256]{1,0:T(8,128)(2,1)}, bf16[576,256]{1,0:T(8,128)(2,1)S(1)}, u32[]{:S(2)}) copy-start(bf16[576,256]{1,0:T(8,128)(2,1)S(1)} %collective-permute-done.2.got_ref) | copy-start | bytes 884740
  87.0 16.4 %collective-permute-start.4 = (bf16[4,72,768]{2,1,0:T(8,128)(2,1)S(1)}, bf16[4,72,768]{2,1,0:T(8,128)(2,1)S(1)}, u32[]{:S(2)}, u32[]{:S(2)}) collective-permute-start(bf16[4,72,768]{2,1,0:T(8,128)(2,1)S(1)} %get-tuple-element.39), channel_id=1, source_target_pairs={{0,128},{64,960},{128,0},{192,320},{256,384},{320,192},{384,256},{... | collective-permute-start | bytes 1327112 | tf_op jit(solution)/shard_map/ppermute | solution.py:379
  157.7 1.1 copy-start.1
  158.9 1.5 copy-start.4
  160.3 1.0 copy-start.8
  161.3 3.6 %copy-start.6 = (bf16[1,768,256]{2,1,0:T(8,128)(2,1)S(1)}, bf16[1,768,256]{2,1,0:T(8,128)(2,1)}, u32[]{:S(2)}) copy-start(bf16[1,768,256]{2,1,0:T(8,128)(2,1)} %param.17) | copy-start | bytes 1179652
  162.8 3.0 %copy-start.11 = (bf16[576,768]{1,0:T(8,128)(2,1)}, bf16[576,768]{1,0:T(8,128)(2,1)S(1)}, u32[]{:S(2)}) copy-start(bf16[576,768]{1,0:T(8,128)(2,1)S(1)} %get-tuple-element.42.hidden_ref) | copy-start | bytes 2654212
  162.8 3.9 %collective-permute-start.5 = (bf16[1152,256]{1,0:T(8,128)(2,1)S(1)}, bf16[1152,256]{1,0:T(8,128)(2,1)S(1)}, u32[]{:S(2)}, u32[]{:S(2)}) collective-permute-start(bf16[1152,256]{1,0:T(8,128)(2,1)S(1)} %get-tuple-element.44), channel_id=1, source_target_pairs={{0,64},{64,0},{128,192},{192,128},{256,320},{320,256},{384,448},{4... | collective-permute-start | bytes 1769480 | tf_op jit(solution)/shard_map/ppermute | solution.py:318
  169.6 12.2 %copy-start.20 = (bf16[576,256]{1,0:T(8,128)(2,1)S(1)}, bf16[576,256]{1,0:T(8,128)(2,1)}, u32[]{:S(2)}) copy-start(bf16[576,256]{1,0:T(8,128)(2,1)} %copy-done.19) | copy-start | bytes 884740
  169.6 45.5 %all-to-all-start.3 = ((bf16[64,72,128]{2,1,0:T(8,128)(2,1)}), bf16[64,72,128]{2,1,0:T(8,128)(2,1)S(1)}, u32[]{:S(2)}, u32[]{:S(2)}) async-start(bf16[64,72,128]{2,1,0:T(8,128)(2,1)} %pack.1), calls=%async_computation.4 | async-start | bytes 2359296 | tf_op jit(solution)/shard_map/all_to_all | solution.py:321
  181.8 2.9 %copy-start.12 = (bf16[576,768]{1,0:T(8,128)(2,1)S(1)}, bf16[576,768]{1,0:T(8,128)(2,1)}, u32[]{:S(2)}) copy-start(bf16[576,768]{1,0:T(8,128)(2,1)} %copy-done.11) | copy-start | bytes 2654212
  181.8 2.9 %copy-start.16 = (bf16[576,256]{1,0:T(8,128)(2,1)S(1)}, bf16[576,256]{1,0:T(8,128)(2,1)}, u32[]{:S(2)}) copy-start(bf16[576,256]{1,0:T(8,128)(2,1)} %copy-done.15) | copy-start | bytes 884740
  182.6 5.1 %copy-start.22 = (f32[64,128]{1,0:T(8,128)S(1)}, f32[64,128]{1,0:T(8,128)}, u32[]{:S(2)}) copy-start(f32[64,128]{1,0:T(8,128)} %get-tuple-element.28.rank_ref) | copy-start | bytes 98308
  182.6 5.1 %copy-start.24 = (f32[64,128]{1,0:T(8,128)S(1)}, f32[64,128]{1,0:T(8,128)}, u32[]{:S(2)}) copy-start(f32[64,128]{1,0:T(8,128)} %get-tuple-element.29.weight_ref) | copy-start | bytes 98308
  182.6 6.4 %copy-start.14 = (bf16[576,256]{1,0:T(8,128)(2,1)S(1)}, bf16[576,256]{1,0:T(8,128)(2,1)}, u32[]{:S(2)}) copy-start(bf16[576,256]{1,0:T(8,128)(2,1)} %copy-done.13) | copy-start | bytes 884740
  182.7 7.6 %collective-permute-start.6 = (bf16[256,1536]{1,0:T(8,128)(2,1)S(1)}, bf16[256,1536]{1,0:T(8,128)(2,1)S(1)}, u32[]{:S(2)}, u32[]{:S(2)}) collective-permute-start(bf16[256,1536]{1,0:T(8,128)(2,1)S(1)} %convolution_convert_fusion), channel_id=1, source_target_pairs={{0,64},{64,0},{128,192},{192,128},{256,320},{320,256},{384,448},{4... | collective-permute-start | bytes 2359304 | tf_op jit(solution)/shard_map/ppermute | solution.py:318
  185.3 3.7 %collective-permute-start.7 = (bf16[768,256]{1,0:T(8,128)(2,1)S(1)}, bf16[768,256]{1,0:T(8,128)(2,1)S(1)}, u32[]{:S(2)}, u32[]{:S(2)}) collective-permute-start(bf16[768,256]{1,0:T(8,128)(2,1)S(1)} %convolution_convert_fusion.1), channel_id=1, source_target_pairs={{0,64},{64,0},{128,192},{192,128},{256,320},{320,256},{384,448},{4... | collective-permute-start | bytes 1179656 | tf_op jit(solution)/shard_map/ppermute | solution.py:318
  188.2 2.3 %copy-start.17 = (bf16[128,1152]{1,0:T(8,128)(2,1)}, bf16[128,1152]{1,0:T(8,128)(2,1)S(1)}, u32[]{:S(2)}) copy-start(bf16[128,1152]{1,0:T(8,128)(2,1)S(1)} %get-tuple-element.45.pick_ref) | copy-start | bytes 884740
  188.2 2.3 %copy-start.3 = (bf16[576,256]{1,0:T(8,128)(2,1)S(1)}, bf16[576,256]{1,0:T(8,128)(2,1)}, u32[]{:S(2)}) copy-start(bf16[576,256]{1,0:T(8,128)(2,1)} %copy-done.2) | copy-start | bytes 884740
  215.1 1.0 copy-start.18
Sparse Core Ops, SparseCore 0:
  54.0 51.4 reduce-scatter.1
  108.2 49.5 all-gather.1

commit v7 on v6

--- a/solution.py
+++ b/solution.py
@@ -140,15 +140,15 @@
     cot_out[...] = mul(coefs, sides).reshape(experts, chunk, lanes).astype(LOW)
 
 
-def table_kernel(capacity, rank_ref, weight_ref, pick_out, weight_out):
+def table_kernel(capacity, rank_ref, weight_ref, table_out):
     experts, tok_rows = rank_ref.shape
     slots = experts * capacity
     owner = owners((experts, slots), 1, capacity)
     place = remainder(number((1, slots), 1), capacity)
     picked = mul(rank_ref[...].T.astype(LOW), owner) == place
-    pick_out[...] = low_if(picked)
+    table_out[0:tok_rows, :] = low_if(picked)
     for at, part in enumerate(split_low(weight_ref[...].T)):
-        weight_out[at * tok_rows : (at + 1) * tok_rows, :] = jnp.where(
+        table_out[(at + 1) * tok_rows : (at + 2) * tok_rows, :] = jnp.where(
             picked, mul(part, owner), 0.0
         ).astype(LOW)
 
@@ -196,45 +196,88 @@
     moves = places(GROUP, capacity, False)
     core = core_ref[0]
     for in_ref, base in ((mine_ref, core * half), (got_ref, (1 - core) * half)):
-        for at in range(half // GROUP):
+        for at in range(0, half // GROUP, 2):
             stacked = jnp.concatenate(
                 [
-                    in_ref[first + at * rows : first + (at + 1) * rows, cols]
+                    jnp.concatenate(
+                        [
+                            in_ref[first + now * rows : first + (now + 1) * rows, cols]
+                            for now in (at, at + 1)
+                        ],
+                        axis=1,
+                    )
                     for first in (0, half * capacity)
                     for cols in (slice(0, lanes), slice(lanes, 2 * lanes))
                 ],
                 axis=0,
             )
-            chunks_out[pl.ds(base + at * GROUP, GROUP)] = (
-                mul(moves, stacked).reshape(GROUP, 4 * capacity, lanes).astype(LOW)
-            )
+            moved = mul(moves, stacked)
+            for side in range(2):
+                chunks_out[pl.ds(base + (at + side) * GROUP, GROUP)] = (
+                    moved[:, side * lanes : (side + 1) * lanes]
+                    .reshape(GROUP, 4 * capacity, lanes)
+                    .astype(LOW)
+                )
 
 
 def merge_kernel(
-    capacity, chunks_ref, pick_ref, weight_ref, layer_out, token_out, out_rows, grad_rows
+    capacity,
+    chunks_ref,
+    table_ref,
+    layer_out,
+    token_out,
+    out_rows,
+    grad_rows,
 ):
     experts, _, lanes = chunks_ref.shape
     tok_rows = layer_out.shape[0]
     rows = GROUP * capacity
     moves = places(GROUP, capacity, True)
-    for at in range(experts // GROUP):
-        chunk = chunks_ref[at * GROUP : (at + 1) * GROUP].reshape(4 * rows, lanes)
-        pieces = mul(moves, chunk).astype(LOW)
+    for at in range(0, experts // GROUP, 2):
+        chunks = [
+            chunks_ref[now * GROUP : (now + 1) * GROUP].reshape(4 * rows, lanes)
+            for now in (at, at + 1)
+        ]
+        pieces = mul(moves, jnp.concatenate(chunks, axis=1)).astype(LOW)
         for piece in range(4):
             target = (out_rows, grad_rows)[piece // 2]
             cols = slice(piece % 2 * lanes, (piece % 2 + 1) * lanes)
-            target[at * rows : (at + 1) * rows, cols] = pieces[piece * rows : (piece + 1) * rows]
-    sums = mul(weight_ref[...], out_rows[...])
+            for side in range(2):
+                first = (at + side) * rows
+                target[first : first + rows, cols] = pieces[
+                    piece * rows : (piece + 1) * rows, side * lanes : (side + 1) * lanes
+                ]
+    sums = mul(table_ref[tok_rows:, :], out_rows[...])
     layer_out[...] = (sums[:tok_rows] + sums[tok_rows:]).astype(LOW)
-    token_out[...] = mul(pick_ref[...], grad_rows[...]).astype(LOW)
-
-
-def gate_up_kernel(keep_ref, got_ref, gate_ref, up_ref, other_ref, out_ref):
+    token_out[...] = mul(table_ref[0:tok_rows, :], grad_rows[...]).astype(LOW)
+
+
+def gate_up_kernel(
+    keep_ref,
+    got_ref,
+    gate_ref,
+    up_ref,
+    other_ref,
+    out_hbm,
+    out_ref,
+    sems,
+):
     ff = gate_ref.shape[1]
+    step = ff // 3
+    copies = []
     keep, got = keep_ref[...], got_ref[...]
-    for at, own_ref in enumerate((gate_ref, up_ref)):
-        cols = slice(at * ff, (at + 1) * ff)
-        out_ref[:, cols] = (mul(keep, own_ref[...]) + mul(got, other_ref[:, cols])).astype(LOW)
+    for at in range(6):
+        own_ref = (gate_ref, up_ref)[at // 3]
+        cols = slice(at * step, (at + 1) * step)
+        own_cols = slice(at % 3 * step, (at % 3 + 1) * step)
+        out_ref[:, cols] = (mul(keep, own_ref[:, own_cols]) + mul(got, other_ref[:, cols])).astype(
+            LOW
+        )
+        copy = pltpu.make_async_copy(out_ref.at[:, cols], out_hbm.at[:, cols], sems.at[at])
+        copy.start()
+        copies.append(copy)
+    for copy in copies:
+        copy.wait()
 
 
 def hidden_grad_kernel(parity_ref, keep_ref, got_ref, own_ref, other_ref, stay_out, leave_out):
@@ -255,13 +298,46 @@
     out_ref[...] = total.astype(LOW)
 
 
-def give_kernel(
-    shares_ref, grad_ref, gu_ref, down_ref, hidden_out, derived_out, give_out
+def rows_kernel(
+    shares_hbm,
+    grad_hbm,
+    gu_hbm,
+    down_hbm,
+    gu_own_hbm,
+    down_own_hbm,
+    hidden_out,
+    derived_out,
+    give_out,
+    mine_out,
+    shares_ref,
+    grad_ref,
+    gu_ref,
+    down_ref,
+    gu_own_ref,
+    down_own_ref,
+    sems,
 ):
     half, ff = grad_ref.shape
-    step = GROUP * (half // 4 // GROUP)
-    for start in range(0, half, step):
-        rows = slice(start, start + step)
+    step = half // 4
+    blocks = [slice(at * step, (at + 1) * step) for at in range(4)]
+    loads = [
+        (
+            pltpu.make_async_copy(grad_hbm.at[rows], grad_ref.at[rows], sems.at[6 + at]),
+            pltpu.make_async_copy(shares_hbm.at[rows], shares_ref.at[rows], sems.at[at]),
+        )
+        for at, rows in enumerate(blocks)
+    ]
+    weights = [
+        pltpu.make_async_copy(down_hbm, down_ref, sems.at[4]),
+        pltpu.make_async_copy(gu_hbm, gu_ref, sems.at[5]),
+        pltpu.make_async_copy(down_own_hbm, down_own_ref, sems.at[10]),
+        pltpu.make_async_copy(gu_own_hbm, gu_own_ref, sems.at[11]),
+    ]
+    for copy in [copy for load in loads for copy in load] + weights:
+        copy.start()
+    for rows, load in zip(blocks, loads):
+        for copy in load:
+            copy.wait()
         gate_val = shares_ref[rows, :ff].astype(WIDE)
         up_val = shares_ref[rows, ff:].astype(WIDE)
         grad_hidden = grad_ref[rows, :].astype(WIDE)
@@ -269,14 +345,14 @@
         hidden_out[rows, :] = (active * up_val).astype(LOW)
         derived_out[rows, :ff] = (grad_hidden * up_val * slope).astype(LOW)
         derived_out[rows, ff:] = (grad_hidden * active).astype(LOW)
-    give_out[:half, :] = mul(hidden_out[...], down_ref[...]).astype(LOW)
-    give_out[half:, :] = against(derived_out[...], gu_ref[...]).astype(LOW)
-
-
-def mine_kernel(hidden_ref, derived_ref, gu_ref, down_ref, mine_out):
-    half = hidden_ref.shape[0]
-    mine_out[:half, :] = mul(hidden_ref[...], down_ref[...]).astype(LOW)
-    mine_out[half:, :] = against(derived_ref[...], gu_ref[...]).astype(LOW)
+    for copy in weights:
+        copy.wait()
+    for out_ref, lower_ref, upper_ref in (
+        (give_out, down_ref, gu_ref),
+        (mine_out, down_own_ref, gu_own_ref),
+    ):
+        out_ref[:half, :] = mul(hidden_out[...], lower_ref[...]).astype(LOW)
+        out_ref[half:, :] = against(derived_out[...], upper_ref[...]).astype(LOW)
 
 
 def body(
@@ -311,8 +387,9 @@
     tok_shape = jax.ShapeDtypeStruct((tok_rows, width), LOW)
     in_smem = pl.BlockSpec(memory_space=pltpu.SMEM)
     in_vmem = pl.BlockSpec(memory_space=pltpu.VMEM)
+    in_hbm = pl.BlockSpec(memory_space=pltpu.HBM)
     anywhere = pl.BlockSpec(memory_space=pl.ANY)
-    params = pltpu.CompilerParams(vmem_limit_bytes=40 * 1024 * 1024)
+    params = pltpu.CompilerParams(vmem_limit_bytes=16 * 1024 * 1024)
 
     def swap(values):
         return lax.ppermute(values, "dp", swap_pairs)
@@ -360,6 +437,9 @@
     gate_up = pl.pallas_call(
         gate_up_kernel,
         out_shape=jax.ShapeDtypeStruct((half, 2 * ff), LOW),
+        in_specs=[in_vmem] * 5,
+        out_specs=in_hbm,
+        scratch_shapes=[pltpu.VMEM((half, 2 * ff), LOW), pltpu.SemaphoreType.DMA((6,))],
         compiler_params=params,
         name="gate_up",
     )(token_keep, token_got, gate_own, up_own, gu_other)
@@ -376,8 +456,8 @@
         compiler_params=params,
         name="hidden_grad",
     )(parity, grad_keep, grad_got, down_own, down_other)
-    joined = (stay.astype(WIDE) + lax.ppermute(leave, "dp", near_pairs).astype(WIDE)).astype(LOW)
-    shares, joined = lax.optimization_barrier((shares, joined))
+    shares, near = lax.optimization_barrier((shares, lax.ppermute(leave, "dp", near_pairs)))
+    joined = (stay.astype(WIDE) + near.astype(WIDE)).astype(LOW)
     shares_full = lax.all_gather(shares, "dp", axis=0, tiled=True, axis_index_groups=column)
     grad_parts = lax.all_to_all(
         joined, "dp", split_axis=0, concat_axis=0, tiled=True, axis_index_groups=alike
@@ -390,22 +470,27 @@
     )(grad_parts)
     grad_full = lax.all_gather(grad_total, "dp", axis=0, tiled=True, axis_index_groups=column)
     pair_shape = jax.ShapeDtypeStruct((2 * half, width), LOW)
-    hidden_full, derived_full, give = pl.pallas_call(
-        give_kernel,
+    hidden_full, derived_full, give, mine = pl.pallas_call(
+        rows_kernel,
         out_shape=(
             jax.ShapeDtypeStruct((half, ff), LOW),
             jax.ShapeDtypeStruct((half, 2 * ff), LOW),
             pair_shape,
+            pair_shape,
         ),
-        compiler_params=params,
-        name="give_rows",
-    )(shares_full, grad_full, gu_other, down_other)
-    mine = pl.pallas_call(
-        mine_kernel,
-        out_shape=pair_shape,
-        compiler_params=params,
-        name="mine_rows",
-    )(hidden_full, derived_full, gu_own, down_own)
+        in_specs=[anywhere] * 6,
+        scratch_shapes=[
+            pltpu.VMEM((half, 2 * ff), LOW),
+            pltpu.VMEM((half, ff), LOW),
+            pltpu.VMEM((width, 2 * ff), LOW),
+            pltpu.VMEM((ff, width), LOW),
+            pltpu.VMEM((width, 2 * ff), LOW),
+            pltpu.VMEM((ff, width), LOW),
+            pltpu.SemaphoreType.DMA((12,)),
+        ],
+        compiler_params=pltpu.CompilerParams(vmem_limit_bytes=63 * 1024 * 1024),
+        name="expert_rows",
+    )(shares_full, grad_full, gu_other, down_other, gu_own, down_own)
     back = exchange(
         pl.pallas_call(
             functools.partial(pack_kernel, capacity),
@@ -422,14 +507,11 @@
     gate_grads = (outer(token_keep, derived_full[:, :ff]) + upper_got[:, :ff]).astype(LOW)
     up_grads = (outer(token_keep, derived_full[:, ff:]) + upper_got[:, ff:]).astype(LOW)
 
-    picks, weights = pl.pallas_call(
+    table = pl.pallas_call(
         functools.partial(table_kernel, capacity),
-        out_shape=(
-            jax.ShapeDtypeStruct((tok_rows, slots), LOW),
-            jax.ShapeDtypeStruct((2 * tok_rows, slots), LOW),
-        ),
+        out_shape=jax.ShapeDtypeStruct((3 * tok_rows, slots), LOW),
         compiler_params=params,
-        name="tables",
+        name="table",
     )(rank, weight)
     rows_scratch = pltpu.VMEM((slots, width), LOW)
     layer_out, token_grads = pl.pallas_call(
@@ -438,7 +520,7 @@
         scratch_shapes=[rows_scratch, rows_scratch],
         compiler_params=params,
         name="merge",
-    )(back, picks, weights)
+    )(back, table)
     return (layer_out, token_grads, gate_grads[None], up_grads[None], down_grads[None])
 
 

time: 226 us -> 226 us (level)
  local copies, waits for them, and re-layouts: 6.09 us -> 2.57 us
    unnamed x54 -> x38, local copies, waits for them, and re-layouts: 6.09 us -> 2.57 us
    pallas_call x3 -> x2, Pallas kernels: 2.76 us -> 5.65 us  [the longest x1 5.19 us: body(): pl.pallas_call(rows_kernel, out_shape=(jax.ShapeDtypeStruct((half, ff), L...]
  transfers between devices with their start and end apart: 13 -> 13, of which waited for: 10 -> 9; matrix products, arithmetic and copies ran while one was open for 3% -> 4% of each run, Pallas kernels for 3% -> 2%
where the time goes in v7:
time: 226 us; the launch traced here: 225 us
  waiting for transfers between devices  73.4 us (32%)
  starting transfers between devices  54 us (24%)
  blocking collectives  52.5 us (23%)
  Pallas kernels  19.6 us (9%)
  between operations  14.5 us (6%)
  matrix products  6.64 us (3%)
  local copies, waits for them, and re-layouts  2.57 us (1%)
    all_to_all x3, waiting for transfers between devices, exchange(): lax.all_to_all(chunks, 'expert', split_axis=0, concat_axis=0, tiled=True)  53.8 us
    all_to_all x3, starting transfers between devices, exchange(): lax.all_to_all(chunks, 'expert', split_axis=0, concat_axis=0, tiled=True)  35.1 us
    all_gather x1, blocking collectives, body(): lax.all_gather(grad_total, 'dp', axis=0, tiled=True, axis_index_groups=co...  30 us
    all_to_all x1, blocking collectives, body(): lax.all_to_all(joined, 'dp', split_axis=0, concat_axis=0, tiled=True, axi...  22.5 us
    ppermute x7, starting transfers between devices, swap(): return lax.ppermute(values, 'dp', swap_pairs)  13.9 us
    ppermute x1, waiting for transfers between devices, body(): lax.ppermute(leave, 'dp', near_pairs)  11.4 us
    dot_general x5, matrix products, outer(): lax.dot_general(left, right, (((0,), (0,)), ((), ())), preferred_element_...  6.64 us
    ppermute x7, waiting for transfers between devices, swap(): return lax.ppermute(values, 'dp', swap_pairs)  6.04 us
  transfers between devices with their start and end apart: 13, of which 9 were waited for; matrix products, arithmetic and copies ran while one was open for 4% of the time, Pallas kernels for 2%

profile of v7, /device:TPU:4, one launch (start us, length us, event | category | flops | bytes accessed | tf_op | source)
XLA Modules:
  0.0 224.8 jit_solution(18412069251506754406)
XLA Ops:
  7.2 2.8 %token_rows.1 = (bf16[64,40,128]{2,1,0:T(8,128)(2,1)}, f32[64,128]{1,0:T(8,128)}, f32[64,128]{1,0:T(8,128)}) custom-call(s32[8,128]{1,0:T(8,128)} %bitcast.31, f32[8,128]{1,0:T(8,128)} %bitcast.32, s32[1,64]{1,0:T(1,128)} %bitcast.33, bf16[128,256]{1,0:T(8,128)(2,1)} %tokens_hbm.1), custom_call_target="tpu_custom_call" | custom-call | tf_op jit(solution)/shard_map/token_rows/pallas_call | solution.py:415
  10.0 0.0 copy-start.10
  10.0 0.0 copy-start.12
  10.1 17.3 %all-to-all-start = ((bf16[64,40,128]{2,1,0:T(8,128)(2,1)}), bf16[64,40,128]{2,1,0:T(8,128)(2,1)S(1)}, u32[]{:S(2)}, u32[]{:S(2)}) async-start(bf16[64,40,128]{2,1,0:T(8,128)(2,1)} %get-tuple-element.26), calls=%async_computation | async-start | bytes 1310720 | tf_op jit(solution)/shard_map/all_to_all | solution.py:398
  27.4 0.0 copy-start.5
  27.4 0.0 copy-start.6
  27.4 0.0 reduce-scatter.2.cloned.1.call-start
  27.5 1.2 pad_maximum_fusion.gu_own_hbm
  28.7 1.9 collective-permute-start.1
  30.7 2.6 %grad_rows.1 = bf16[64,40,128]{2,1,0:T(8,128)(2,1)} custom-call(f32[64,128]{1,0:T(8,128)S(1)} %copy-done.10, f32[64,128]{1,0:T(8,128)S(1)} %copy-done.12, s32[1,128]{1,0:T(1,128)S(1)} %bitcast.30, bf16[128,256]{1,0:T(8,128)(2,1)S(1)} %copy-done.14), custom_call_target="tpu_custom_call" | custom-call | tf_op jit(solution)/shard_map/grad_rows/pallas_call | solution.py:429
  33.3 12.6 %all-to-all-done.chunks_ref = bf16[64,40,128]{2,1,0:T(8,128)(2,1)S(1)} async-done(((bf16[64,40,128]{2,1,0:T(8,128)(2,1)}), bf16[64,40,128]{2,1,0:T(8,128)(2,1)S(1)}, u32[]{:S(2)}, u32[]{:S(2)}) %all-to-all-start) | async-done | bytes 655392 | tf_op jit(solution)/shard_map/all_to_all | solution.py:398
  45.9 0.8 unpack.2
  46.6 1.9 collective-permute-start
  48.6 0.0 collective-permute-done.1.other_ref.gu_hbm
  48.6 1.5 collective-permute-done.got_ref
  50.1 0.0 copy-done.6
  50.1 2.1 gate_up.1
  52.3 0.0 copy-start.1
  52.3 0.7 copy-done.1
  53.0 0.7 copy-done.8
  53.7 0.0 reduce-scatter.2.cloned.1.call-update
  53.7 5.6 %all-to-all-start.1 = ((bf16[64,40,128]{2,1,0:T(8,128)(2,1)}), bf16[64,40,128]{2,1,0:T(8,128)(2,1)S(1)}, u32[]{:S(2)}, u32[]{:S(2)}) async-start(bf16[64,40,128]{2,1,0:T(8,128)(2,1)} %grad_rows.1), calls=%async_computation.2 | async-start | bytes 1310720 | tf_op jit(solution)/shard_map/all_to_all | solution.py:398
  59.4 0.0 all-gather.2.cloned.1.call-start
  59.4 1.9 collective-permute-start.3
  61.3 20.5 %all-to-all-done.1.chunks_ref = bf16[64,40,128]{2,1,0:T(8,128)(2,1)S(1)} async-done(((bf16[64,40,128]{2,1,0:T(8,128)(2,1)}), bf16[64,40,128]{2,1,0:T(8,128)(2,1)S(1)}, u32[]{:S(2)}, u32[]{:S(2)}) %all-to-all-start.1) | async-done | bytes 655392 | tf_op jit(solution)/shard_map/all_to_all | solution.py:398
  81.8 0.8 unpack.3
  82.6 1.9 collective-permute-start.2
  84.6 0.0 collective-permute-done.3.other_ref.down_hbm
  84.6 0.0 copy-start.4
  84.6 1.5 collective-permute-done.2.got_ref
  86.1 0.7 hidden_grad.1
  86.8 4.9 %collective-permute-start.4 = (bf16[4,72,768]{2,1,0:T(8,128)(2,1)S(1)}, bf16[4,72,768]{2,1,0:T(8,128)(2,1)S(1)}, u32[]{:S(2)}, u32[]{:S(2)}) collective-permute-start(bf16[4,72,768]{2,1,0:T(8,128)(2,1)S(1)} %get-tuple-element.37), channel_id=1, source_target_pairs={{0,128},{64,960},{128,0},{192,320},{256,384},{320,192},{384,256},{... | collective-permute-start | bytes 1327112 | tf_op jit(solution)/shard_map/ppermute | solution.py:459
  91.7 11.4 %collective-permute-done.4 = bf16[4,72,768]{2,1,0:T(8,128)(2,1)S(1)} collective-permute-done((bf16[4,72,768]{2,1,0:T(8,128)(2,1)S(1)}, bf16[4,72,768]{2,1,0:T(8,128)(2,1)S(1)}, u32[]{:S(2)}, u32[]{:S(2)}) %collective-permute-start.4) | collective-permute-done | bytes 442400 | tf_op jit(solution)/shard_map/ppermute | solution.py:459
  103.1 2.2 reduce-scatter.2.cloned.1.call-done
  105.3 0.0 all-gather.2.cloned.1.call-update
  105.3 0.1 add_convert_fusion
  105.4 22.5 %all_to_all.20.parts_ref = bf16[4,72,768]{2,1,0:T(8,128)(2,1)S(1)} all-to-all(bf16[4,72,768]{2,1,0:T(8,128)(2,1)S(1)} %add_convert_fusion), channel_id=1, replica_groups={{0,256,512,768},{128,384,640,896},{64,320,576,832},{192,448,704,960},{1..., dimensions={0} | all-to-all | bytes 884736 | tf_op jit(solution)/shard_map/all_to_all | solution.py:462
  127.9 0.1 total.1
  128.0 30.0 %all_gather.7.grad_hbm = bf16[576,768]{1,0:T(8,128)(2,1)} all-gather(bf16[72,768]{1,0:T(8,128)(2,1)S(1)} %total.1), channel_id=1, replica_groups={{0,128,256,384,512,640,768,896},{64,192,320,448,576,704,832,960},{1,129..., dimensions={0}, use_global_device_ids=true | all-gather | bytes 995328 | tf_op jit(solution)/shard_map/all_gather | solution.py:471
  157.9 5.2 %expert_rows.1 = (bf16[576,768]{1,0:T(8,128)(2,1)}, bf16[576,1536]{1,0:T(8,128)(2,1)}, bf16[1152,256]{1,0:T(8,128)(2,1)}, bf16[1152,256]{1,0:T(8,128)(2,1)}) custom-call(bf16[576,1536]{1,0:T(8,128)(2,1)} %all-gather.2.cloned.1.call-done.shares_hbm, bf16[576,768]{1,0:T(8,128)(2,1)} %all_gather.7.grad_hbm, bf16[256,1536]{1,0:T(8,128)(2,1)} %copy-done, ...), custom_call_target="tpu_custom_call" | custom-call | tf_op jit(solution)/shard_map/expert_rows/pallas_call | solution.py:473
  163.2 1.9 collective-permute-start.5
  165.1 2.2 collective-permute-done.5.got_ref
  167.3 1.1 copy-done.7
  168.3 2.1 pack.1
  170.5 12.1 %all-to-all-start.3 = ((bf16[64,72,128]{2,1,0:T(8,128)(2,1)}), bf16[64,72,128]{2,1,0:T(8,128)(2,1)S(1)}, u32[]{:S(2)}, u32[]{:S(2)}) async-start(bf16[64,72,128]{2,1,0:T(8,128)(2,1)} %pack.1), calls=%async_computation.4 | async-start | bytes 2359296 | tf_op jit(solution)/shard_map/all_to_all | solution.py:398
  182.6 0.0 copy-start.18
  182.6 0.0 copy-done.9
  182.6 2.3 %convolution_convert_fusion = bf16[256,1536]{1,0:T(8,128)(2,1)S(1)} fusion(bf16[576,256]{1,0:T(8,128)(2,1)S(1)} %copy-done.9, bf16[576,1536]{1,0:T(8,128)(2,1)} %get-tuple-element.45), kind=kOutput, calls=%fused_computation | convolution fusion | flops 453378048 | bytes 2850816 | tf_op jit(solution)/shard_map/dot_general | solution.py:29
  185.0 0.0 copy-start.11
  185.0 0.0 copy-start.13
  185.0 1.9 collective-permute-start.6
  186.9 0.5 convolution_convert_fusion.1
  187.5 2.4 %collective-permute-start.7 = (bf16[768,256]{1,0:T(8,128)(2,1)S(1)}, bf16[768,256]{1,0:T(8,128)(2,1)S(1)}, u32[]{:S(2)}, u32[]{:S(2)}) collective-permute-start(bf16[768,256]{1,0:T(8,128)(2,1)S(1)} %convolution_convert_fusion.1), channel_id=1, source_target_pairs={{0,64},{64,0},{128,192},{192,128},{256,320},{320,256},{384,448},{4... | collective-permute-start | bytes 1179656 | tf_op jit(solution)/shard_map/ppermute | solution.py:395
  189.9 0.0 copy-done.11
  189.9 0.5 table.1.table_ref
  190.4 0.0 copy-start.2
  190.4 0.8 collective-permute-done.7
  191.2 1.3 fusion.3
  192.5 0.0 collective-permute-done.6
  192.5 0.2 convert_element_type.34
  192.7 1.3 fusion.4
  193.9 1.3 fusion.5
  195.2 20.7 %all-to-all-done.3.chunks_ref = bf16[64,72,128]{2,1,0:T(8,128)(2,1)S(1)} async-done(((bf16[64,72,128]{2,1,0:T(8,128)(2,1)}), bf16[64,72,128]{2,1,0:T(8,128)(2,1)S(1)}, u32[]{:S(2)}, u32[]{:S(2)}) %all-to-all-start.3) | async-done | bytes 1179680 | tf_op jit(solution)/shard_map/all_to_all | solution.py:398
  215.9 2.0 merge.1
  (23 shorter events, 0.0 us)
Async XLA Ops:
  7.2 23.5 %copy-start.15 = (s32[128]{0:T(128)S(1)}, s32[128]{0:T(128)}, u32[]{:S(2)}) copy-start(s32[128]{0:T(128)} %param.12) | copy-start | bytes 1540
  7.2 23.5 %copy-start.14 = (bf16[128,256]{1,0:T(8,128)(2,1)S(1)}, bf16[128,256]{1,0:T(8,128)(2,1)}, u32[]{:S(2)}) copy-start(bf16[128,256]{1,0:T(8,128)(2,1)} %cot_ref.1) | copy-start | bytes 196612
  10.0 20.6 %copy-start.10 = (f32[64,128]{1,0:T(8,128)S(1)}, f32[64,128]{1,0:T(8,128)}, u32[]{:S(2)}) copy-start(f32[64,128]{1,0:T(8,128)} %get-tuple-element.27.rank_ref) | copy-start | bytes 98308
  10.0 20.6 %copy-start.12 = (f32[64,128]{1,0:T(8,128)S(1)}, f32[64,128]{1,0:T(8,128)}, u32[]{:S(2)}) copy-start(f32[64,128]{1,0:T(8,128)} %get-tuple-element.28.weight_ref) | copy-start | bytes 98308
  10.1 35.8 %all-to-all-start = ((bf16[64,40,128]{2,1,0:T(8,128)(2,1)}), bf16[64,40,128]{2,1,0:T(8,128)(2,1)S(1)}, u32[]{:S(2)}, u32[]{:S(2)}) async-start(bf16[64,40,128]{2,1,0:T(8,128)(2,1)} %get-tuple-element.26), calls=%async_computation | async-start | bytes 1310720 | tf_op jit(solution)/shard_map/all_to_all | solution.py:398
  27.4 22.7 %copy-start.5 = (bf16[1,256,768]{2,1,0:T(8,128)(2,1)S(1)}, bf16[1,256,768]{2,1,0:T(8,128)(2,1)}, u32[]{:S(2)}) copy-start(bf16[1,256,768]{2,1,0:T(8,128)(2,1)} %param.15) | copy-start | bytes 1179652
  27.4 22.7 %copy-start.6 = (bf16[1,256,768]{2,1,0:T(8,128)(2,1)S(1)}, bf16[1,256,768]{2,1,0:T(8,128)(2,1)}, u32[]{:S(2)}) copy-start(bf16[1,256,768]{2,1,0:T(8,128)(2,1)} %param.16) | copy-start | bytes 1179652
  27.4 77.8 %reduce-scatter.2.cloned.1.call-start = ((), (), s32[]{:S(2)}) async-start(), calls=%async_computation.5 | async-start | bytes 1990656 | tf_op jit(solution)/shard_map/reduce_scatter | solution.py:447
  28.7 23.5 %copy-start.16 = (bf16[256,1536]{1,0:T(8,128)(2,1)}, bf16[256,1536]{1,0:T(8,128)(2,1)S(1)}, u32[]{:S(2)}) copy-start(bf16[256,1536]{1,0:T(8,128)(2,1)S(1)} %pad_maximum_fusion.gu_own_hbm) | copy-start | bytes 2359300
  28.7 19.9 %collective-permute-start.1 = (bf16[256,1536]{1,0:T(8,128)(2,1)S(1)}, bf16[256,1536]{1,0:T(8,128)(2,1)S(1)}, u32[]{:S(2)}, u32[]{:S(2)}) collective-permute-start(bf16[256,1536]{1,0:T(8,128)(2,1)S(1)} %pad_maximum_fusion.gu_own_hbm), channel_id=1, source_target_pairs={{0,64},{64,0},{128,192},{192,128},{256,320},{320,256},{384,448},{4... | collective-permute-start | bytes 2359304 | tf_op jit(solution)/shard_map/ppermute | solution.py:395
  46.6 3.5 %collective-permute-start = (bf16[576,256]{1,0:T(8,128)(2,1)S(1)}, bf16[576,256]{1,0:T(8,128)(2,1)S(1)}, u32[]{:S(2)}, u32[]{:S(2)}) collective-permute-start(bf16[576,256]{1,0:T(8,128)(2,1)S(1)} %get-tuple-element.31), channel_id=1, source_target_pairs={{0,64},{64,0},{128,192},{192,128},{256,320},{320,256},{384,448},{4... | collective-permute-start | bytes 884744 | tf_op jit(solution)/shard_map/ppermute | solution.py:395
  48.6 3.7 %copy-start = (bf16[256,1536]{1,0:T(8,128)(2,1)}, bf16[256,1536]{1,0:T(8,128)(2,1)S(1)}, u32[]{:S(2)}) copy-start(bf16[256,1536]{1,0:T(8,128)(2,1)S(1)} %collective-permute-done.1.other_ref.gu_hbm) | copy-start | bytes 2359300
  52.3 0.7 copy-start.1
  53.0 0.7 copy-start.8
  53.7 5.7 %copy-start.3 = (bf16[1,768,256]{2,1,0:T(8,128)(2,1)S(1)}, bf16[1,768,256]{2,1,0:T(8,128)(2,1)}, u32[]{:S(2)}) copy-start(bf16[1,768,256]{2,1,0:T(8,128)(2,1)} %param.17) | copy-start | bytes 1179652
  53.7 28.1 %all-to-all-start.1 = ((bf16[64,40,128]{2,1,0:T(8,128)(2,1)}), bf16[64,40,128]{2,1,0:T(8,128)(2,1)S(1)}, u32[]{:S(2)}, u32[]{:S(2)}) async-start(bf16[64,40,128]{2,1,0:T(8,128)(2,1)} %grad_rows.1), calls=%async_computation.2 | async-start | bytes 1310720 | tf_op jit(solution)/shard_map/all_to_all | solution.py:398
  59.4 98.6 %all-gather.2.cloned.1.call-start = ((), (), s32[]{:S(2)}) async-start(), calls=%async_computation.6 | async-start | bytes 1990656 | tf_op jit(solution)/shard_map/all_gather | solution.py:461
  59.4 25.2 %collective-permute-start.3 = (bf16[768,256]{1,0:T(8,128)(2,1)S(1)}, bf16[768,256]{1,0:T(8,128)(2,1)S(1)}, u32[]{:S(2)}, u32[]{:S(2)}) collective-permute-start(bf16[768,256]{1,0:T(8,128)(2,1)S(1)} %bitcast.24), channel_id=1, source_target_pairs={{0,64},{64,0},{128,192},{192,128},{256,320},{320,256},{384,448},{4... | collective-permute-start | bytes 1179656 | tf_op jit(solution)/shard_map/ppermute | solution.py:395
  82.6 3.5 %collective-permute-start.2 = (bf16[576,256]{1,0:T(8,128)(2,1)S(1)}, bf16[576,256]{1,0:T(8,128)(2,1)S(1)}, u32[]{:S(2)}, u32[]{:S(2)}) collective-permute-start(bf16[576,256]{1,0:T(8,128)(2,1)S(1)} %get-tuple-element.36), channel_id=1, source_target_pairs={{0,64},{64,0},{128,192},{192,128},{256,320},{320,256},{384,448},{4... | collective-permute-start | bytes 884744 | tf_op jit(solution)/shard_map/ppermute | solution.py:395
  84.6 43.3 %copy-start.4 = (bf16[768,256]{1,0:T(8,128)(2,1)}, bf16[768,256]{1,0:T(8,128)(2,1)S(1)}, u32[]{:S(2)}) copy-start(bf16[768,256]{1,0:T(8,128)(2,1)S(1)} %collective-permute-done.3.other_ref.down_hbm) | copy-start | bytes 1179652
  86.8 16.3 %collective-permute-start.4 = (bf16[4,72,768]{2,1,0:T(8,128)(2,1)S(1)}, bf16[4,72,768]{2,1,0:T(8,128)(2,1)S(1)}, u32[]{:S(2)}, u32[]{:S(2)}) collective-permute-start(bf16[4,72,768]{2,1,0:T(8,128)(2,1)S(1)} %get-tuple-element.37), channel_id=1, source_target_pairs={{0,128},{64,960},{128,0},{192,320},{256,384},{320,192},{384,256},{... | collective-permute-start | bytes 1327112 | tf_op jit(solution)/shard_map/ppermute | solution.py:459
  163.2 4.1 %collective-permute-start.5 = (bf16[1152,256]{1,0:T(8,128)(2,1)}, bf16[1152,256]{1,0:T(8,128)(2,1)S(1)}, u32[]{:S(2)}, u32[]{:S(2)}) collective-permute-start(bf16[1152,256]{1,0:T(8,128)(2,1)} %get-tuple-element.42), channel_id=1, source_target_pairs={{0,64},{64,0},{128,192},{192,128},{256,320},{320,256},{384,448},{4... | collective-permute-start | bytes 1769480 | tf_op jit(solution)/shard_map/ppermute | solution.py:395
  167.3 1.1 copy-start.7
  170.5 12.2 %copy-start.9 = (bf16[576,256]{1,0:T(8,128)(2,1)S(1)}, bf16[576,256]{1,0:T(8,128)(2,1)}, u32[]{:S(2)}) copy-start(bf16[576,256]{1,0:T(8,128)(2,1)} %copy-done.8) | copy-start | bytes 884740
  170.5 45.4 %all-to-all-start.3 = ((bf16[64,72,128]{2,1,0:T(8,128)(2,1)}), bf16[64,72,128]{2,1,0:T(8,128)(2,1)S(1)}, u32[]{:S(2)}, u32[]{:S(2)}) async-start(bf16[64,72,128]{2,1,0:T(8,128)(2,1)} %pack.1), calls=%async_computation.4 | async-start | bytes 2359296 | tf_op jit(solution)/shard_map/all_to_all | solution.py:398
  182.6 4.3 %copy-start.18 = (bf16[576,768]{1,0:T(8,128)(2,1)S(1)}, bf16[576,768]{1,0:T(8,128)(2,1)}, u32[]{:S(2)}) copy-start(bf16[576,768]{1,0:T(8,128)(2,1)} %get-tuple-element.46) | copy-start | bytes 2654212
  185.0 4.9 %copy-start.11 = (f32[64,128]{1,0:T(8,128)S(1)}, f32[64,128]{1,0:T(8,128)}, u32[]{:S(2)}) copy-start(f32[64,128]{1,0:T(8,128)} %get-tuple-element.27.rank_ref) | copy-start | bytes 98308
  185.0 4.9 %copy-start.13 = (f32[64,128]{1,0:T(8,128)S(1)}, f32[64,128]{1,0:T(8,128)}, u32[]{:S(2)}) copy-start(f32[64,128]{1,0:T(8,128)} %get-tuple-element.28.weight_ref) | copy-start | bytes 98308
  185.0 7.5 %collective-permute-start.6 = (bf16[256,1536]{1,0:T(8,128)(2,1)S(1)}, bf16[256,1536]{1,0:T(8,128)(2,1)S(1)}, u32[]{:S(2)}, u32[]{:S(2)}) collective-permute-start(bf16[256,1536]{1,0:T(8,128)(2,1)S(1)} %convolution_convert_fusion), channel_id=1, source_target_pairs={{0,64},{64,0},{128,192},{192,128},{256,320},{320,256},{384,448},{4... | collective-permute-start | bytes 2359304 | tf_op jit(solution)/shard_map/ppermute | solution.py:395
  187.5 3.7 %collective-permute-start.7 = (bf16[768,256]{1,0:T(8,128)(2,1)S(1)}, bf16[768,256]{1,0:T(8,128)(2,1)S(1)}, u32[]{:S(2)}, u32[]{:S(2)}) collective-permute-start(bf16[768,256]{1,0:T(8,128)(2,1)S(1)} %convolution_convert_fusion.1), channel_id=1, source_target_pairs={{0,64},{64,0},{128,192},{192,128},{256,320},{320,256},{384,448},{4... | collective-permute-start | bytes 1179656 | tf_op jit(solution)/shard_map/ppermute | solution.py:395
  190.4 2.3 %copy-start.2 = (bf16[576,256]{1,0:T(8,128)(2,1)S(1)}, bf16[576,256]{1,0:T(8,128)(2,1)}, u32[]{:S(2)}) copy-start(bf16[576,256]{1,0:T(8,128)(2,1)} %copy-done.1) | copy-start | bytes 884740
  190.4 2.3 %copy-start.17 = (bf16[576,1536]{1,0:T(8,128)(2,1)S(1)}, bf16[576,1536]{1,0:T(8,128)(2,1)}, u32[]{:S(2)}) copy-start(bf16[576,1536]{1,0:T(8,128)(2,1)} %get-tuple-element.45) | copy-start | bytes 5308420
Sparse Core Ops, SparseCore 0:
  53.8 51.4 reduce-scatter.1
  107.9 48.9 all-gather.1

commit v8 on v7

--- a/solution.py
+++ b/solution.py
@@ -58,6 +58,7 @@
 
 
 def token_kernel(
+    capacity,
     pad,
     routes_hbm,
     combine_hbm,
@@ -88,9 +89,11 @@
     top_count, tok_rows = routes_ref.shape
     experts = limits_ref.shape[1]
     chunk = 2 * pad
-    slots = experts * chunk
-    owner = owners((slots, experts), 0, chunk)
-    left, right = wanted((slots, tok_rows), 0, pad)
+    slots = experts * capacity
+    owner = owners((slots, experts), 0, capacity)
+    place = remainder(number((slots, 1), 0), capacity)
+    rows = GROUP * capacity
+    moves = [shifts((GROUP * chunk, rows), 1, capacity, pad, side) for side in range(2)]
     before = number((tok_rows, tok_rows), 0) < number((tok_rows, tok_rows), 1)
     square = (experts, experts)
     for copy in copies:
@@ -109,12 +112,22 @@
     rank = jnp.where(kept, rank, -1.0)
     rank_out[...] = rank
     weight_out[...] = weight
-    spread = mul(owner, rank.astype(LOW))
-    tokens = tokens_ref[...]
-    lanes = tokens.shape[1] // 2
-    picked = jnp.concatenate([low_if(spread == left), low_if(spread == right)], axis=1)
-    sides = jnp.concatenate([tokens[:, :lanes], tokens[:, lanes:]], axis=0)
-    tok_out[...] = mul(picked, sides).reshape(experts, chunk, lanes).astype(LOW)
+    picked = low_if(mul(owner, rank.astype(LOW)) == place)
+    compact = mul(picked, tokens_ref[...]).astype(LOW)
+    lanes = compact.shape[1] // 2
+    for at in range(0, experts // GROUP, 2):
+        first = compact[at * rows : (at + 1) * rows]
+        second = compact[(at + 1) * rows : (at + 2) * rows]
+        moved = mul(moves[0], jnp.concatenate([first[:, :lanes], second[:, :lanes]], axis=1))
+        moved = moved + mul(
+            moves[1], jnp.concatenate([first[:, lanes:], second[:, lanes:]], axis=1)
+        )
+        for side in range(2):
+            tok_out[(at + side) * GROUP : (at + side + 1) * GROUP] = (
+                moved[:, side * lanes : (side + 1) * lanes]
+                .reshape(GROUP, chunk, lanes)
+                .astype(LOW)
+            )
 
 
 def grad_kernel(pad, rank_ref, weight_ref, clip_ref, cot_ref, cot_out):
@@ -189,13 +202,25 @@
                 ).astype(LOW)
 
 
-def pack_kernel(capacity, core_ref, mine_ref, got_ref, chunks_out):
+def pack_kernel(
+    capacity, core_ref, mine_hbm, got_hbm, chunks_out, mine_ref, got_ref, sems
+):
+    loads = [
+        pltpu.make_async_copy(mine_hbm, mine_ref, sems.at[0]),
+        pltpu.make_async_copy(got_hbm, got_ref, sems.at[1]),
+    ]
+    for load in loads:
+        load.start()
     lanes = chunks_out.shape[2]
     half = chunks_out.shape[0] // 2
     rows = GROUP * capacity
     moves = places(GROUP, capacity, False)
     core = core_ref[0]
-    for in_ref, base in ((mine_ref, core * half), (got_ref, (1 - core) * half)):
+    for in_ref, base, load in (
+        (mine_ref, core * half, loads[0]),
+        (got_ref, (1 - core) * half, loads[1]),
+    ):
+        load.wait()
         for at in range(0, half // GROUP, 2):
             stacked = jnp.concatenate(
                 [
@@ -305,6 +330,10 @@
     down_hbm,
     gu_own_hbm,
     down_own_hbm,
+    hidden_hbm,
+    derived_hbm,
+    give_hbm,
+    mine_hbm,
     hidden_out,
     derived_out,
     give_out,
@@ -335,6 +364,12 @@
     ]
     for copy in [copy for load in loads for copy in load] + weights:
         copy.start()
+    stores = []
+
+    def store(source, target):
+        stores.append(pltpu.make_async_copy(source, target, sems.at[12 + len(stores)]))
+        stores[-1].start()
+
     for rows, load in zip(blocks, loads):
         for copy in load:
             copy.wait()
@@ -345,14 +380,20 @@
         hidden_out[rows, :] = (active * up_val).astype(LOW)
         derived_out[rows, :ff] = (grad_hidden * up_val * slope).astype(LOW)
         derived_out[rows, ff:] = (grad_hidden * active).astype(LOW)
+        store(hidden_out.at[rows], hidden_hbm.at[rows])
+        store(derived_out.at[rows], derived_hbm.at[rows])
     for copy in weights:
         copy.wait()
-    for out_ref, lower_ref, upper_ref in (
-        (give_out, down_ref, gu_ref),
-        (mine_out, down_own_ref, gu_own_ref),
+    for out_ref, out_hbm, lower_ref, upper_ref in (
+        (give_out, give_hbm, down_ref, gu_ref),
+        (mine_out, mine_hbm, down_own_ref, gu_own_ref),
     ):
         out_ref[:half, :] = mul(hidden_out[...], lower_ref[...]).astype(LOW)
+        store(out_ref.at[:half], out_hbm.at[:half])
         out_ref[half:, :] = against(derived_out[...], upper_ref[...]).astype(LOW)
+        store(out_ref.at[half:], out_hbm.at[half:])
+    for copy in stores:
+        copy.wait()
 
 
 def body(
@@ -413,7 +454,7 @@
     down_other = swap(down_own)
 
     token_send, rank, weight = pl.pallas_call(
-        functools.partial(token_kernel, pad),
+        functools.partial(token_kernel, capacity, pad),
         out_shape=(chunk_shape, rank_shape, rank_shape),
         in_specs=[anywhere] * 4,
         scratch_shapes=[
@@ -479,14 +520,19 @@
             pair_shape,
         ),
         in_specs=[anywhere] * 6,
+        out_specs=(anywhere,) * 4,
         scratch_shapes=[
+            pltpu.VMEM((half, ff), LOW),
+            pltpu.VMEM((half, 2 * ff), LOW),
+            pltpu.VMEM((2 * half, width), LOW),
+            pltpu.VMEM((2 * half, width), LOW),
             pltpu.VMEM((half, 2 * ff), LOW),
             pltpu.VMEM((half, ff), LOW),
             pltpu.VMEM((width, 2 * ff), LOW),
             pltpu.VMEM((ff, width), LOW),
             pltpu.VMEM((width, 2 * ff), LOW),
             pltpu.VMEM((ff, width), LOW),
-            pltpu.SemaphoreType.DMA((12,)),
+            pltpu.SemaphoreType.DMA((24,)),
         ],
         compiler_params=pltpu.CompilerParams(vmem_limit_bytes=63 * 1024 * 1024),
         name="expert_rows",
@@ -495,8 +541,13 @@
         pl.pallas_call(
             functools.partial(pack_kernel, capacity),
             out_shape=jax.ShapeDtypeStruct((experts, 4 * capacity, lanes), LOW),
-            in_specs=[in_smem] + [in_vmem] * 2,
-            compiler_params=params,
+            in_specs=[in_smem] + [anywhere] * 2,
+            scratch_shapes=[
+                pltpu.VMEM((2 * half, width), LOW),
+                pltpu.VMEM((2 * half, width), LOW),
+                pltpu.SemaphoreType.DMA((2,)),
+            ],
+            compiler_params=pltpu.CompilerParams(vmem_limit_bytes=63 * 1024 * 1024),
             name="pack",
         )(core, mine, swap(give))
     )

time: 226 us -> 226 us (level)
  no operation moved by 1% of the time
where the time goes in v8:
time: 226 us; the launch traced here: 225 us
  waiting for transfers between devices  73.4 us (32%)
  starting transfers between devices  53.6 us (24%)
  blocking collectives  52.7 us (23%)
  Pallas kernels  21.4 us (9%)
  between operations  14.5 us (6%)
  matrix products  6.64 us (3%)
    all_to_all x3, waiting for transfers between devices, exchange(): lax.all_to_all(chunks, 'expert', split_axis=0, concat_axis=0, tiled=True)  53.8 us
    all_to_all x3, starting transfers between devices, exchange(): lax.all_to_all(chunks, 'expert', split_axis=0, concat_axis=0, tiled=True)  34.4 us
    all_gather x1, blocking collectives, body(): lax.all_gather(grad_total, 'dp', axis=0, tiled=True, axis_index_groups=co...  30.2 us
    all_to_all x1, blocking collectives, body(): lax.all_to_all(joined, 'dp', split_axis=0, concat_axis=0, tiled=True, axi...  22.5 us
    ppermute x7, starting transfers between devices, swap(): return lax.ppermute(values, 'dp', swap_pairs)  14.1 us
    ppermute x1, waiting for transfers between devices, body(): lax.ppermute(leave, 'dp', near_pairs)  11.4 us
    dot_general x5, matrix products, outer(): lax.dot_general(left, right, (((0,), (0,)), ((), ())), preferred_element_...  6.64 us
    ppermute x7, waiting for transfers between devices, swap(): return lax.ppermute(values, 'dp', swap_pairs)  5.99 us
  transfers between devices with their start and end apart: 13, of which 9 were waited for; matrix products, arithmetic and copies ran while one was open for 4% of the time, Pallas kernels for 2%

profile of v8, /device:TPU:4, one launch (start us, length us, event | category | flops | bytes accessed | tf_op | source)
XLA Modules:
  0.0 225.2 jit_solution(7394817855508511059)
XLA Ops:
  7.2 2.9 %token_rows.1 = (bf16[64,40,128]{2,1,0:T(8,128)(2,1)}, f32[64,128]{1,0:T(8,128)}, f32[64,128]{1,0:T(8,128)}) custom-call(s32[8,128]{1,0:T(8,128)} %bitcast.31, f32[8,128]{1,0:T(8,128)} %bitcast.32, s32[1,64]{1,0:T(1,128)} %bitcast.33, bf16[128,256]{1,0:T(8,128)(2,1)} %tokens_hbm.1), custom_call_target="tpu_custom_call" | custom-call | tf_op jit(solution)/shard_map/token_rows/pallas_call | solution.py:456
  10.1 0.0 copy-start.9
  10.1 0.0 copy-start.11
  10.1 17.3 %all-to-all-start = ((bf16[64,40,128]{2,1,0:T(8,128)(2,1)}), bf16[64,40,128]{2,1,0:T(8,128)(2,1)S(1)}, u32[]{:S(2)}, u32[]{:S(2)}) async-start(bf16[64,40,128]{2,1,0:T(8,128)(2,1)} %get-tuple-element.26), calls=%async_computation | async-start | bytes 1310720 | tf_op jit(solution)/shard_map/all_to_all | solution.py:439
  27.5 0.0 copy-start.5
  27.5 0.0 copy-start.6
  27.5 0.0 reduce-scatter.2.cloned.1.call-start
  27.6 1.2 pad_maximum_fusion.gu_own_hbm
  28.8 1.9 collective-permute-start.1
  30.8 2.6 %grad_rows.1 = bf16[64,40,128]{2,1,0:T(8,128)(2,1)} custom-call(f32[64,128]{1,0:T(8,128)S(1)} %copy-done.9, f32[64,128]{1,0:T(8,128)S(1)} %copy-done.11, s32[1,128]{1,0:T(1,128)S(1)} %bitcast.30, bf16[128,256]{1,0:T(8,128)(2,1)S(1)} %copy-done.13), custom_call_target="tpu_custom_call" | custom-call | tf_op jit(solution)/shard_map/grad_rows/pallas_call | solution.py:470
  33.4 12.6 %all-to-all-done.chunks_ref = bf16[64,40,128]{2,1,0:T(8,128)(2,1)S(1)} async-done(((bf16[64,40,128]{2,1,0:T(8,128)(2,1)}), bf16[64,40,128]{2,1,0:T(8,128)(2,1)S(1)}, u32[]{:S(2)}, u32[]{:S(2)}) %all-to-all-start) | async-done | bytes 655392 | tf_op jit(solution)/shard_map/all_to_all | solution.py:439
  46.0 0.8 unpack.2
  46.7 1.9 collective-permute-start
  48.7 0.0 collective-permute-done.1.other_ref.gu_hbm
  48.7 0.0 copy-start
  48.7 1.5 collective-permute-done.got_ref
  50.2 2.1 gate_up.1
  52.3 0.0 copy-done.15
  52.3 0.0 copy-done
  52.3 0.0 copy-start.1
  52.4 0.7 copy-done.1
  53.1 0.7 copy-done.7
  53.8 0.0 reduce-scatter.2.cloned.1.call-update
  53.8 5.6 %all-to-all-start.1 = ((bf16[64,40,128]{2,1,0:T(8,128)(2,1)}), bf16[64,40,128]{2,1,0:T(8,128)(2,1)S(1)}, u32[]{:S(2)}, u32[]{:S(2)}) async-start(bf16[64,40,128]{2,1,0:T(8,128)(2,1)} %grad_rows.1), calls=%async_computation.2 | async-start | bytes 1310720 | tf_op jit(solution)/shard_map/all_to_all | solution.py:439
  59.4 0.0 all-gather.2.cloned.1.call-start
  59.5 1.9 collective-permute-start.3
  61.4 20.5 %all-to-all-done.1.chunks_ref = bf16[64,40,128]{2,1,0:T(8,128)(2,1)S(1)} async-done(((bf16[64,40,128]{2,1,0:T(8,128)(2,1)}), bf16[64,40,128]{2,1,0:T(8,128)(2,1)S(1)}, u32[]{:S(2)}, u32[]{:S(2)}) %all-to-all-start.1) | async-done | bytes 655392 | tf_op jit(solution)/shard_map/all_to_all | solution.py:439
  81.9 0.8 unpack.3
  82.7 1.9 collective-permute-start.2
  84.7 0.0 collective-permute-done.3.other_ref.down_hbm
  84.7 0.0 copy-start.4
  84.7 1.5 collective-permute-done.2.got_ref
  86.2 0.7 hidden_grad.1
  86.8 4.9 %collective-permute-start.4 = (bf16[4,72,768]{2,1,0:T(8,128)(2,1)S(1)}, bf16[4,72,768]{2,1,0:T(8,128)(2,1)S(1)}, u32[]{:S(2)}, u32[]{:S(2)}) collective-permute-start(bf16[4,72,768]{2,1,0:T(8,128)(2,1)S(1)} %get-tuple-element.37), channel_id=1, source_target_pairs={{0,128},{64,960},{128,0},{192,320},{256,384},{320,192},{384,256},{... | collective-permute-start | bytes 1327112 | tf_op jit(solution)/shard_map/ppermute | solution.py:500
  91.8 11.4 %collective-permute-done.4 = bf16[4,72,768]{2,1,0:T(8,128)(2,1)S(1)} collective-permute-done((bf16[4,72,768]{2,1,0:T(8,128)(2,1)S(1)}, bf16[4,72,768]{2,1,0:T(8,128)(2,1)S(1)}, u32[]{:S(2)}, u32[]{:S(2)}) %collective-permute-start.4) | collective-permute-done | bytes 442400 | tf_op jit(solution)/shard_map/ppermute | solution.py:500
  103.2 2.2 reduce-scatter.2.cloned.1.call-done
  105.4 0.0 all-gather.2.cloned.1.call-update
  105.4 0.1 add_convert_fusion
  105.5 22.5 %all_to_all.20.parts_ref = bf16[4,72,768]{2,1,0:T(8,128)(2,1)S(1)} all-to-all(bf16[4,72,768]{2,1,0:T(8,128)(2,1)S(1)} %add_convert_fusion), channel_id=1, replica_groups={{0,256,512,768},{128,384,640,896},{64,320,576,832},{192,448,704,960},{1..., dimensions={0} | all-to-all | bytes 884736 | tf_op jit(solution)/shard_map/all_to_all | solution.py:503
  128.0 0.1 total.1
  128.1 30.2 %all_gather.7.grad_hbm = bf16[576,768]{1,0:T(8,128)(2,1)} all-gather(bf16[72,768]{1,0:T(8,128)(2,1)S(1)} %total.1), channel_id=1, replica_groups={{0,128,256,384,512,640,768,896},{64,192,320,448,576,704,832,960},{1,129..., dimensions={0}, use_global_device_ids=true | all-gather | bytes 995328 | tf_op jit(solution)/shard_map/all_gather | solution.py:512
  158.2 5.7 %expert_rows.1 = (bf16[576,768]{1,0:T(8,128)(2,1)}, bf16[576,1536]{1,0:T(8,128)(2,1)}, bf16[1152,256]{1,0:T(8,128)(2,1)}, bf16[1152,256]{1,0:T(8,128)(2,1)}) custom-call(bf16[576,1536]{1,0:T(8,128)(2,1)} %all-gather.2.cloned.1.call-done.shares_hbm, bf16[576,768]{1,0:T(8,128)(2,1)} %all_gather.7.grad_hbm, bf16[256,1536]{1,0:T(8,128)(2,1)} %copy-done, ...), custom_call_target="tpu_custom_call" | custom-call | tf_op jit(solution)/shard_map/expert_rows/pallas_call | solution.py:514
  163.9 2.1 collective-permute-start.5
  166.1 2.1 collective-permute-done.5.got_hbm
  168.2 3.4 %pack.1 = bf16[64,72,128]{2,1,0:T(8,128)(2,1)} custom-call(s32[1]{0:T(128)} %bitcast.core_ref, bf16[1152,256]{1,0:T(8,128)(2,1)} %get-tuple-element.41.mine_hbm, bf16[1152,256]{1,0:T(8,128)(2,1)} %collective-permute-done.5.got_hbm), custom_call_target="tpu_custom_call" | custom-call | tf_op jit(solution)/shard_map/pack/pallas_call | solution.py:541
  171.6 0.0 copy-start.8
  171.6 11.4 %all-to-all-start.3 = ((bf16[64,72,128]{2,1,0:T(8,128)(2,1)}), bf16[64,72,128]{2,1,0:T(8,128)(2,1)S(1)}, u32[]{:S(2)}, u32[]{:S(2)}) async-start(bf16[64,72,128]{2,1,0:T(8,128)(2,1)} %pack.1), calls=%async_computation.4 | async-start | bytes 2359296 | tf_op jit(solution)/shard_map/all_to_all | solution.py:439
  183.0 0.0 copy-start.17
  183.0 2.3 %convolution_convert_fusion = bf16[256,1536]{1,0:T(8,128)(2,1)S(1)} fusion(bf16[576,256]{1,0:T(8,128)(2,1)S(1)} %copy-done.8, bf16[576,1536]{1,0:T(8,128)(2,1)} %get-tuple-element.45), kind=kOutput, calls=%fused_computation | convolution fusion | flops 453378048 | bytes 2850816 | tf_op jit(solution)/shard_map/dot_general | solution.py:29
  185.4 0.0 copy-start.10
  185.4 0.0 copy-start.12
  185.4 1.9 collective-permute-start.6
  187.4 0.5 convolution_convert_fusion.1
  187.9 2.4 %collective-permute-start.7 = (bf16[768,256]{1,0:T(8,128)(2,1)S(1)}, bf16[768,256]{1,0:T(8,128)(2,1)S(1)}, u32[]{:S(2)}, u32[]{:S(2)}) collective-permute-start(bf16[768,256]{1,0:T(8,128)(2,1)S(1)} %convolution_convert_fusion.1), channel_id=1, source_target_pairs={{0,64},{64,0},{128,192},{192,128},{256,320},{320,256},{384,448},{4... | collective-permute-start | bytes 1179656 | tf_op jit(solution)/shard_map/ppermute | solution.py:436
  190.3 0.5 table.1.table_ref
  190.8 0.0 copy-start.2
  190.8 0.8 collective-permute-done.7
  191.6 1.3 fusion.3
  192.9 0.0 collective-permute-done.6
  192.9 0.2 convert_element_type.34
  193.1 1.3 fusion.4
  194.3 1.3 fusion.5
  195.6 20.7 %all-to-all-done.3.chunks_ref = bf16[64,72,128]{2,1,0:T(8,128)(2,1)S(1)} async-done(((bf16[64,72,128]{2,1,0:T(8,128)(2,1)}), bf16[64,72,128]{2,1,0:T(8,128)(2,1)S(1)}, u32[]{:S(2)}, u32[]{:S(2)}) %all-to-all-start.3) | async-done | bytes 1179680 | tf_op jit(solution)/shard_map/all_to_all | solution.py:439
  216.3 2.0 merge.1
  (21 shorter events, 0.0 us)
Async XLA Ops:
  7.2 23.6 %copy-start.14 = (s32[128]{0:T(128)S(1)}, s32[128]{0:T(128)}, u32[]{:S(2)}) copy-start(s32[128]{0:T(128)} %param.12) | copy-start | bytes 1540
  7.2 23.6 %copy-start.13 = (bf16[128,256]{1,0:T(8,128)(2,1)S(1)}, bf16[128,256]{1,0:T(8,128)(2,1)}, u32[]{:S(2)}) copy-start(bf16[128,256]{1,0:T(8,128)(2,1)} %cot_ref.1) | copy-start | bytes 196612
  10.1 20.6 %copy-start.9 = (f32[64,128]{1,0:T(8,128)S(1)}, f32[64,128]{1,0:T(8,128)}, u32[]{:S(2)}) copy-start(f32[64,128]{1,0:T(8,128)} %get-tuple-element.27.rank_ref) | copy-start | bytes 98308
  10.1 20.6 %copy-start.11 = (f32[64,128]{1,0:T(8,128)S(1)}, f32[64,128]{1,0:T(8,128)}, u32[]{:S(2)}) copy-start(f32[64,128]{1,0:T(8,128)} %get-tuple-element.28.weight_ref) | copy-start | bytes 98308
  10.1 35.8 %all-to-all-start = ((bf16[64,40,128]{2,1,0:T(8,128)(2,1)}), bf16[64,40,128]{2,1,0:T(8,128)(2,1)S(1)}, u32[]{:S(2)}, u32[]{:S(2)}) async-start(bf16[64,40,128]{2,1,0:T(8,128)(2,1)} %get-tuple-element.26), calls=%async_computation | async-start | bytes 1310720 | tf_op jit(solution)/shard_map/all_to_all | solution.py:439
  27.5 22.7 %copy-start.5 = (bf16[1,256,768]{2,1,0:T(8,128)(2,1)S(1)}, bf16[1,256,768]{2,1,0:T(8,128)(2,1)}, u32[]{:S(2)}) copy-start(bf16[1,256,768]{2,1,0:T(8,128)(2,1)} %param.15) | copy-start | bytes 1179652
  27.5 22.7 %copy-start.6 = (bf16[1,256,768]{2,1,0:T(8,128)(2,1)S(1)}, bf16[1,256,768]{2,1,0:T(8,128)(2,1)}, u32[]{:S(2)}) copy-start(bf16[1,256,768]{2,1,0:T(8,128)(2,1)} %param.16) | copy-start | bytes 1179652
  27.5 77.8 %reduce-scatter.2.cloned.1.call-start = ((), (), s32[]{:S(2)}) async-start(), calls=%async_computation.5 | async-start | bytes 1990656 | tf_op jit(solution)/shard_map/reduce_scatter | solution.py:488
  28.8 23.5 %copy-start.15 = (bf16[256,1536]{1,0:T(8,128)(2,1)}, bf16[256,1536]{1,0:T(8,128)(2,1)S(1)}, u32[]{:S(2)}) copy-start(bf16[256,1536]{1,0:T(8,128)(2,1)S(1)} %pad_maximum_fusion.gu_own_hbm) | copy-start | bytes 2359300
  28.8 19.9 %collective-permute-start.1 = (bf16[256,1536]{1,0:T(8,128)(2,1)S(1)}, bf16[256,1536]{1,0:T(8,128)(2,1)S(1)}, u32[]{:S(2)}, u32[]{:S(2)}) collective-permute-start(bf16[256,1536]{1,0:T(8,128)(2,1)S(1)} %pad_maximum_fusion.gu_own_hbm), channel_id=1, source_target_pairs={{0,64},{64,0},{128,192},{192,128},{256,320},{320,256},{384,448},{4... | collective-permute-start | bytes 2359304 | tf_op jit(solution)/shard_map/ppermute | solution.py:436
  46.7 3.5 %collective-permute-start = (bf16[576,256]{1,0:T(8,128)(2,1)S(1)}, bf16[576,256]{1,0:T(8,128)(2,1)S(1)}, u32[]{:S(2)}, u32[]{:S(2)}) collective-permute-start(bf16[576,256]{1,0:T(8,128)(2,1)S(1)} %get-tuple-element.31), channel_id=1, source_target_pairs={{0,64},{64,0},{128,192},{192,128},{256,320},{320,256},{384,448},{4... | collective-permute-start | bytes 884744 | tf_op jit(solution)/shard_map/ppermute | solution.py:436
  48.7 3.7 %copy-start = (bf16[256,1536]{1,0:T(8,128)(2,1)}, bf16[256,1536]{1,0:T(8,128)(2,1)S(1)}, u32[]{:S(2)}) copy-start(bf16[256,1536]{1,0:T(8,128)(2,1)S(1)} %collective-permute-done.1.other_ref.gu_hbm) | copy-start | bytes 2359300
  52.3 0.7 copy-start.1
  53.1 0.7 copy-start.7
  53.8 5.7 %copy-start.3 = (bf16[1,768,256]{2,1,0:T(8,128)(2,1)S(1)}, bf16[1,768,256]{2,1,0:T(8,128)(2,1)}, u32[]{:S(2)}) copy-start(bf16[1,768,256]{2,1,0:T(8,128)(2,1)} %param.17) | copy-start | bytes 1179652
  53.8 28.1 %all-to-all-start.1 = ((bf16[64,40,128]{2,1,0:T(8,128)(2,1)}), bf16[64,40,128]{2,1,0:T(8,128)(2,1)S(1)}, u32[]{:S(2)}, u32[]{:S(2)}) async-start(bf16[64,40,128]{2,1,0:T(8,128)(2,1)} %grad_rows.1), calls=%async_computation.2 | async-start | bytes 1310720 | tf_op jit(solution)/shard_map/all_to_all | solution.py:439
  59.4 98.8 %all-gather.2.cloned.1.call-start = ((), (), s32[]{:S(2)}) async-start(), calls=%async_computation.6 | async-start | bytes 1990656 | tf_op jit(solution)/shard_map/all_gather | solution.py:502
  59.5 25.2 %collective-permute-start.3 = (bf16[768,256]{1,0:T(8,128)(2,1)S(1)}, bf16[768,256]{1,0:T(8,128)(2,1)S(1)}, u32[]{:S(2)}, u32[]{:S(2)}) collective-permute-start(bf16[768,256]{1,0:T(8,128)(2,1)S(1)} %bitcast.24), channel_id=1, source_target_pairs={{0,64},{64,0},{128,192},{192,128},{256,320},{320,256},{384,448},{4... | collective-permute-start | bytes 1179656 | tf_op jit(solution)/shard_map/ppermute | solution.py:436
  82.7 3.5 %collective-permute-start.2 = (bf16[576,256]{1,0:T(8,128)(2,1)S(1)}, bf16[576,256]{1,0:T(8,128)(2,1)S(1)}, u32[]{:S(2)}, u32[]{:S(2)}) collective-permute-start(bf16[576,256]{1,0:T(8,128)(2,1)S(1)} %get-tuple-element.36), channel_id=1, source_target_pairs={{0,64},{64,0},{128,192},{192,128},{256,320},{320,256},{384,448},{4... | collective-permute-start | bytes 884744 | tf_op jit(solution)/shard_map/ppermute | solution.py:436
  84.7 43.3 %copy-start.4 = (bf16[768,256]{1,0:T(8,128)(2,1)}, bf16[768,256]{1,0:T(8,128)(2,1)S(1)}, u32[]{:S(2)}) copy-start(bf16[768,256]{1,0:T(8,128)(2,1)S(1)} %collective-permute-done.3.other_ref.down_hbm) | copy-start | bytes 1179652
  86.8 16.4 %collective-permute-start.4 = (bf16[4,72,768]{2,1,0:T(8,128)(2,1)S(1)}, bf16[4,72,768]{2,1,0:T(8,128)(2,1)S(1)}, u32[]{:S(2)}, u32[]{:S(2)}) collective-permute-start(bf16[4,72,768]{2,1,0:T(8,128)(2,1)S(1)} %get-tuple-element.37), channel_id=1, source_target_pairs={{0,128},{64,960},{128,0},{192,320},{256,384},{320,192},{384,256},{... | collective-permute-start | bytes 1327112 | tf_op jit(solution)/shard_map/ppermute | solution.py:500
  163.9 4.2 %collective-permute-start.5 = (bf16[1152,256]{1,0:T(8,128)(2,1)}, bf16[1152,256]{1,0:T(8,128)(2,1)}, u32[]{:S(2)}, u32[]{:S(2)}) collective-permute-start(bf16[1152,256]{1,0:T(8,128)(2,1)} %get-tuple-element.42), channel_id=1, source_target_pairs={{0,64},{64,0},{128,192},{192,128},{256,320},{320,256},{384,448},{4... | collective-permute-start | bytes 1769480 | tf_op jit(solution)/shard_map/ppermute | solution.py:436
  171.6 11.5 %copy-start.8 = (bf16[576,256]{1,0:T(8,128)(2,1)S(1)}, bf16[576,256]{1,0:T(8,128)(2,1)}, u32[]{:S(2)}) copy-start(bf16[576,256]{1,0:T(8,128)(2,1)} %copy-done.7) | copy-start | bytes 884740
  171.6 44.7 %all-to-all-start.3 = ((bf16[64,72,128]{2,1,0:T(8,128)(2,1)}), bf16[64,72,128]{2,1,0:T(8,128)(2,1)S(1)}, u32[]{:S(2)}, u32[]{:S(2)}) async-start(bf16[64,72,128]{2,1,0:T(8,128)(2,1)} %pack.1), calls=%async_computation.4 | async-start | bytes 2359296 | tf_op jit(solution)/shard_map/all_to_all | solution.py:439
  183.0 4.3 %copy-start.17 = (bf16[576,768]{1,0:T(8,128)(2,1)S(1)}, bf16[576,768]{1,0:T(8,128)(2,1)}, u32[]{:S(2)}) copy-start(bf16[576,768]{1,0:T(8,128)(2,1)} %get-tuple-element.46) | copy-start | bytes 2654212
  185.4 4.9 %copy-start.10 = (f32[64,128]{1,0:T(8,128)S(1)}, f32[64,128]{1,0:T(8,128)}, u32[]{:S(2)}) copy-start(f32[64,128]{1,0:T(8,128)} %get-tuple-element.27.rank_ref) | copy-start | bytes 98308
  185.4 4.9 %copy-start.12 = (f32[64,128]{1,0:T(8,128)S(1)}, f32[64,128]{1,0:T(8,128)}, u32[]{:S(2)}) copy-start(f32[64,128]{1,0:T(8,128)} %get-tuple-element.28.weight_ref) | copy-start | bytes 98308
  185.4 7.5 %collective-permute-start.6 = (bf16[256,1536]{1,0:T(8,128)(2,1)S(1)}, bf16[256,1536]{1,0:T(8,128)(2,1)S(1)}, u32[]{:S(2)}, u32[]{:S(2)}) collective-permute-start(bf16[256,1536]{1,0:T(8,128)(2,1)S(1)} %convolution_convert_fusion), channel_id=1, source_target_pairs={{0,64},{64,0},{128,192},{192,128},{256,320},{320,256},{384,448},{4... | collective-permute-start | bytes 2359304 | tf_op jit(solution)/shard_map/ppermute | solution.py:436
  187.9 3.7 %collective-permute-start.7 = (bf16[768,256]{1,0:T(8,128)(2,1)S(1)}, bf16[768,256]{1,0:T(8,128)(2,1)S(1)}, u32[]{:S(2)}, u32[]{:S(2)}) collective-permute-start(bf16[768,256]{1,0:T(8,128)(2,1)S(1)} %convolution_convert_fusion.1), channel_id=1, source_target_pairs={{0,64},{64,0},{128,192},{192,128},{256,320},{320,256},{384,448},{4... | collective-permute-start | bytes 1179656 | tf_op jit(solution)/shard_map/ppermute | solution.py:436
  190.8 2.3 %copy-start.2 = (bf16[576,256]{1,0:T(8,128)(2,1)S(1)}, bf16[576,256]{1,0:T(8,128)(2,1)}, u32[]{:S(2)}) copy-start(bf16[576,256]{1,0:T(8,128)(2,1)} %copy-done.1) | copy-start | bytes 884740
  190.8 2.3 %copy-start.16 = (bf16[576,1536]{1,0:T(8,128)(2,1)S(1)}, bf16[576,1536]{1,0:T(8,128)(2,1)}, u32[]{:S(2)}) copy-start(bf16[576,1536]{1,0:T(8,128)(2,1)} %get-tuple-element.45) | copy-start | bytes 5308420
Sparse Core Ops, SparseCore 0:
  53.9 51.4 reduce-scatter.1
  108.0 48.5 all-gather.1
